TPU v7x, 32 devices: a whole 2x2x4 slice. The times are simulated.
32 devices in a mesh: dp: 8 (over z, x), fsdp: 4 (over y, core).
Axes of the slice: x: 2, y: 2, z: 4, core: 2. Of those that a mesh axis runs over, the one named last changes fastest.
Arguments:
- doc_tokens: bfloat16 [8, 3072, 1024], P('dp', 'fsdp'), may hold values from -6 to 6
- query_tokens: bfloat16 [8, 4, 32, 1024], P('dp', 'fsdp'), may hold values from -6 to 6
- doc_lengths: int32 [8], P('dp'), may hold values from 64 to 3072, as said below
- labels: int32 [8, 4], replicated, may hold values from 0 to 7
- query_weight: bfloat16 [1024, 1024], P(('dp', 'fsdp')), may hold values from -0.1875 to 0.1875
- query_bias: bfloat16 [1024], P(('dp', 'fsdp')), may hold values from -1.75 to 1.75
- key_weight: bfloat16 [1024, 1024], P(('dp', 'fsdp')), may hold values from -0.1875 to 0.1875
- key_bias: bfloat16 [1024], P(('dp', 'fsdp')), may hold values from -1.75 to 1.75
- value_weight: bfloat16 [1024, 1024], P(('dp', 'fsdp')), may hold values from -0.1875 to 0.1875
- value_bias: bfloat16 [1024], P(('dp', 'fsdp')), may hold values from -1.75 to 1.75
- out_weight: bfloat16 [1024, 1024], P(('dp', 'fsdp')), may hold values from -0.75 to 0.75
- out_bias: bfloat16 [1024], P(('dp', 'fsdp')), may hold values from -1.75 to 1.75
- first_gain: bfloat16 [1024], P(('dp', 'fsdp')), may hold values from 0.5 to 1.5
- first_shift: bfloat16 [1024], P(('dp', 'fsdp')), may hold values from -1.75 to 1.75
- inner_weight: bfloat16 [1024, 4096], P(('dp', 'fsdp')), may hold values from -0.1875 to 0.1875
- inner_bias: bfloat16 [4096], P(('dp', 'fsdp')), may hold values from -1.75 to 1.75
- outer_weight: bfloat16 [4096, 1024], P(('dp', 'fsdp')), may hold values from -0.09375 to 0.09375
- outer_bias: bfloat16 [1024], P(('dp', 'fsdp')), may hold values from -1.75 to 1.75
- second_gain: bfloat16 [1024], P(('dp', 'fsdp')), may hold values from 0.5 to 1.5
- second_shift: bfloat16 [1024], P(('dp', 'fsdp')), may hold values from -1.75 to 1.75
- vector_weight: bfloat16 [1024, 128], P(('dp', 'fsdp')), may hold values from -0.1875 to 0.1875
Outputs:
- losses: float32 [3, 32], replicated
- doc_out: bfloat16 [8, 3072, 1024], P('dp', 'fsdp')
- query_out: bfloat16 [8, 4, 32, 1024], P('dp', 'fsdp')
- doc_grad: bfloat16 [8, 3072, 1024], P('dp', 'fsdp')
- query_grad: bfloat16 [8, 4, 32, 1024], P('dp', 'fsdp')
- query_weight_grad: float32 [1024, 1024], P(('dp', 'fsdp'))
- query_bias_grad: float32 [1024], P(('dp', 'fsdp'))
- key_weight_grad: float32 [1024, 1024], P(('dp', 'fsdp'))
- key_bias_grad: float32 [1024], P(('dp', 'fsdp'))
- value_weight_grad: float32 [1024, 1024], P(('dp', 'fsdp'))
- value_bias_grad: float32 [1024], P(('dp', 'fsdp'))
- out_weight_grad: float32 [1024, 1024], P(('dp', 'fsdp'))
- out_bias_grad: float32 [1024], P(('dp', 'fsdp'))
- first_gain_grad: float32 [1024], P(('dp', 'fsdp'))
- first_shift_grad: float32 [1024], P(('dp', 'fsdp'))
- inner_weight_grad: float32 [1024, 4096], P(('dp', 'fsdp'))
- inner_bias_grad: float32 [4096], P(('dp', 'fsdp'))
- outer_weight_grad: float32 [4096, 1024], P(('dp', 'fsdp'))
- outer_bias_grad: float32 [1024], P(('dp', 'fsdp'))
- second_gain_grad: float32 [1024], P(('dp', 'fsdp'))
- second_shift_grad: float32 [1024], P(('dp', 'fsdp'))
- vector_weight_grad: float32 [1024, 128], P(('dp', 'fsdp'))
Inputs may be any that keep to these rules, and one draw needn't show every extreme that they name: `doc_lengths`: heavy-tailed lengths; one document of every draw has all 3072 positions valid and another exactly 64.
All inputs are finite; a program needn't handle non-finite values.
Results may differ from a plain program's by a relative error of at most 0.035.
Values may be sent and summed in bfloat16 or wider, within the bound.
A program may use at most 384 MiB of HBM per device.

v0:
```python
import jax
import jax.numpy as jnp
from jax import lax
from jax.sharding import PartitionSpec as P

D = 1024
HEAD_DIM = 64
PROJ = 128
QLEN = 32


norm_eps = 1e-05
vector_eps = 1e-06
rope_base = 10000.0
smooth_temp = 0.05
loss_temp = 0.02
masked_score = -1e30
group_cols = 128


def combined_all(part, axis, combine):
    gathered = lax.all_gather(part, axis)

    def take(source):
        return lax.dynamic_index_in_dim(gathered, source, 0, False)

    return lax.fori_loop(
        1, lax.axis_size(axis), lambda source, state: combine(state, take(source)), take(0)
    )


def dense(left, right):
    return jnp.dot(left, right, preferred_element_type=jnp.float32)


def rotate(flat_rows, positions):
    row_count = flat_rows.shape[0]
    by_head = flat_rows.reshape(row_count, -1, HEAD_DIM)
    half_dim = HEAD_DIM // 2
    frequency = rope_base ** (-jnp.arange(half_dim, dtype=jnp.float32) / half_dim)
    angles = positions.astype(jnp.float32)[:, None] * frequency[None, :]
    cosine = jnp.cos(angles)[:, None, :]
    sine_part = jnp.sin(angles)[:, None, :]
    leading = by_head[..., :half_dim]
    trailing = by_head[..., half_dim:]
    turned = jnp.concatenate(
        [leading * cosine - trailing * sine_part, trailing * cosine + leading * sine_part], axis=-1
    )
    return turned.reshape(row_count, -1)


def layer_norm(summed, gain_row, shift_row):
    centered = summed - jnp.mean(summed, axis=-1, keepdims=True)
    variance = jnp.mean(centered * centered, axis=-1, keepdims=True)
    return centered * lax.rsqrt(variance + norm_eps) * gain_row + shift_row


def exact_gelu(values):
    return jax.nn.gelu(values, approximate=False)


def normalize(projected):
    result_list = []
    for columns in (PROJ, PROJ * 3 // 4, PROJ // 2):
        leading = projected[:, :columns]
        result_list.append(
            leading * lax.rsqrt(jnp.sum(leading * leading, axis=-1, keepdims=True) + vector_eps)
        )
    return tuple(result_list)


def to_groups(flat_rows):
    row_count = flat_rows.shape[0]
    return flat_rows.reshape(row_count, -1, group_cols).transpose(1, 0, 2)


def from_groups(grouped):
    return grouped.transpose(1, 0, 2).reshape(grouped.shape[1], -1)


def group_scores(query_part, key_part, allowed):
    row_count = query_part.shape[0]
    key_count = key_part.shape[0]
    heads_here = query_part.shape[1] // HEAD_DIM
    query_heads = query_part.reshape(row_count, heads_here, HEAD_DIM)
    key_heads = key_part.reshape(key_count, heads_here, HEAD_DIM)
    raw_scores = jnp.einsum(
        "rhd,khd->hrk", query_heads, key_heads, preferred_element_type=jnp.float32
    )
    return (
        jnp.where(allowed[None, None, :], raw_scores * HEAD_DIM ** (-0.5), masked_score),
        query_heads,
        key_heads,
    )


def attend_group(query_part, key_part, value_part, allowed):
    row_count = query_part.shape[0]
    scaled, query_heads, key_heads = group_scores(query_part, key_part, allowed)
    value_heads = value_part.reshape(key_heads.shape)
    largest = jnp.max(scaled, axis=-1, keepdims=True)
    powers = jnp.exp(scaled - largest)
    row_total = jnp.sum(powers, axis=-1, keepdims=True)
    softmax_rows = powers / row_total
    mixed_heads = jnp.einsum(
        "hrk,khd->rhd",
        softmax_rows.astype(jnp.bfloat16),
        value_heads,
        preferred_element_type=jnp.float32,
    )
    return (mixed_heads.reshape(row_count, -1), (largest + jnp.log(row_total))[..., 0])


def attend_back(query_part, key_part, value_part, allowed, log_total, mixed_part, grad_part):
    row_count = query_part.shape[0]
    key_count = key_part.shape[0]
    scaled, query_heads, key_heads = group_scores(query_part, key_part, allowed)
    value_heads = value_part.reshape(key_heads.shape)
    grad_heads = grad_part.reshape(query_heads.shape)
    mixed_heads = mixed_part.reshape(query_heads.shape)
    softmax_rows = jnp.exp(scaled - log_total[:, :, None])
    row_dots = jnp.transpose(jnp.sum(grad_heads.astype(jnp.float32) * mixed_heads, axis=-1), (1, 0))
    grad_soft = jnp.einsum(
        "rhd,khd->hrk", grad_heads, value_heads, preferred_element_type=jnp.float32
    )
    grad_scores = (softmax_rows * (grad_soft - row_dots[:, :, None]) * HEAD_DIM ** (-0.5)).astype(
        jnp.bfloat16
    )
    grad_query = jnp.einsum(
        "hrk,khd->rhd", grad_scores, key_heads, preferred_element_type=jnp.float32
    )
    grad_key = jnp.einsum(
        "hrk,rhd->khd", grad_scores, query_heads, preferred_element_type=jnp.float32
    )
    grad_value = jnp.einsum(
        "hrk,rhd->khd",
        softmax_rows.astype(jnp.bfloat16),
        grad_heads,
        preferred_element_type=jnp.float32,
    )
    return (
        grad_query.reshape(row_count, -1),
        grad_key.reshape(key_count, -1),
        grad_value.reshape(key_count, -1),
    )


def attention(query_low, key_low, value_low, allowed):
    return lax.map(
        lambda grouped_in: attend_group(grouped_in[0], grouped_in[1], grouped_in[2], allowed),
        (to_groups(query_low), to_groups(key_low), to_groups(value_low)),
    )


def attention_back(query_low, key_low, value_low, allowed, log_total, kept_mixed, grad_low):
    return lax.map(
        lambda grouped_in: attend_back(
            grouped_in[0],
            grouped_in[1],
            grouped_in[2],
            allowed,
            grouped_in[3],
            grouped_in[4],
            grouped_in[5],
        ),
        (
            to_groups(query_low),
            to_groups(key_low),
            to_groups(value_low),
            log_total,
            kept_mixed,
            to_groups(grad_low),
        ),
    )


def shards(
    doc_tokens,
    query_tokens,
    doc_lengths,
    labels,
    query_weight,
    query_bias,
    key_weight,
    key_bias,
    value_weight,
    value_bias,
    out_weight,
    out_bias,
    first_gain,
    first_shift,
    inner_weight,
    inner_bias,
    outer_weight,
    outer_bias,
    second_gain,
    second_shift,
    vector_weight,
):
    gathered = (
        lax.all_gather(query_weight, ("dp", "fsdp"), axis=0, tiled=True),
        lax.all_gather(query_bias, ("dp", "fsdp"), axis=0, tiled=True),
        lax.all_gather(key_weight, ("dp", "fsdp"), axis=0, tiled=True),
        lax.all_gather(key_bias, ("dp", "fsdp"), axis=0, tiled=True),
        lax.all_gather(value_weight, ("dp", "fsdp"), axis=0, tiled=True),
        lax.all_gather(value_bias, ("dp", "fsdp"), axis=0, tiled=True),
        lax.all_gather(out_weight, ("dp", "fsdp"), axis=0, tiled=True),
        lax.all_gather(out_bias, ("dp", "fsdp"), axis=0, tiled=True),
        lax.all_gather(first_gain, ("dp", "fsdp"), axis=0, tiled=True),
        lax.all_gather(first_shift, ("dp", "fsdp"), axis=0, tiled=True),
        lax.all_gather(inner_weight, ("dp", "fsdp"), axis=0, tiled=True),
        lax.all_gather(inner_bias, ("dp", "fsdp"), axis=0, tiled=True),
        lax.all_gather(outer_weight, ("dp", "fsdp"), axis=0, tiled=True),
        lax.all_gather(outer_bias, ("dp", "fsdp"), axis=0, tiled=True),
        lax.all_gather(second_gain, ("dp", "fsdp"), axis=0, tiled=True),
        lax.all_gather(second_shift, ("dp", "fsdp"), axis=0, tiled=True),
        lax.all_gather(vector_weight, ("dp", "fsdp"), axis=0, tiled=True),
    )
    (
        query_mat,
        query_vec,
        key_mat,
        key_vec,
        value_mat,
        value_vec,
        out_mat,
        out_vec,
        gain_one,
        shift_one,
        inner_mat,
        inner_vec,
        outer_mat,
        outer_vec,
        gain_two,
        shift_two,
        vector_mat,
    ) = gathered
    fsdp_index = lax.axis_index("fsdp")
    dp_index = lax.axis_index("dp")
    doc_count = doc_tokens.shape[1]
    seq_len = doc_count * lax.axis_size("fsdp")
    length = doc_lengths[0]
    rows_in = jnp.concatenate(
        [query_tokens.reshape(QLEN, D), doc_tokens.reshape(doc_count, D)], axis=0
    )
    positions = jnp.concatenate(
        [
            jnp.arange(QLEN, dtype=jnp.int32),
            fsdp_index * doc_count + jnp.arange(doc_count, dtype=jnp.int32),
        ]
    )
    query_lin = dense(rows_in, query_mat) + query_vec.astype(jnp.float32)
    key_lin = dense(rows_in, key_mat) + key_vec.astype(jnp.float32)
    query_low = rotate(query_lin, positions).astype(jnp.bfloat16)
    key_low = rotate(key_lin, positions).astype(jnp.bfloat16)
    value_low = (dense(rows_in, value_mat) + value_vec.astype(jnp.float32)).astype(jnp.bfloat16)
    keys_all, values_all = (
        lax.all_gather(key_low[QLEN:], "fsdp", axis=0, tiled=True),
        lax.all_gather(value_low[QLEN:], "fsdp", axis=0, tiled=True),
    )
    key_allowed = jnp.arange(seq_len, dtype=jnp.int32) < length
    own_allowed = jnp.ones((QLEN,), dtype=jnp.bool_)
    doc_mixed, doc_log = attention(query_low[QLEN:], keys_all, values_all, key_allowed)
    own_mixed, own_log = attention(query_low[:QLEN], key_low[:QLEN], value_low[:QLEN], own_allowed)
    attended_low = jnp.concatenate([from_groups(own_mixed), from_groups(doc_mixed)], axis=0).astype(
        jnp.bfloat16
    )
    sum_one = (
        rows_in.astype(jnp.float32) + dense(attended_low, out_mat) + out_vec.astype(jnp.float32)
    )
    normed_one = layer_norm(sum_one, gain_one.astype(jnp.float32), shift_one.astype(jnp.float32))
    normed_low = normed_one.astype(jnp.bfloat16)
    inner_pre = dense(normed_low, inner_mat) + inner_vec.astype(jnp.float32)
    activ_low = exact_gelu(inner_pre).astype(jnp.bfloat16)
    sum_two = normed_one + dense(activ_low, outer_mat) + outer_vec.astype(jnp.float32)
    normed_two = layer_norm(sum_two, gain_two.astype(jnp.float32), shift_two.astype(jnp.float32))
    encoded = normed_two.astype(jnp.bfloat16)
    projected = dense(encoded, vector_mat)
    query_all = lax.all_gather(projected[:QLEN], ("dp", "fsdp"), axis=0, tiled=True)
    query_unit = [entry.astype(jnp.bfloat16) for entry in normalize(query_all)]
    doc_unit = [entry.astype(jnp.bfloat16) for entry in normalize(projected[QLEN:])]
    doc_allowed = positions[QLEN:] < length
    smooth_all = []
    partials = []
    for width_index in range(3):
        similar = jnp.einsum(
            "tc,jc->tj",
            query_unit[width_index],
            doc_unit[width_index],
            preferred_element_type=jnp.float32,
        )
        smooth = jnp.where(doc_allowed[None, :], similar / smooth_temp, masked_score)
        smooth_all.append(smooth)
        partials.append(jax.nn.logsumexp(smooth, axis=-1))
    merged = combined_all(jnp.stack(partials), "fsdp", jnp.logaddexp)
    query_total = query_all.shape[0] // QLEN
    own_scores = smooth_temp * jnp.mean(merged.reshape(3, query_total, QLEN), axis=-1)
    all_scores = lax.all_gather(own_scores[:, :, None], "dp", axis=2, tiled=True)
    doc_total = all_scores.shape[2]
    chosen = labels.reshape(-1)[:, None] == jnp.arange(doc_total, dtype=jnp.int32)[None, :]

    def batch_loss(score_table):
        logits = score_table / loss_temp
        picked = jnp.sum(jnp.where(chosen[None], logits, 0.0), axis=-1)
        return jax.nn.logsumexp(logits, axis=-1) - picked

    losses, loss_back = jax.vjp(batch_loss, all_scores)
    (grad_table,) = loss_back(jnp.ones_like(losses))
    own_grad = lax.dynamic_index_in_dim(grad_table, dp_index, axis=2, keepdims=False)
    token_coef = jnp.repeat(own_grad, QLEN, axis=1) / QLEN
    query_cot = []
    doc_cot = []
    for width_index in range(3):
        token_weights = jnp.exp(smooth_all[width_index] - merged[width_index][:, None])
        grad_similar = (token_coef[width_index][:, None] * token_weights).astype(jnp.bfloat16)
        query_cot.append(
            jnp.einsum(
                "tj,jc->tc", grad_similar, doc_unit[width_index], preferred_element_type=jnp.float32
            )
        )
        doc_cot.append(
            jnp.einsum(
                "tj,tc->jc",
                grad_similar,
                query_unit[width_index],
                preferred_element_type=jnp.float32,
            )
        )
    _, query_norm_back = jax.vjp(normalize, query_all)
    (grad_query_all,) = query_norm_back(tuple(query_cot))
    grad_query_proj = lax.psum_scatter(
        grad_query_all, ("dp", "fsdp"), scatter_dimension=0, tiled=True
    )
    _, doc_norm_back = jax.vjp(normalize, projected[QLEN:])
    (grad_doc_proj,) = doc_norm_back(tuple(doc_cot))
    grad_proj_low = jnp.concatenate([grad_query_proj, grad_doc_proj], axis=0).astype(jnp.bfloat16)
    gathered_back = (
        lax.all_gather(query_weight, ("dp", "fsdp"), axis=0, tiled=True),
        lax.all_gather(query_bias, ("dp", "fsdp"), axis=0, tiled=True),
        lax.all_gather(key_weight, ("dp", "fsdp"), axis=0, tiled=True),
        lax.all_gather(key_bias, ("dp", "fsdp"), axis=0, tiled=True),
        lax.all_gather(value_weight, ("dp", "fsdp"), axis=0, tiled=True),
        lax.all_gather(value_bias, ("dp", "fsdp"), axis=0, tiled=True),
        lax.all_gather(out_weight, ("dp", "fsdp"), axis=0, tiled=True),
        lax.all_gather(out_bias, ("dp", "fsdp"), axis=0, tiled=True),
        lax.all_gather(first_gain, ("dp", "fsdp"), axis=0, tiled=True),
        lax.all_gather(first_shift, ("dp", "fsdp"), axis=0, tiled=True),
        lax.all_gather(inner_weight, ("dp", "fsdp"), axis=0, tiled=True),
        lax.all_gather(inner_bias, ("dp", "fsdp"), axis=0, tiled=True),
        lax.all_gather(outer_weight, ("dp", "fsdp"), axis=0, tiled=True),
        lax.all_gather(outer_bias, ("dp", "fsdp"), axis=0, tiled=True),
        lax.all_gather(second_gain, ("dp", "fsdp"), axis=0, tiled=True),
        lax.all_gather(second_shift, ("dp", "fsdp"), axis=0, tiled=True),
        lax.all_gather(vector_weight, ("dp", "fsdp"), axis=0, tiled=True),
    )
    (
        query_mat,
        query_vec,
        key_mat,
        key_vec,
        value_mat,
        value_vec,
        out_mat,
        out_vec,
        gain_one,
        shift_one,
        inner_mat,
        inner_vec,
        outer_mat,
        outer_vec,
        gain_two,
        shift_two,
        vector_mat,
    ) = gathered_back
    grad_vector_mat = jnp.einsum(
        "rd,rp->dp", encoded, grad_proj_low, preferred_element_type=jnp.float32
    )
    grad_normed_two = jnp.einsum(
        "rp,dp->rd", grad_proj_low, vector_mat, preferred_element_type=jnp.float32
    )
    _, norm_two_back = jax.vjp(
        layer_norm, sum_two, gain_two.astype(jnp.float32), shift_two.astype(jnp.float32)
    )
    grad_sum_two, grad_gain_two, grad_shift_two = norm_two_back(grad_normed_two)
    grad_ffn_low = grad_sum_two.astype(jnp.bfloat16)
    grad_outer_mat = jnp.einsum(
        "rf,rd->fd", activ_low, grad_ffn_low, preferred_element_type=jnp.float32
    )
    grad_outer_vec = jnp.sum(grad_ffn_low.astype(jnp.float32), axis=0)
    grad_activ = jnp.einsum(
        "rd,fd->rf", grad_ffn_low, outer_mat, preferred_element_type=jnp.float32
    )
    _, gelu_back = jax.vjp(exact_gelu, inner_pre)
    grad_inner_low = gelu_back(grad_activ)[0].astype(jnp.bfloat16)
    grad_inner_mat = jnp.einsum(
        "rd,rf->df", normed_low, grad_inner_low, preferred_element_type=jnp.float32
    )
    grad_inner_vec = jnp.sum(grad_inner_low.astype(jnp.float32), axis=0)
    grad_normed_one = grad_sum_two + jnp.einsum(
        "rf,df->rd", grad_inner_low, inner_mat, preferred_element_type=jnp.float32
    )
    _, norm_one_back = jax.vjp(
        layer_norm, sum_one, gain_one.astype(jnp.float32), shift_one.astype(jnp.float32)
    )
    grad_sum_one, grad_gain_one, grad_shift_one = norm_one_back(grad_normed_one)
    grad_attn_low = grad_sum_one.astype(jnp.bfloat16)
    grad_out_mat = jnp.einsum(
        "rd,re->de", attended_low, grad_attn_low, preferred_element_type=jnp.float32
    )
    grad_out_vec = jnp.sum(grad_attn_low.astype(jnp.float32), axis=0)
    grad_attended = jnp.einsum(
        "re,de->rd", grad_attn_low, out_mat, preferred_element_type=jnp.float32
    ).astype(jnp.bfloat16)
    doc_grad_query, doc_grad_key, doc_grad_value = attention_back(
        query_low[QLEN:],
        keys_all,
        values_all,
        key_allowed,
        doc_log,
        doc_mixed,
        grad_attended[QLEN:],
    )
    own_grad_query, own_grad_key, own_grad_value = attention_back(
        query_low[:QLEN],
        key_low[:QLEN],
        value_low[:QLEN],
        own_allowed,
        own_log,
        own_mixed,
        grad_attended[:QLEN],
    )
    doc_key_sum, doc_value_sum = (
        lax.psum_scatter(from_groups(doc_grad_key), "fsdp", scatter_dimension=0, tiled=True),
        lax.psum_scatter(from_groups(doc_grad_value), "fsdp", scatter_dimension=0, tiled=True),
    )
    grad_query_rot = jnp.concatenate(
        [from_groups(own_grad_query), from_groups(doc_grad_query)], axis=0
    )
    grad_key_rot = jnp.concatenate([from_groups(own_grad_key), doc_key_sum], axis=0)
    grad_value_low = jnp.concatenate([from_groups(own_grad_value), doc_value_sum], axis=0).astype(
        jnp.bfloat16
    )
    _, rotate_back = jax.vjp(lambda lin_rows: rotate(lin_rows, positions), query_lin)
    grad_query_low = rotate_back(grad_query_rot)[0].astype(jnp.bfloat16)
    grad_key_low = rotate_back(grad_key_rot)[0].astype(jnp.bfloat16)
    grad_query_mat = jnp.einsum(
        "rd,re->de", rows_in, grad_query_low, preferred_element_type=jnp.float32
    )
    grad_key_mat = jnp.einsum(
        "rd,re->de", rows_in, grad_key_low, preferred_element_type=jnp.float32
    )
    grad_value_mat = jnp.einsum(
        "rd,re->de", rows_in, grad_value_low, preferred_element_type=jnp.float32
    )
    grad_query_vec = jnp.sum(grad_query_low.astype(jnp.float32), axis=0)
    grad_key_vec = jnp.sum(grad_key_low.astype(jnp.float32), axis=0)
    grad_value_vec = jnp.sum(grad_value_low.astype(jnp.float32), axis=0)
    grad_rows = (
        grad_sum_one
        + jnp.einsum("re,de->rd", grad_query_low, query_mat, preferred_element_type=jnp.float32)
        + jnp.einsum("re,de->rd", grad_key_low, key_mat, preferred_element_type=jnp.float32)
        + jnp.einsum("re,de->rd", grad_value_low, value_mat, preferred_element_type=jnp.float32)
    )
    grad_rows_low = grad_rows.astype(jnp.bfloat16)
    grad_shards = (
        lax.psum_scatter(grad_query_mat, ("dp", "fsdp"), scatter_dimension=0, tiled=True),
        lax.psum_scatter(grad_query_vec, ("dp", "fsdp"), scatter_dimension=0, tiled=True),
        lax.psum_scatter(grad_key_mat, ("dp", "fsdp"), scatter_dimension=0, tiled=True),
        lax.psum_scatter(grad_key_vec, ("dp", "fsdp"), scatter_dimension=0, tiled=True),
        lax.psum_scatter(grad_value_mat, ("dp", "fsdp"), scatter_dimension=0, tiled=True),
        lax.psum_scatter(grad_value_vec, ("dp", "fsdp"), scatter_dimension=0, tiled=True),
        lax.psum_scatter(grad_out_mat, ("dp", "fsdp"), scatter_dimension=0, tiled=True),
        lax.psum_scatter(grad_out_vec, ("dp", "fsdp"), scatter_dimension=0, tiled=True),
        lax.psum_scatter(grad_gain_one, ("dp", "fsdp"), scatter_dimension=0, tiled=True),
        lax.psum_scatter(grad_shift_one, ("dp", "fsdp"), scatter_dimension=0, tiled=True),
        lax.psum_scatter(grad_inner_mat, ("dp", "fsdp"), scatter_dimension=0, tiled=True),
        lax.psum_scatter(grad_inner_vec, ("dp", "fsdp"), scatter_dimension=0, tiled=True),
        lax.psum_scatter(grad_outer_mat, ("dp", "fsdp"), scatter_dimension=0, tiled=True),
        lax.psum_scatter(grad_outer_vec, ("dp", "fsdp"), scatter_dimension=0, tiled=True),
        lax.psum_scatter(grad_gain_two, ("dp", "fsdp"), scatter_dimension=0, tiled=True),
        lax.psum_scatter(grad_shift_two, ("dp", "fsdp"), scatter_dimension=0, tiled=True),
        lax.psum_scatter(grad_vector_mat, ("dp", "fsdp"), scatter_dimension=0, tiled=True),
    )
    return (
        losses,
        encoded[QLEN:].reshape(1, doc_count, D),
        encoded[:QLEN].reshape(1, 1, QLEN, D),
        grad_rows_low[QLEN:].reshape(1, doc_count, D),
        grad_rows_low[:QLEN].reshape(1, 1, QLEN, D),
    ) + tuple(grad_shards)


def solution(mesh):
    in_specs = (
        P("dp", "fsdp", None),
        P("dp", "fsdp", None, None),
        P("dp"),
        P(),
        P(("dp", "fsdp"), None),
        P(("dp", "fsdp")),
        P(("dp", "fsdp"), None),
        P(("dp", "fsdp")),
        P(("dp", "fsdp"), None),
        P(("dp", "fsdp")),
        P(("dp", "fsdp"), None),
        P(("dp", "fsdp")),
        P(("dp", "fsdp")),
        P(("dp", "fsdp")),
        P(("dp", "fsdp"), None),
        P(("dp", "fsdp")),
        P(("dp", "fsdp"), None),
        P(("dp", "fsdp")),
        P(("dp", "fsdp")),
        P(("dp", "fsdp")),
        P(("dp", "fsdp"), None),
    )
    out_specs = (
        P(),
        P("dp", "fsdp", None),
        P("dp", "fsdp", None, None),
        P("dp", "fsdp", None),
        P("dp", "fsdp", None, None),
        P(("dp", "fsdp"), None),
        P(("dp", "fsdp")),
        P(("dp", "fsdp"), None),
        P(("dp", "fsdp")),
        P(("dp", "fsdp"), None),
        P(("dp", "fsdp")),
        P(("dp", "fsdp"), None),
        P(("dp", "fsdp")),
        P(("dp", "fsdp")),
        P(("dp", "fsdp")),
        P(("dp", "fsdp"), None),
        P(("dp", "fsdp")),
        P(("dp", "fsdp"), None),
        P(("dp", "fsdp")),
        P(("dp", "fsdp")),
        P(("dp", "fsdp")),
        P(("dp", "fsdp"), None),
    )
    return jax.shard_map(shards, mesh=mesh, in_specs=in_specs, out_specs=out_specs, check_vma=False)
```

profile of v0, /device:TPU:1, one launch (start us, length us, event | category | flops | bytes accessed | tf_op | source)
XLA Modules:
  0.0 2502.6 jit_solution(11363414760452933719)
XLA Ops:
  17.0 41.8 %all-reduce.28 = (bf16[1024]{0:T(1024)(128)(2,1)S(1)}, bf16[1024]{0:T(1024)(128)(2,1)S(1)}, bf16[1024]{0:T(1024)(128)(2,1)S(1)}, bf16[1024]{0:T(1024)(128)(2,1)S...) all-reduce(bf16[1024]{0:T(1024)(128)(2,1)S(1)} %dynamic-update-slic, ...), channel_id=1, replica_groups=mesh['dp'=8,'fsdp'=4] {'dp','fsdp'}, use_global_device_ids=true, to_apply=%add.11 | all-reduce | flops 9216 | bytes 36864
  58.8 11.1 all-gather.12.cloned.1.call-done
  77.1 51.1 %all-gather.14.cloned.1.call-done = bf16[1024,1024]{1,0:T(8,128)(2,1)} async-done(((bf16[32,1024]{1,0:T(8,128)(2,1)}), bf16[1024,1024]{1,0:T(8,128)(2,1)}) %all-gather.14.cloned.1.call-update) | async-done | bytes 2097168 | tf_op jit(solution)/shard_map/all_gather | solution.py:201
  135.5 50.9 %all-gather.16.cloned.1.call-done = bf16[1024,1024]{1,0:T(8,128)(2,1)} async-done(((bf16[32,1024]{1,0:T(8,128)(2,1)}), bf16[1024,1024]{1,0:T(8,128)(2,1)}) %all-gather.16.cloned.1.call-update) | async-done | bytes 2097168 | tf_op jit(solution)/shard_map/all_gather | solution.py:203
  206.2 38.7 %all-gather.1 = bf16[32,1,128]{2,1,0:T(2,128)(2,1)S(1)} all-gather(bf16[1,1,128]{2,1,0:T(2,128)(2,1)S(1)} %bitcast.330), channel_id=1, replica_groups=mesh['dp'=8,'fsdp'=4] {'dp','fsdp'}, dimensions={0}, use_global_device_ids=true | all-gather | bytes 8448 | tf_op jit(solution)/shard_map/all_gather | solution.py:212
  247.4 40.8 %all_gather.96 = bf16[1024,128]{1,0:T(8,128)(2,1)} all-gather(bf16[32,128]{1,0:T(8,128)(2,1)S(1)} %copy-done.59), channel_id=1, replica_groups=mesh['dp'=8,'fsdp'=4] {'dp','fsdp'}, dimensions={0}, use_global_device_ids=true | all-gather | bytes 270336 | tf_op jit(solution)/shard_map/all_gather | solution.py:217
  293.9 10.8 while.69
  305.6 8.6 copy.175
  314.6 259.8 %while.72 = (s32[]{:T(128)}, f32[8,768,128]{1,2,0:T(8,128)S(1)}, f32[8,2,768]{2,1,0:T(2,128)}, bf16[8,3072,128]{1,2,0:T(8,128)(2,1)}, bf16[8,768,128]{1,2,0:T(8,...) while((s32[]{:T(128)}, f32[8,768,128]{1,2,0:T(8,128)S(1)}, ...), condition=%wide.region_7.8_spmd.clone, body=%wide.region_4.7_spmd.clone.sunk | while | flops 1264584192 | bytes 63173220 | solution.py:149
  326.6 10.7 fusion.204
  337.9 9.2 fusion.205
  351.1 8.1 fusion.203
  359.1 10.4 fusion.204
  370.1 9.3 fusion.205
  391.5 11.6 fusion.204
  403.7 9.1 fusion.205
  424.9 10.4 fusion.204
  435.8 9.1 fusion.205
  457.0 10.4 fusion.204
  468.1 9.6 fusion.205
  481.7 8.1 fusion.203
  489.8 10.7 fusion.204
  501.2 9.0 fusion.205
  522.2 10.4 fusion.204
  533.2 9.0 fusion.205
  554.3 10.4 fusion.204
  565.3 9.0 fusion.205
  584.1 41.2 %multiply_convert_fusion.1 = (bf16[800,4096]{1,0:T(8,128)(2,1)}, f32[800,4096]{1,0:T(8,128)}, f32[800,4096]{1,0:T(8,128)}) fusion(f32[4096]{0:T(1024)S(1)} %bitcast.325, bf16[1024,4096]{1,0:T(8,128)(2,1)} %all-gather.24.cloned.1.call-done, f32[800,1024]{1,0:T(8,128)} %copy-done.6, f32[1024]{0:T(1024)S(1)} %copy-done.60, f32[1024]{0:T(1024)S(1)} %copy-done.47, ...), kind=kOutput, calls=%fused_computation.87 | convolution fusion | flops 6931251200 | bytes 44464384 | tf_op jit(solution)/shard_map/dot_general | solution.py:33
  625.3 12.2 fusion.90
  640.0 39.9 %all_gather.97 = f32[1024,128]{1,0:T(8,128)S(1)} all-gather(f32[32,128]{1,0:T(8,128)S(1)} %slice.157), channel_id=1, replica_groups=mesh['dp'=8,'fsdp'=4] {'dp','fsdp'}, dimensions={0}, use_global_device_ids=true | all-gather | bytes 540672 | tf_op jit(solution)/shard_map/all_gather | solution.py:279
  691.9 21.4 all_gather.100
  727.3 128.1 %reduce-scatter.11.cloned.1.call-done = f32[32,128]{1,0:T(8,128)} async-done(((f32[1024,128]{1,0:T(8,128)}), f32[32,128]{1,0:T(8,128)}) %reduce-scatter.11.cloned.1.call-update) | async-done | bytes 16400 | tf_op jit(solution)/shard_map/reduce_scatter | solution.py:331
  863.4 22.2 convert_reduce_fusion
  885.7 13.4 multiply_reduce_fusion.3
  908.8 318.7 %while.73 = (s32[]{:T(128)}, f32[8,768,128]{1,2,0:T(8,128)S(1)}, f32[8,3072,128]{1,2,0:T(8,128)}, f32[8,3072,128]{1,2,0:T(8,128)}, bf16[8,3072,128]{1,2,0:T(8,12...) while((s32[]{:T(128)}, f32[8,768,128]{1,2,0:T(8,128)S(1)}, ...), condition=%wide.region_46.47_spmd.clone, body=%wide.region_44.46_spmd.clone.sunk | while | flops 3072099840 | bytes 104052376 | solution.py:156
  923.4 10.0 multiply_convert_fusion.24
  935.2 8.5 fusion.218
  963.4 10.0 multiply_convert_fusion.24
  975.2 8.5 fusion.218
  1003.2 10.0 multiply_convert_fusion.24
  1015.0 8.5 fusion.218
  1043.0 10.0 multiply_convert_fusion.24
  1054.9 8.5 fusion.218
  1082.8 10.0 multiply_convert_fusion.24
  1094.7 8.5 fusion.218
  1122.6 10.0 multiply_convert_fusion.24
  1134.4 8.5 fusion.218
  1162.5 10.0 multiply_convert_fusion.24
  1174.3 8.5 fusion.218
  1202.3 10.0 multiply_convert_fusion.24
  1214.1 8.5 fusion.218
  1239.3 17.4 fusion.77
  1258.5 14.3 fusion.97
  1274.0 42.1 %while.71 = (s32[]{:T(128)}, f32[8,32,128]{2,1,0:T(8,128)S(1)}, f32[8,32,128]{2,1,0:T(8,128)S(1)}, bf16[8,32,128]{2,1,0:T(8,128)(2,1)S(1)}, bf16[8,32,128]{2,1,0...) while((s32[]{:T(128)}, f32[8,32,128]{2,1,0:T(8,128)S(1)}, ...), condition=%wide.region_43.44_spmd, body=%wide.region_41.43_spmd.sunk | while | flops 1337282 | bytes 604045 | solution.py:156
  1316.3 11.5 reduce-scatter.15.cloned.1.call-done
  1338.2 91.5 %reduce-scatter.13.cloned.1.call-done = f32[768,1024]{0,1:T(8,128)} async-done(((f32[3072,1024]{0,1:T(8,128)}), f32[768,1024]{0,1:T(8,128)}) %reduce-scatter.13.cloned.1.call-update) | async-done | bytes 3145744 | tf_op jit(solution)/shard_map/reduce_scatter | solution.py:433
  1454.1 40.7 %all-reduce.27 = (f32[1024]{0:T(1024)S(1)}, f32[1024]{0:T(1024)S(1)}, f32[1024]{0:T(1024)S(1)}, f32[1024]{0:T(1024)S(1)}, f32[1024]{0:T(1024)S(1)}, /*index=5*/f...) all-reduce(f32[1024]{0:T(1024)S(1)} %reduce_sum.407, ...), channel_id=7, replica_groups=mesh['dp'=8,'fsdp'=4] {'dp','fsdp'}, use_global_device_ids=true, to_apply=%region_51.52.clone | all-reduce | flops 13312 | bytes 106496
  1513.0 48.2 %reduce-scatter.29.cloned.1.call-done = f32[32,128]{1,0:T(8,128)} async-done(((f32[1024,128]{1,0:T(8,128)}), f32[32,128]{1,0:T(8,128)}) %reduce-scatter.29.cloned.1.call-update) | async-done | bytes 16400 | tf_op jit(solution)/shard_map/reduce_scatter | solution.py:482
  1561.2 140.2 %reduce-scatter.23.cloned.1.call-done = f32[32,1024]{1,0:T(8,128)} async-done(((f32[1024,1024]{1,0:T(8,128)}), f32[32,1024]{1,0:T(8,128)}) %reduce-scatter.23.cloned.1.call-update) | async-done | bytes 131088 | tf_op jit(solution)/shard_map/reduce_scatter | solution.py:472
  1701.4 187.9 %reduce-scatter.25.cloned.1.call-done = f32[32,4096]{1,0:T(8,128)} async-done(((f32[1024,4096]{1,0:T(8,128)}), f32[32,4096]{1,0:T(8,128)}) %reduce-scatter.25.cloned.1.call-update) | async-done | bytes 524304 | tf_op jit(solution)/shard_map/reduce_scatter | solution.py:476
  1889.3 187.3 %reduce-scatter.27.cloned.1.call-done = f32[128,1024]{1,0:T(8,128)} async-done(((f32[4096,1024]{1,0:T(8,128)}), f32[128,1024]{1,0:T(8,128)}) %reduce-scatter.27.cloned.1.call-update) | async-done | bytes 524304 | tf_op jit(solution)/shard_map/reduce_scatter | solution.py:478
  2076.6 139.2 %reduce-scatter.21.cloned.1.call-done = f32[32,1024]{1,0:T(8,128)} async-done(((f32[1024,1024]{1,0:T(8,128)}), f32[32,1024]{1,0:T(8,128)}) %reduce-scatter.21.cloned.1.call-update) | async-done | bytes 131088 | tf_op jit(solution)/shard_map/reduce_scatter | solution.py:470
  2215.8 139.8 %reduce-scatter.17.cloned.1.call-done = f32[32,1024]{1,0:T(8,128)} async-done(((f32[1024,1024]{1,0:T(8,128)}), f32[32,1024]{1,0:T(8,128)}) %reduce-scatter.17.cloned.1.call-update) | async-done | bytes 131088 | tf_op jit(solution)/shard_map/reduce_scatter | solution.py:466
  2355.6 139.7 %reduce-scatter.19.cloned.1.call-done = f32[32,1024]{1,0:T(8,128)} async-done(((f32[1024,1024]{1,0:T(8,128)}), f32[32,1024]{1,0:T(8,128)}) %reduce-scatter.19.cloned.1.call-update) | async-done | bytes 131088 | tf_op jit(solution)/shard_map/reduce_scatter | solution.py:468
  (839 shorter events, 482.6 us)
Async XLA Ops:
  7.2 62.8 %all-gather.12.cloned.1.call-start = ((), (), s32[]{:S(2)}) async-start(), calls=%async_computation.10 | async-start | bytes 2162688 | tf_op jit(solution)/shard_map/all_gather | solution.py:205
  7.9 120.2 %all-gather.14.cloned.1.call-start = ((), (), s32[]{:S(2)}) async-start(), calls=%async_computation.11 | async-start | bytes 2162688 | tf_op jit(solution)/shard_map/all_gather | solution.py:201
  8.7 177.6 %all-gather.16.cloned.1.call-start = ((), (), s32[]{:S(2)}) async-start(), calls=%async_computation.12 | async-start | bytes 2162688 | tf_op jit(solution)/shard_map/all_gather | solution.py:203
  9.4 296.2 %all-gather.18.cloned.1.call-start = ((), (), s32[]{:S(2)}) async-start(), calls=%async_computation.13 | async-start | bytes 7864320 | tf_op jit(solution)/shard_map/all_gather | solution.py:259
  76.4 237.9 %all-gather.20.cloned.1.call-start = ((), (), s32[]{:S(2)}) async-start(), calls=%async_computation.14 | async-start | bytes 7864320 | tf_op jit(solution)/shard_map/all_gather | solution.py:258
  77.1 116.5 %copy-start.31 = (f32[800,32]{0,1:T(8,128)}, f32[800,32]{0,1:T(8,128)S(1)}, u32[]{:S(2)}) copy-start(f32[800,32]{0,1:T(8,128)S(1)} %get-tuple-element.530) | copy-start | bytes 307204
  77.1 116.5 %copy-start.32 = (f32[800,32]{0,1:T(8,128)}, f32[800,32]{0,1:T(8,128)S(1)}, u32[]{:S(2)}) copy-start(f32[800,32]{0,1:T(8,128)S(1)} %get-tuple-element.531) | copy-start | bytes 307204
  198.8 4.9 copy-start.66
  198.8 7.4 copy-start.69
  198.8 48.6 %copy-start.59 = (bf16[32,128]{1,0:T(8,128)(2,1)S(1)}, bf16[32,128]{1,0:T(8,128)(2,1)}, u32[]{:S(2)}) copy-start(bf16[32,128]{1,0:T(8,128)(2,1)} %param.51) | copy-start | bytes 24580
  201.6 374.2 %all-gather.22.cloned.1.call-start = ((), (), s32[]{:S(2)}) async-start(), calls=%async_computation.15 | async-start | bytes 2162688 | tf_op jit(solution)/shard_map/all_gather | solution.py:207
  202.2 381.9 %all-gather.24.cloned.1.call-start = ((), (), s32[]{:S(2)}) async-start(), calls=%async_computation.16 | async-start | bytes 8650752 | tf_op jit(solution)/shard_map/all_gather | solution.py:211
  202.9 422.4 %all-gather.26.cloned.1.call-start = ((), (), s32[]{:S(2)}) async-start(), calls=%async_computation.17 | async-start | bytes 8650752 | tf_op jit(solution)/shard_map/all_gather | solution.py:213
  203.7 651.7 %reduce-scatter.11.cloned.1.call-start = ((), (), s32[]{:S(2)}) async-start(), calls=%async_computation.18 | async-start | bytes 540672 | tf_op jit(solution)/shard_map/reduce_scatter | solution.py:331
  304.7 9.5 copy-start.33
  304.7 9.5 copy-start.34
  304.7 9.5 copy-start.35
  304.7 9.5 copy-start.36
  574.4 6.7 copy-start.5
  581.1 3.0 copy-start.47
  581.1 3.0 copy-start.56
  581.1 3.0 copy-start.60
  581.1 317.9 %copy-start.41 = (f32[800]{0:T(1024)}, f32[800]{0:T(1024)S(1)}, u32[]{:S(2)}) copy-start(f32[800]{0:T(1024)S(1)} %broadcast_multiply_fusion.1) | copy-start | bytes 9604
  584.0 315.0 %copy-start.49 = (f32[800]{0:T(1024)}, f32[800]{0:T(1024)S(1)}, u32[]{:S(2)}) copy-start(f32[800]{0:T(1024)S(1)} %fusion.57) | copy-start | bytes 9604
  584.1 41.2 %copy-start.7 = (f32[800,1024]{1,0:T(8,128)S(1)}, f32[800,1024]{1,0:T(8,128)}, u32[]{:S(2)}) copy-start(f32[800,1024]{1,0:T(8,128)} %copy-done.6) | copy-start | bytes 9830404
  584.1 41.2 %copy-start.62 = (f32[1024]{0:T(1024)S(1)}, f32[1024]{0:T(1024)}, u32[]{:S(2)}) copy-start(f32[1024]{0:T(1024)} %convert_element_type.183) | copy-start | bytes 12292
  639.2 42.5 %copy-start.3 = (bf16[800,1024]{1,0:T(8,128)(2,1)}, bf16[800,1024]{1,0:T(8,128)(2,1)S(1)}, u32[]{:S(2)}) copy-start(bf16[800,1024]{1,0:T(8,128)(2,1)S(1)} %add_convert_fusion.4) | copy-start | bytes 4915204
  639.2 41.8 %copy-start.58 = (pred[768]{0:T(1024)(128)(4,1)S(1)}, pred[768]{0:T(1024)(128)(4,1)}, u32[]{:S(2)}) copy-start(pred[768]{0:T(1024)(128)(4,1)} %broadcast_compare_fusion) | copy-start | bytes 2308
  681.8 2.6 copy-start.13
  684.4 7.2 copy-start.14
  684.4 28.9 %copy-start.67 = (pred[32,8]{0,1:T(8,128)(4,1)S(1)}, pred[32,8]{0,1:T(8,128)(4,1)}, u32[]{:S(2)}) copy-start(pred[32,8]{0,1:T(8,128)(4,1)} %iota_compare_fusion.2) | copy-start | bytes 772
  684.4 29.5 %copy-start.68 = (f32[32,1]{0,1:T(1,128)S(1)}, f32[32,1]{0,1:T(1,128)}, u32[]{:S(2)}) copy-start(f32[32,1]{0,1:T(1,128)} %constant_dynamic-slice_fusion.17) | copy-start | bytes 388
  726.3 601.5 %reduce-scatter.15.cloned.1.call-start = ((), (), s32[]{:S(2)}) async-start(), calls=%async_computation.20 | async-start | bytes 15728640 | tf_op jit(solution)/shard_map/reduce_scatter | solution.py:434
  727.3 132.8 %copy-start.22 = (bf16[768,128]{1,0:T(8,128)(2,1)}, bf16[768,128]{1,0:T(8,128)(2,1)S(1)}, u32[]{:S(2)}) copy-start(bf16[768,128]{1,0:T(8,128)(2,1)S(1)} %fusion.51) | copy-start | bytes 589828
  856.1 3.9 copy-start.38
  856.1 4.0 copy-start.1
  863.4 22.2 copy-start.8
  885.7 13.4 copy-start.44
  900.1 5.0 copy-start.9
  900.1 3.1 copy-start.72
  901.1 4.1 copy-start.27
  1229.1 200.6 %reduce-scatter.13.cloned.1.call-start = ((), (), s32[]{:S(2)}) async-start(), calls=%async_computation.19 | async-start | bytes 15728640 | tf_op jit(solution)/shard_map/reduce_scatter | solution.py:433
  1229.1 3.2 copy-start.28
  1229.8 331.4 %reduce-scatter.29.cloned.1.call-start = ((), (), s32[]{:S(2)}) async-start(), calls=%async_computation.27 | async-start | bytes 540672 | tf_op jit(solution)/shard_map/reduce_scatter | solution.py:482
  1232.0 469.3 %reduce-scatter.23.cloned.1.call-start = ((), (), s32[]{:S(2)}) async-start(), calls=%async_computation.24 | async-start | bytes 4325376 | tf_op jit(solution)/shard_map/reduce_scatter | solution.py:472
  1238.6 650.7 %reduce-scatter.25.cloned.1.call-start = ((), (), s32[]{:S(2)}) async-start(), calls=%async_computation.25 | async-start | bytes 17301504 | tf_op jit(solution)/shard_map/reduce_scatter | solution.py:476
  1256.7 819.9 %reduce-scatter.27.cloned.1.call-start = ((), (), s32[]{:S(2)}) async-start(), calls=%async_computation.26 | async-start | bytes 17301504 | tf_op jit(solution)/shard_map/reduce_scatter | solution.py:478
  1272.9 943.0 %reduce-scatter.21.cloned.1.call-start = ((), (), s32[]{:S(2)}) async-start(), calls=%async_computation.23 | async-start | bytes 4325376 | tf_op jit(solution)/shard_map/reduce_scatter | solution.py:470
  1316.1 15.0 copy-start.77
  1316.3 19.8 copy-start.29
  1327.9 3.3 copy-start.73
  1336.1 1019.5 %reduce-scatter.17.cloned.1.call-start = ((), (), s32[]{:S(2)}) async-start(), calls=%async_computation.21 | async-start | bytes 4325376 | tf_op jit(solution)/shard_map/reduce_scatter | solution.py:466
  1442.7 1052.5 %reduce-scatter.19.cloned.1.call-start = ((), (), s32[]{:S(2)}) async-start(), calls=%async_computation.22 | async-start | bytes 4325376 | tf_op jit(solution)/shard_map/reduce_scatter | solution.py:468
  1442.8 3.1 copy-start.75
  1450.3 3.7 copy-start.45
  1450.3 3.7 copy-start.46
  1450.3 3.7 copy-start.54
  1450.3 3.7 copy-start.55
  1450.4 3.7 copy-start.57
  1450.4 3.7 copy-start.64
  1450.4 3.7 copy-start.65
  1500.6 4.5 copy-start.21
  1500.6 4.5 copy-start.71
  1505.1 2.6 copy-start.70
  (32 other events, 44.0 us)
Sparse Core Ops, SparseCore 0:
  10.9 59.0 all-gather.11
  72.8 55.2 all-gather.13
  131.0 55.2 all-gather.15
  188.3 45.3 all-gather.17
  235.1 48.7 all-gather.19
  286.6 56.6 all-gather.21
  346.2 76.4 all-gather.23
  425.5 76.1 all-gather.25
  726.5 128.8 reduce-scatter.10
  1227.6 100.2 reduce-scatter.14
  1330.6 99.0 reduce-scatter.12
  1432.5 128.6 reduce-scatter.28
  1564.0 137.2 reduce-scatter.22
  1704.1 185.1 reduce-scatter.24
  1892.0 184.5 reduce-scatter.26
  2079.3 136.4 reduce-scatter.20
  2218.5 137.0 reduce-scatter.16
  2358.3 136.9 reduce-scatter.18
where the time goes:
time: 2520 us; the launch traced here: 2500 us
  waiting for transfers between devices  1330 us (53%)
  matrix products  580 us (23%)
  blocking collectives  229 us (9%)
  local copies, waits for them, and re-layouts  188 us (7%)
  other arithmetic  155 us (6%)
    reduce_scatter x1, waiting for transfers between devices, shards(): lax.psum_scatter(grad_inner_mat, ('dp', 'fsdp'), scatter_dimension=0, til...  188 us
    reduce_scatter x1, waiting for transfers between devices, shards(): lax.psum_scatter(grad_outer_mat, ('dp', 'fsdp'), scatter_dimension=0, til...  187 us
    reduce_scatter x1, waiting for transfers between devices, shards(): lax.psum_scatter(grad_out_mat, ('dp', 'fsdp'), scatter_dimension=0, tiled...  140 us
    reduce_scatter x1, waiting for transfers between devices, shards(): lax.psum_scatter(grad_query_mat, ('dp', 'fsdp'), scatter_dimension=0, til...  140 us
    reduce_scatter x1, waiting for transfers between devices, shards(): lax.psum_scatter(grad_key_mat, ('dp', 'fsdp'), scatter_dimension=0, tiled...  140 us
    reduce_scatter x1, waiting for transfers between devices, shards(): lax.psum_scatter(grad_value_mat, ('dp', 'fsdp'), scatter_dimension=0, til...  139 us
    dot_general x32, matrix products, group_scores(): jnp.einsum('rhd,khd->hrk', query_heads, key_heads, preferred_element_type...  130 us
    reduce_scatter x1, waiting for transfers between devices, shards(): lax.psum_scatter(grad_query_all, ('dp', 'fsdp'), scatter_dimension=0, til...  128 us
  transfers between devices with their start and end apart: 18, of which 13 were waited for; matrix products, arithmetic and copies ran while one was open for 20% of the time, Pallas kernels for 0%

commit v1 on v0

v1 whole, which is shorter than its diff:
```python
import functools
import math

import jax
import jax.numpy as jnp
import numpy as np
from jax import lax
from jax.experimental import pallas as pl
from jax.experimental.pallas import tpu as pltpu
from jax.sharding import PartitionSpec as P

D = 1024
HEAD_DIM = 64
PROJ = 128
QLEN = 32
LANES = 128

norm_eps = 1e-05
vector_eps = 1e-06
rope_base = 10000.0
smooth_temp = 0.05
loss_temp = 0.02
masked_score = -1e30
log2e = math.log2(math.e)
AXES = ("dp", "fsdp")
BF = jnp.bfloat16
F32 = jnp.float32
VMEM_MOST = 60 << 20


def dot_nn(left, right):
    return lax.dot_general(left, right, (((1,), (0,)), ((), ())), preferred_element_type=F32)


def dot_nt(left, right):
    return lax.dot_general(left, right, (((1,), (1,)), ((), ())), preferred_element_type=F32)


def dot_tn(left, right):
    return lax.dot_general(left, right, (((0,), (0,)), ((), ())), preferred_element_type=F32)


def lanes_of(shape):
    return lax.broadcasted_iota(jnp.int32, shape, len(shape) - 1)


def split_three(value):
    high = value.astype(BF)
    rest = value - high.astype(F32)
    middle = rest.astype(BF)
    return high, middle, (rest - middle.astype(F32)).astype(BF)


def params(**more):
    return pltpu.CompilerParams(vmem_limit_bytes=VMEM_MOST, **more)


def rope_tables(parts, doc_rows):
    half_dim = HEAD_DIM // 2
    frequency = rope_base ** (-np.arange(half_dim, dtype=np.float64) / half_dim)
    own = [
        np.concatenate([part * doc_rows + np.arange(doc_rows), np.arange(QLEN)])
        for part in range(parts)
    ]
    angles = np.concatenate(own)[:, None] * frequency[None, :]
    cosine, sine = np.cos(angles), np.sin(angles)
    shape = (parts, doc_rows + QLEN, LANES)
    return (
        np.concatenate([cosine] * 4, axis=1).astype(np.float32).reshape(shape),
        np.concatenate([-sine, sine, -sine, sine], axis=1).astype(np.float32).reshape(shape),
    )


def turn(tile, cosine, sine):
    first = lanes_of(tile.shape) % HEAD_DIM < HEAD_DIM // 2
    partner = jnp.where(first, pltpu.roll(tile, LANES - 32, 1), pltpu.roll(tile, 32, 1))
    return tile * cosine + partner * sine


def heads_kernel(doc_rows, len_ref, x_ref, w_ref, b_ref, cos_ref, sin_ref, q_ref, k_ref, v_ref):
    part = pl.program_id(0)
    rows = x_ref.shape[1]
    cosine, sine = cos_ref[0], sin_ref[0]
    lane = lanes_of((rows, LANES))
    row = lax.broadcasted_iota(jnp.int32, (rows, LANES), 0)
    allowed = (row >= doc_rows) | (part * doc_rows + row < len_ref[0])
    mask = jnp.where(allowed, 0.0, masked_score)
    width = w_ref.shape[1] // 3
    line = dot_nn(x_ref[0], w_ref[...]) + b_ref[...]
    for pair in range(width // LANES):
        here = pair * LANES
        query = turn(line[:, here : here + LANES], cosine, sine) * (log2e * HEAD_DIM**-0.5)
        key = turn(line[:, width + here : width + here + LANES], cosine, sine)
        value = line[:, 2 * width + here : 2 * width + here + LANES]
        for half in range(2):
            if half:
                query, key, value = (pltpu.roll(entry, 64, 1) for entry in (query, key, value))
            q_ref[2 * pair + half] = jnp.where(
                lane < 64, query, jnp.where(lane == 64, 1.0, 0.0)
            ).astype(BF)
            k_ref[2 * pair + half] = jnp.where(
                lane < 64, key, jnp.where(lane == 64, mask, jnp.where(lane < 68, 1.0, 0.0))
            ).astype(BF)
            v_ref[2 * pair + half] = jnp.where(
                lane < 64, value, jnp.where(lane < 67, 1.0, 0.0)
            ).astype(BF)


def project_heads(length, x_all, w_heads, b_heads, cosine, sine, doc_rows):
    parts, rows, _ = x_all.shape
    heads = w_heads.shape[1] // 3 // HEAD_DIM
    block = pl.BlockSpec((heads, rows, LANES), lambda part: (0, part, 0))
    shape = jax.ShapeDtypeStruct((heads, parts * rows, LANES), BF)
    table = pl.BlockSpec((1, rows, LANES), lambda part: (part, 0, 0))
    return pl.pallas_call(
        functools.partial(heads_kernel, doc_rows),
        grid=(parts,),
        in_specs=[
            pl.BlockSpec(memory_space=pltpu.SMEM),
            pl.BlockSpec((1, rows, D), lambda part: (part, 0, 0)),
            pl.BlockSpec(w_heads.shape, lambda part: (0, 0)),
            pl.BlockSpec(b_heads.shape, lambda part: (0, 0)),
            table,
            table,
        ],
        out_specs=[block] * 3,
        out_shape=[shape] * 3,
        compiler_params=params(),
        name="project_heads",
    )(length, x_all, w_heads, b_heads, cosine, sine)


def attend_rows(query, chunks):
    largest = jnp.full((query.shape[0], 1), -1e38, F32)
    total = jnp.zeros((query.shape[0], LANES), F32)
    for key, value in chunks:
        scores = dot_nt(query, key())
        newest = jnp.maximum(largest, jnp.max(scores, axis=1, keepdims=True))
        powers = jnp.exp2(scores - newest).astype(BF)
        total = total * jnp.exp2(largest - newest) + dot_nn(powers, value())
        largest = newest
    row_sum = total[:, 64:65]
    return total / row_sum, largest + jnp.log2(row_sum)


def attend_kernel(
    doc_rows, parts, q_ref, k_ref, v_ref, ko_ref, vo_ref, o_ref, full_ref, qa_ref
):
    rows = doc_rows + QLEN
    for span, own in ((slice(0, doc_rows), False), (slice(doc_rows, rows), True)):
        mixed = []
        for head in range(2):
            query = q_ref[head, span, :]
            lane = lanes_of(query.shape)
            if own:
                chunks = [(lambda: ko_ref[head], lambda: vo_ref[head])]
            else:
                chunks = [
                    (
                        lambda part=part: k_ref[head, part * rows : part * rows + doc_rows, :],
                        lambda part=part: v_ref[head, part * rows : part * rows + doc_rows, :],
                    )
                    for part in range(parts)
                ]
            out, log_sum = attend_rows(query, chunks)
            mixed.append(out)
            high, middle, low = split_three(-log_sum)
            qa_ref[head, span, :] = jnp.where(
                lane == 65,
                high,
                jnp.where(lane == 66, middle, jnp.where(lane == 67, low, query)),
            )
        joined = jnp.where(lanes_of(mixed[0].shape) < 64, mixed[0], pltpu.roll(mixed[1], 64, 1))
        full_ref[0, span, :] = joined
        o_ref[0, span, :] = joined.astype(BF)


def attend(query, key, value, parts, doc_rows):
    heads, total, _ = query.shape
    rows = total // parts
    own_at = rows // QLEN
    mine = pl.BlockSpec((2, rows, LANES), lambda pair, part: (pair, part, 0))
    whole = pl.BlockSpec((2, total, LANES), lambda pair, part: (pair, 0, 0))
    own = pl.BlockSpec((2, QLEN, LANES), lambda pair, part: (pair, part * own_at + own_at - 1, 0))
    flat = pl.BlockSpec((1, rows, LANES), lambda pair, part: (part, 0, pair))
    flops = 4 * heads * total * total * 256
    return pl.pallas_call(
        functools.partial(attend_kernel, doc_rows, parts),
        grid=(heads // 2, parts),
        in_specs=[mine, whole, whole, own, own],
        out_specs=[flat, flat, mine],
        out_shape=[
            jax.ShapeDtypeStruct((parts, rows, heads * HEAD_DIM), BF),
            jax.ShapeDtypeStruct((parts, rows, heads * HEAD_DIM), F32),
            jax.ShapeDtypeStruct(query.shape, BF),
        ],
        compiler_params=params(),
        cost_estimate=pl.CostEstimate(flops=flops, bytes_accessed=1 << 24, transcendentals=0),
        name="attend",
    )(query, key, value, key, value)


def attend_back_kernel(
    doc_rows,
    parts,
    q_ref,
    k_ref,
    v_ref,
    ko_ref,
    vo_ref,
    do_ref,
    o_ref,
    cos_ref,
    sin_ref,
    dq_ref,
    dk_ref,
    dv_ref,
    dk_doc,
    dv_doc,
    dk_own,
    dv_own,
):
    rows = doc_rows + QLEN
    at = pl.program_id(1)

    @pl.when(at == 0)
    def _():
        dk_doc[...] = jnp.zeros_like(dk_doc)
        dv_doc[...] = jnp.zeros_like(dv_doc)

    for span, own in ((slice(0, doc_rows), False), (slice(doc_rows, rows), True)):
        grad_pair = do_ref[0, span, :]
        lane = lanes_of(grad_pair.shape)
        product = grad_pair.astype(F32) * o_ref[0, span, :]
        turned = pltpu.roll(grad_pair.astype(F32), 64, 1).astype(BF)
        pieces = []
        for head in range(2):
            query = q_ref[head, span, :]
            inside = lane < 64 if head == 0 else lane >= 64
            row_dot = jnp.sum(jnp.where(inside, product, 0.0), axis=1, keepdims=True)
            high, middle, low = split_three(-row_dot)
            grad = jnp.where(
                lane < 64,
                turned if head else grad_pair,
                jnp.where(
                    lane == 64,
                    high,
                    jnp.where(
                        lane == 65, middle, jnp.where(lane == 66, low, jnp.zeros_like(grad_pair))
                    ),
                ),
            )
            query_t, grad_t = query.T, grad.T
            grad_query = jnp.zeros(query.shape, F32)
            for part in range(1 if own else parts):
                if own:
                    key, value = ko_ref[head], vo_ref[head]
                else:
                    key = k_ref[head, part * rows : part * rows + doc_rows, :]
                    value = v_ref[head, part * rows : part * rows + doc_rows, :]
                powers = jnp.exp2(dot_nt(query, key))
                grad_scores = (powers * dot_nt(grad, value)).astype(BF)
                if own:
                    dv_own[head, at] = dot_nn(grad_t, powers.astype(BF))
                    dk_own[head, at] = dot_nn(query_t, grad_scores)
                else:
                    dv_doc[head, part] += dot_nn(grad_t, powers.astype(BF))
                    dk_doc[head, part] += dot_nn(query_t, grad_scores)
                grad_query += dot_nn(grad_scores, key)
            pieces.append(grad_query)
        joined = jnp.where(lane < 64, pieces[0], pltpu.roll(pieces[1], 64, 1)) * HEAD_DIM**-0.5
        dq_ref[0, span, :] = turn(joined, cos_ref[at, span, :], -sin_ref[at, span, :]).astype(BF)

    @pl.when(at == parts - 1)
    def _():
        def both(kept, part):
            first, second = kept[0, part].T, kept[1, part].T
            return jnp.where(lanes_of(first.shape) < 64, first, pltpu.roll(second, 64, 1))

        for part in range(parts):
            for span, keys, values in (
                (slice(0, doc_rows), dk_doc, dv_doc),
                (slice(doc_rows, rows), dk_own, dv_own),
            ):
                grad_key = both(keys, part) * (1.0 / log2e)
                dk_ref[part, span, :] = turn(
                    grad_key, cos_ref[part, span, :], -sin_ref[part, span, :]
                ).astype(BF)
                dv_ref[part, span, :] = both(values, part).astype(BF)


def attend_back(query, key, value, grad, mixed, cosine, sine, doc_rows):
    heads, total, _ = query.shape
    parts, rows, width = grad.shape
    own_at = rows // QLEN
    mine = pl.BlockSpec((2, rows, LANES), lambda pair, part: (pair, part, 0))
    whole = pl.BlockSpec((2, total, LANES), lambda pair, part: (pair, 0, 0))
    own = pl.BlockSpec((2, QLEN, LANES), lambda pair, part: (pair, part * own_at + own_at - 1, 0))
    flat = pl.BlockSpec((1, rows, LANES), lambda pair, part: (part, 0, pair))
    full = pl.BlockSpec((parts, rows, LANES), lambda pair, part: (0, 0, pair))
    table = pl.BlockSpec((parts, rows, LANES), lambda pair, part: (0, 0, 0))
    shape = jax.ShapeDtypeStruct(grad.shape, BF)
    return pl.pallas_call(
        functools.partial(attend_back_kernel, doc_rows, parts),
        grid=(heads // 2, parts),
        in_specs=[mine, whole, whole, own, own, flat, flat, table, table],
        out_specs=[flat, full, full],
        out_shape=[shape] * 3,
        scratch_shapes=[
            pltpu.VMEM((2, parts, LANES, doc_rows), F32),
            pltpu.VMEM((2, parts, LANES, doc_rows), F32),
            pltpu.VMEM((2, parts, LANES, QLEN), F32),
            pltpu.VMEM((2, parts, LANES, QLEN), F32),
        ],
        compiler_params=params(),
        cost_estimate=pl.CostEstimate(
            flops=10 * heads * total * total * 256, bytes_accessed=1 << 24, transcendentals=0
        ),
        name="attend_back",
    )(query, key, value, key, value, grad, mixed, cosine, sine)


def normed(summed):
    centered = summed - jnp.mean(summed, axis=-1, keepdims=True)
    variance = jnp.mean(centered * centered, axis=-1, keepdims=True)
    inverse = lax.rsqrt(variance + norm_eps)
    return centered * inverse, inverse


def rows_kernel(
    att_ref,
    x_ref,
    wo_ref,
    wi_ref,
    wu_ref,
    wv_ref,
    bi_ref,
    vec_ref,
    hat1_ref,
    inv1_ref,
    low1_ref,
    act_ref,
    slope_ref,
    hat2_ref,
    inv2_ref,
    enc_ref,
    proj_ref,
    sum_ref,
):
    step = pl.program_id(0)
    parts, _, width = att_ref.shape

    @pl.when(step == 0)
    def _():
        summed = x_ref[...].astype(F32) + vec_ref[0:1, :]
        for part in range(parts):
            summed += dot_nn(att_ref[part], wo_ref[part * width : (part + 1) * width, :])
        hat, inverse = normed(summed)
        hat1_ref[...] = hat.astype(BF)
        inv1_ref[...] = jnp.broadcast_to(inverse, inv1_ref.shape)
        out = hat * vec_ref[1:2, :] + vec_ref[2:3, :]
        low1_ref[...] = out.astype(BF)
        sum_ref[...] = out + vec_ref[3:4, :]

    inner = dot_nn(low1_ref[...], wi_ref[...]) + bi_ref[...]
    share = 0.5 * lax.erf(inner * math.sqrt(0.5)) + 0.5
    act = (inner * share).astype(BF)
    act_ref[...] = act
    density = jnp.exp(inner * inner * -0.5) * (1.0 / math.sqrt(2.0 * math.pi))
    slope_ref[...] = (share + inner * density).astype(BF)
    sum_ref[...] += dot_nn(act, wu_ref[...])

    @pl.when(step == pl.num_programs(0) - 1)
    def _():
        hat, inverse = normed(sum_ref[...])
        hat2_ref[...] = hat.astype(BF)
        inv2_ref[...] = jnp.broadcast_to(inverse, inv2_ref.shape)
        low = (hat * vec_ref[4:5, :] + vec_ref[5:6, :]).astype(BF)
        enc_ref[...] = low
        proj_ref[...] = dot_nn(low, wv_ref[...])


def rows_forward(att, rows_in, wo, wi, wu, wv, inner_bias, vectors):
    rows = rows_in.shape[0]
    hidden = wi.shape[1]
    chunk = 512
    keep = lambda shape: pl.BlockSpec(shape, lambda step: (0,) * len(shape))
    columns = pl.BlockSpec((rows, chunk), lambda step: (0, step))
    wide = jax.ShapeDtypeStruct((rows, D), BF)
    thin = jax.ShapeDtypeStruct((rows, LANES), F32)
    big = jax.ShapeDtypeStruct((rows, hidden), BF)
    return pl.pallas_call(
        rows_kernel,
        grid=(hidden // chunk,),
        in_specs=[
            keep(att.shape),
            keep(rows_in.shape),
            keep(wo.shape),
            pl.BlockSpec((D, chunk), lambda step: (0, step)),
            pl.BlockSpec((chunk, D), lambda step: (step, 0)),
            keep(wv.shape),
            pl.BlockSpec((1, chunk), lambda step: (0, step)),
            keep(vectors.shape),
        ],
        out_specs=[
            keep((rows, D)),
            keep((rows, LANES)),
            keep((rows, D)),
            columns,
            columns,
            keep((rows, D)),
            keep((rows, LANES)),
            keep((rows, D)),
            keep((rows, LANES)),
        ],
        out_shape=[wide, thin, wide, big, big, wide, thin, wide, thin],
        scratch_shapes=[pltpu.VMEM((rows, D), F32)],
        compiler_params=params(),
        cost_estimate=pl.CostEstimate(
            flops=2 * rows * D * (D + 2 * hidden), bytes_accessed=1 << 25, transcendentals=0
        ),
        name="rows_forward",
    )(att, rows_in, wo, wi, wu, wv, inner_bias, vectors)


def norm_back(grad, hat, inverse, gain):
    scaled = grad * gain
    first = jnp.mean(scaled, axis=-1, keepdims=True)
    second = jnp.mean(scaled * hat, axis=-1, keepdims=True)
    return (scaled - first - hat * second) * inverse


def column_sum(value):
    return jnp.sum(value, axis=0, keepdims=True)


def rows_back_kernel(
    dproj_ref,
    enc_ref,
    hat2_ref,
    inv2_ref,
    wv_ref,
    act_ref,
    slope_ref,
    wu_ref,
    wi_ref,
    low1_ref,
    hat1_ref,
    inv1_ref,
    att_ref,
    wo_ref,
    vec_ref,
    dwv_ref,
    dwu_ref,
    dwi_ref,
    dbi_ref,
    dwo_ref,
    datt_ref,
    dsum_ref,
    dvec_ref,
    low_ref,
    total_ref,
):
    step = pl.program_id(0)
    parts, _, width = att_ref.shape

    @pl.when(step == 0)
    def _():
        dproj = dproj_ref[...]
        dwv_ref[...] = dot_tn(enc_ref[...], dproj).astype(BF)
        grad = dot_nt(dproj, wv_ref[...])
        hat = hat2_ref[...].astype(F32)
        dvec_ref[4:5, :] = column_sum(grad * hat)
        dvec_ref[5:6, :] = column_sum(grad)
        back = norm_back(grad, hat, inv2_ref[:, :1], vec_ref[4:5, :])
        low = back.astype(BF)
        low_ref[...] = low
        total_ref[...] = back
        dvec_ref[3:4, :] = column_sum(low.astype(F32))

    low = low_ref[...]
    dinner = (dot_nt(low, wu_ref[...]) * slope_ref[...].astype(F32)).astype(BF)
    dbi_ref[...] = column_sum(dinner.astype(F32))
    dwu_ref[...] = dot_tn(act_ref[...], low).astype(BF)
    dwi_ref[...] = dot_tn(low1_ref[...], dinner).astype(BF)
    total_ref[...] += dot_nt(dinner, wi_ref[...])

    @pl.when(step == pl.num_programs(0) - 1)
    def _():
        grad = total_ref[...]
        hat = hat1_ref[...].astype(F32)
        dvec_ref[1:2, :] = column_sum(grad * hat)
        dvec_ref[2:3, :] = column_sum(grad)
        back = norm_back(grad, hat, inv1_ref[:, :1], vec_ref[1:2, :])
        dsum_ref[...] = back
        attn_low = back.astype(BF)
        dvec_ref[0:1, :] = column_sum(attn_low.astype(F32))
        for part in range(parts):
            here = slice(part * width, (part + 1) * width)
            dwo_ref[here, :] = dot_tn(att_ref[part], attn_low).astype(BF)
            datt_ref[part] = dot_nt(attn_low, wo_ref[here, :]).astype(BF)


def rows_backward(
    dproj, enc, hat2, inv2, wv, act, slope, wu, wi, low1, hat1, inv1, att, wo, vectors
):
    rows, hidden = act.shape
    chunk = 512
    keep = lambda shape: pl.BlockSpec(shape, lambda step: (0,) * len(shape))
    columns = pl.BlockSpec((rows, chunk), lambda step: (0, step))
    up = pl.BlockSpec((chunk, D), lambda step: (step, 0))
    down = pl.BlockSpec((D, chunk), lambda step: (0, step))
    bias = pl.BlockSpec((1, chunk), lambda step: (0, step))
    operands = (dproj, enc, hat2, inv2, wv, act, slope, wu, wi, low1, hat1, inv1, att, wo, vectors)
    special = {5: columns, 6: columns, 7: up, 8: down}
    return pl.pallas_call(
        rows_back_kernel,
        grid=(hidden // chunk,),
        in_specs=[special.get(i, keep(entry.shape)) for i, entry in enumerate(operands)],
        out_specs=[
            keep(wv.shape),
            up,
            down,
            bias,
            keep(wo.shape),
            keep(att.shape),
            keep((rows, D)),
            keep((8, D)),
        ],
        out_shape=[
            jax.ShapeDtypeStruct(wv.shape, BF),
            jax.ShapeDtypeStruct(wu.shape, BF),
            jax.ShapeDtypeStruct(wi.shape, BF),
            jax.ShapeDtypeStruct((1, hidden), F32),
            jax.ShapeDtypeStruct(wo.shape, BF),
            jax.ShapeDtypeStruct(att.shape, BF),
            jax.ShapeDtypeStruct((rows, D), F32),
            jax.ShapeDtypeStruct((8, D), F32),
        ],
        scratch_shapes=[pltpu.VMEM((rows, D), BF), pltpu.VMEM((rows, D), F32)],
        compiler_params=params(),
        cost_estimate=pl.CostEstimate(
            flops=4 * rows * D * (D + 2 * hidden), bytes_accessed=1 << 26, transcendentals=0
        ),
        name="rows_backward",
    )(*operands)


def heads_back_kernel(x_ref, dq_ref, dk_ref, dv_ref, w_ref, dx_ref, dw_ref, db_ref, acc_ref):
    part = pl.program_id(0)
    width = dq_ref.shape[2]

    @pl.when(part == 0)
    def _():
        acc_ref[...] = jnp.zeros_like(acc_ref)
        db_ref[...] = jnp.zeros_like(db_ref)

    total = None
    for index, ref in enumerate((dq_ref, dk_ref, dv_ref)):
        here = slice(index * width, (index + 1) * width)
        grad = ref[0]
        term = dot_nt(grad, w_ref[:, here])
        total = term if total is None else total + term
        acc_ref[:, here] += dot_tn(x_ref[0], grad)
        db_ref[:, here] += column_sum(grad.astype(F32))
    dx_ref[0] = total.astype(BF)

    @pl.when(part == pl.num_programs(0) - 1)
    def _():
        dw_ref[...] = acc_ref[...].astype(BF)


def heads_backward(x_all, dq, dk, dv, w_heads):
    parts, rows, width = dq.shape
    flat = pl.BlockSpec((1, rows, width), lambda part: (part, 0, 0))
    wide = pl.BlockSpec((1, rows, D), lambda part: (part, 0, 0))
    return pl.pallas_call(
        heads_back_kernel,
        grid=(parts,),
        in_specs=[wide, flat, flat, flat, pl.BlockSpec(w_heads.shape, lambda part: (0, 0))],
        out_specs=[
            wide,
            pl.BlockSpec(w_heads.shape, lambda part: (0, 0)),
            pl.BlockSpec((1, 3 * width), lambda part: (0, 0)),
        ],
        out_shape=[
            jax.ShapeDtypeStruct(x_all.shape, BF),
            jax.ShapeDtypeStruct(w_heads.shape, BF),
            jax.ShapeDtypeStruct((1, 3 * width), F32),
        ],
        scratch_shapes=[pltpu.VMEM(w_heads.shape, F32)],
        compiler_params=params(),
        name="heads_backward",
    )(x_all, dq, dk, dv, w_heads)


class Exchange:
    def __init__(self, axis, size, send, recv):
        self.axis, self.size, self.send, self.recv = axis, size, send, recv
        self.me = lax.axis_index(axis)
        self.going = []

    def to(self, offset):
        return lax.rem(self.me + offset, self.size)

    def source(self, offset):
        return lax.rem(self.me - offset + self.size, self.size)

    def start(self, source_of, target_of):
        for offset in range(1, self.size):
            partner = self.to(offset)
            copy = pltpu.make_async_remote_copy(
                src_ref=source_of(partner),
                dst_ref=target_of(offset),
                send_sem=self.send.at[offset - 1],
                recv_sem=self.recv.at[offset - 1],
                device_id={self.axis: partner},
                device_id_type=pl.DeviceIdType.MESH,
            )
            copy.start()
            self.going.append(copy)

    def arrived(self):
        for copy in self.going:
            copy.wait_recv()

    def sent(self):
        for copy in self.going:
            copy.wait_send()


def greet(sizes):
    barrier = pltpu.get_barrier_semaphore()
    for axis, size in sizes.items():
        for offset in range(1, size):
            partner = lax.rem(lax.axis_index(axis) + offset, size)
            pl.semaphore_signal(
                barrier,
                inc=1,
                device_id={axis: partner},
                device_id_type=pl.DeviceIdType.MESH,
            )
    pl.semaphore_wait(barrier, sum(size - 1 for size in sizes.values()))


widths = (PROJ, PROJ * 3 // 4, PROJ // 2)
token_block = 1024


def unit(projected, columns):
    leading = jnp.where(lanes_of(projected.shape) < columns, projected, 0.0)
    inverse = lax.rsqrt(jnp.sum(leading * leading, axis=-1, keepdims=True) + vector_eps)
    return leading, inverse, (leading * inverse).astype(BF)


def unit_back(leading, inverse, grad):
    along = jnp.sum(leading * grad, axis=-1, keepdims=True)
    return grad * inverse - leading * (along * (inverse * inverse * inverse))


def exact(left, right):
    return lax.dot_general(
        left,
        right,
        (((1,), (0,)), ((), ())),
        precision=lax.Precision.HIGHEST,
        preferred_element_type=F32,
    )


def maxsim_kernel(
    n_dp,
    n_fs,
    pq_ref,
    pd_ref,
    mask_ref,
    label_ref,
    loss_ref,
    dq_ref,
    dd_ref,
    all_ref,
    power_ref,
    part_ref,
    score_ref,
    grad_ref,
    first_ref,
    total_ref,
    second_ref,
    *sems,
):
    tokens = n_dp * n_fs * QLEN
    blocks = tokens // token_block
    spots = label_ref.shape[1]
    my_dp, my_fs = lax.axis_index("dp"), lax.axis_index("fsdp")
    over = [
        Exchange(axis, n_dp if axis == "dp" else n_fs, sems[2 * i], sems[2 * i + 1])
        for i, axis in enumerate(("dp", "fsdp", "fsdp", "dp", "fsdp", "dp"))
    ]
    greet({"dp": n_dp, "fsdp": n_fs})

    own = all_ref.at[my_fs, my_dp]
    all_ref[my_fs, my_dp] = pq_ref[...]
    over[0].start(lambda partner: own, lambda offset: own)
    docs = [unit(pd_ref[...], columns) for columns in widths]
    over[0].arrived()
    over[1].start(lambda partner: all_ref.at[my_fs], lambda offset: all_ref.at[my_fs])
    over[1].arrived()

    def queries(block):
        every = all_ref[...].reshape(tokens, PROJ)
        return every[block * token_block : (block + 1) * token_block]

    def powers(index, block):
        similar = dot_nt(docs[index][2], unit(queries(block), widths[index])[2])
        return jnp.exp2(similar * (log2e / smooth_temp)) * mask_ref[:, :1]

    mine = part_ref.at[my_fs]
    part_ref[my_fs] = jnp.ones((8, tokens), F32)
    for block in range(blocks):
        here = slice(block * token_block, (block + 1) * token_block)
        for index in range(3):
            power = powers(index, block)
            if blocks == 1:
                power_ref[index] = power
            part_ref[my_fs, index : index + 1, here] = column_sum(power)
    over[2].start(lambda partner: mine, lambda offset: mine)
    over[2].arrived()
    total = part_ref[0]
    for source in range(1, n_fs):
        total = total + part_ref[source]

    token_of = lax.broadcasted_iota(jnp.int32, (tokens, spots), 0) // QLEN
    pool = jnp.where(token_of == lanes_of((tokens, spots)), 1.0, 0.0)
    score = exact(jnp.log(total), pool) * (smooth_temp / QLEN)
    score_ref[my_dp] = score
    row = score_ref.at[my_dp]
    over[3].start(lambda partner: row, lambda offset: row)
    over[3].arrived()
    logits = score_ref[...] * (1.0 / loss_temp)
    largest = jnp.max(logits, axis=0)
    log_sum = largest + jnp.log(jnp.sum(jnp.exp(logits - largest[None]), axis=0))
    label = label_ref[...]
    picked = jnp.zeros_like(log_sum)
    for index in range(n_dp):
        picked += jnp.where(label == index, logits[index], 0.0)
    loss_ref[...] = log_sum - picked
    dscore = jnp.exp(score * (1.0 / loss_temp) - log_sum) - jnp.where(label == my_dp, 1.0, 0.0)
    query_of = lax.broadcasted_iota(jnp.int32, (spots, tokens), 0)
    spread = jnp.where(lanes_of((spots, tokens)) // QLEN == query_of, 1.0, 0.0)
    factor = exact(dscore * (1.0 / (loss_temp * QLEN)), spread) / total

    grad_doc = [jnp.zeros(pd_ref.shape, F32)] * 3
    for block in range(blocks):
        here = slice(block * token_block, (block + 1) * token_block)
        grad_query = jnp.zeros((token_block, PROJ), F32)
        for index, columns in enumerate(widths):
            leading, inverse, vector = unit(queries(block), columns)
            power = power_ref[index] if blocks == 1 else powers(index, block)
            dsim = (power * factor[index : index + 1, here]).astype(BF)
            grad_query += unit_back(leading, inverse, dot_tn(dsim, docs[index][2]))
            grad_doc[index] += dot_nn(dsim, vector)
        if blocks == 1:
            grad_ref[...] = grad_query.reshape(grad_ref.shape)
        else:
            flat = block * token_block // QLEN
            count = token_block // QLEN
            grad_ref[flat // n_dp, flat % n_dp : flat % n_dp + count] = grad_query.reshape(
                count, QLEN, PROJ
            )
    over[4].start(lambda partner: grad_ref.at[partner], lambda offset: first_ref.at[offset - 1])
    dd = jnp.zeros(pd_ref.shape, F32)
    for index in range(3):
        dd += unit_back(docs[index][0], docs[index][1], grad_doc[index])
    dd_ref[...] = dd.astype(BF)
    over[4].arrived()
    summed = grad_ref[my_fs]
    for offset in range(n_fs - 1):
        summed = summed + first_ref[offset]
    total_ref[...] = summed
    over[5].start(lambda partner: total_ref.at[partner], lambda offset: second_ref.at[offset - 1])
    over[5].arrived()
    dq = total_ref[my_dp]
    for offset in range(n_dp - 1):
        dq = dq + second_ref[offset]
    dq_ref[...] = dq.astype(BF)
    for exchange in over:
        exchange.sent()


def maxsim(proj_query, proj_doc, doc_allowed, labels):
    n_dp, n_fs = lax.axis_size("dp"), lax.axis_size("fsdp")
    query_total = n_dp * n_fs
    tokens = query_total * QLEN
    blocks = tokens // token_block
    spots = -(-query_total // LANES) * LANES
    doc_rows = proj_doc.shape[0]
    ordered = jnp.transpose(labels).reshape(1, query_total)
    ordered = jnp.pad(ordered, ((0, 0), (0, spots - query_total)), constant_values=-1)
    mask = jnp.broadcast_to(doc_allowed[:, None], (doc_rows, LANES)).astype(F32)
    dma = lambda axis: [pltpu.SemaphoreType.DMA(((n_dp if axis == "dp" else n_fs) - 1,))] * 2
    whole = pl.BlockSpec(memory_space=pltpu.VMEM)
    loss, grad_query, grad_doc = pl.pallas_call(
        functools.partial(maxsim_kernel, n_dp, n_fs),
        in_specs=[whole] * 4,
        out_specs=[whole] * 3,
        out_shape=[
            jax.ShapeDtypeStruct((8, spots), F32),
            jax.ShapeDtypeStruct((QLEN, PROJ), BF),
            jax.ShapeDtypeStruct((doc_rows, PROJ), BF),
        ],
        scratch_shapes=[
            pltpu.VMEM((n_fs, n_dp, QLEN, PROJ), F32),
            pltpu.VMEM((3, doc_rows, token_block) if blocks == 1 else (3, 8, LANES), F32),
            pltpu.VMEM((n_fs, 8, tokens), F32),
            pltpu.VMEM((n_dp, 8, spots), F32),
            pltpu.VMEM((n_fs, n_dp, QLEN, PROJ), F32),
            pltpu.VMEM((n_fs - 1, n_dp, QLEN, PROJ), F32),
            pltpu.VMEM((n_dp, QLEN, PROJ), F32),
            pltpu.VMEM((n_dp - 1, QLEN, PROJ), F32),
        ]
        + [sem for axis in ("dp", "fsdp", "fsdp", "dp", "fsdp", "dp") for sem in dma(axis)],
        compiler_params=params(collective_id=1, has_side_effects=True),
        name="maxsim",
    )(proj_query, proj_doc, mask, jnp.broadcast_to(ordered, (8, spots)))
    losses = loss[:3, :query_total].reshape(3, n_fs, n_dp).transpose(0, 2, 1)
    return losses.reshape(3, query_total), grad_query, grad_doc


def other_core(parts):
    return [(part, part ^ 1) for part in range(parts)]


def other_chip(parts):
    return [(part, part ^ 2) for part in range(parts)]


def shards(
    doc_tokens,
    query_tokens,
    doc_lengths,
    labels,
    query_weight,
    query_bias,
    key_weight,
    key_bias,
    value_weight,
    value_bias,
    out_weight,
    out_bias,
    first_gain,
    first_shift,
    inner_weight,
    inner_bias,
    outer_weight,
    outer_bias,
    second_gain,
    second_shift,
    vector_weight,
):
    parts = lax.axis_size("fsdp")
    mine = lax.axis_index("fsdp")
    doc_rows = doc_tokens.shape[1]
    rows = doc_rows + QLEN
    width = D // parts
    split = query_weight.shape[0]

    w_split = jnp.concatenate(
        [
            entry[:, part * width : (part + 1) * width]
            for part in range(parts)
            for entry in (query_weight, key_weight, value_weight)
        ],
        axis=1,
    )
    w_split = lax.all_to_all(w_split, "fsdp", 1, 0, tiled=True)
    w_heads = lax.all_gather(w_split, "dp", axis=0, tiled=True)
    small = [
        query_bias,
        key_bias,
        value_bias,
        out_bias,
        first_gain,
        first_shift,
        outer_bias,
        second_gain,
        second_shift,
    ]
    hidden_split = inner_bias.shape[0]
    packed = lax.all_gather(jnp.concatenate(small + [inner_bias]), AXES, axis=0, tiled=False)
    packed = packed.astype(F32)

    def vector(index):
        return packed[:, index * split : (index + 1) * split].reshape(-1)

    inner_vec = packed[:, len(small) * split :].reshape(1, -1)
    vectors = jnp.stack([vector(i) for i in (3, 4, 5, 6, 7, 8)] + [jnp.zeros((D,), F32)] * 2)
    b_heads = jnp.concatenate(
        [lax.dynamic_slice(vector(i), (mine * width,), (width,)) for i in range(3)]
    ).reshape(1, -1)

    rows_in = jnp.concatenate([doc_tokens.reshape(doc_rows, D), query_tokens.reshape(QLEN, D)])
    x_all = lax.all_gather(rows_in, "fsdp")
    wo = lax.all_gather(out_weight, AXES, axis=0, tiled=True)
    wi = lax.all_gather(inner_weight, AXES, axis=0, tiled=True)
    wu = lax.all_gather(outer_weight, AXES, axis=0, tiled=True)
    wv = lax.all_gather(vector_weight, AXES, axis=0, tiled=True)

    tables = rope_tables(parts, doc_rows)
    cosine, sine = jnp.asarray(tables[0]), jnp.asarray(tables[1])
    query, key, value = project_heads(
        doc_lengths, x_all, w_heads, b_heads, cosine, sine, doc_rows
    )
    mixed, mixed_full, query_log = attend(query, key, value, parts, doc_rows)
    att = lax.all_to_all(mixed, "fsdp", 0, 0, tiled=True)
    hat1, inv1, low1, act, slope, hat2, inv2, enc, proj = rows_forward(
        att, rows_in, wo, wi, wu, wv, inner_vec, vectors
    )

    positions = mine * doc_rows + jnp.arange(doc_rows, dtype=jnp.int32)
    losses, grad_query, grad_doc = maxsim(
        proj[doc_rows:], proj[:doc_rows], positions < doc_lengths[0], labels
    )
    dproj = jnp.concatenate([grad_doc, grad_query])

    dwv, dwu, dwi, dbi, dwo, datt, dsum, dvec = rows_backward(
        dproj, enc, hat2, inv2, wv, act, slope, wu, wi, low1, hat1, inv1, att, wo, vectors
    )
    grad_mixed = lax.all_to_all(datt, "fsdp", 0, 0, tiled=True)
    dq, dk, dv = attend_back(query_log, key, value, grad_mixed, mixed_full, cosine, sine, doc_rows)
    dx, dw, db = heads_backward(x_all, dq, dk, dv, w_heads)

    core, chip = mine % 2, mine // 2
    by_core = dx.reshape(parts // 2, 2, rows, D)
    kept = lax.dynamic_index_in_dim(by_core, core, 1, False)
    sent = lax.dynamic_index_in_dim(by_core, 1 - core, 1, False)
    half = kept.astype(F32) + lax.ppermute(sent, "fsdp", other_core(parts)).astype(F32)
    away = lax.dynamic_index_in_dim(half, 1 - chip, 0, False).astype(BF)
    grad_rows = (
        dsum
        + lax.dynamic_index_in_dim(half, chip, 0, False)
        + lax.ppermute(away, "fsdp", other_chip(parts)).astype(F32)
    )
    grad_low = grad_rows.astype(BF)

    dw_dp = lax.psum_scatter(dw, "dp", scatter_dimension=0, tiled=True)
    dw_own = lax.all_to_all(dw_dp, "fsdp", 0, 1, tiled=True).astype(F32)
    dw_own = dw_own.reshape(split, parts, 3, width).transpose(2, 0, 1, 3).reshape(3, split, D)
    dwo_own = lax.psum_scatter(dwo, "dp", scatter_dimension=0, tiled=True)
    dwo_own = lax.psum_scatter(dwo_own, "fsdp", scatter_dimension=0, tiled=True).astype(F32)
    dwi_own = lax.psum_scatter(dwi, "dp", scatter_dimension=0, tiled=True)
    dwi_own = lax.psum_scatter(dwi_own, "fsdp", scatter_dimension=0, tiled=True).astype(F32)
    dwu_own = lax.psum_scatter(dwu, "dp", scatter_dimension=0, tiled=True)
    dwu_own = lax.psum_scatter(dwu_own, "fsdp", scatter_dimension=0, tiled=True).astype(F32)
    dwv_own = lax.psum_scatter(dwv, "dp", scatter_dimension=0, tiled=True)
    dwv_own = lax.psum_scatter(dwv_own, "fsdp", scatter_dimension=0, tiled=True).astype(F32)
    place = jnp.arange(parts, dtype=jnp.int32)[None, :, None] == mine
    db_all = jnp.where(place, db.reshape(3, 1, width), 0.0).reshape(3, D)
    vector_grads = jnp.concatenate([db_all, dvec[:6]]).reshape(9, -1, split).transpose(1, 0, 2)
    vector_grads = jnp.concatenate(
        [vector_grads.reshape(-1, 9 * split), dbi.reshape(-1, hidden_split)], axis=1
    )
    summed = lax.psum_scatter(vector_grads, AXES, scatter_dimension=0, tiled=False)
    vec_own = [summed[index * split : (index + 1) * split] for index in range(9)]
    dbi_own = summed[9 * split :]
    return (
        losses,
        enc[:doc_rows].reshape(1, doc_rows, D),
        enc[doc_rows:].reshape(1, 1, QLEN, D),
        grad_low[:doc_rows].reshape(1, doc_rows, D),
        grad_low[doc_rows:].reshape(1, 1, QLEN, D),
        dw_own[0],
        vec_own[0],
        dw_own[1],
        vec_own[1],
        dw_own[2],
        vec_own[2],
        dwo_own,
        vec_own[3],
        vec_own[4],
        vec_own[5],
        dwi_own,
        dbi_own,
        dwu_own,
        vec_own[6],
        vec_own[7],
        vec_own[8],
        dwv_own,
    )


def solution(mesh):
    rows = P(AXES, None)
    line = P(AXES)
    doc = P("dp", "fsdp", None)
    query = P("dp", "fsdp", None, None)
    weights = (rows, line) * 4 + (line, line, rows, line, rows, line, line, line, rows)
    return jax.shard_map(
        shards,
        mesh=mesh,
        in_specs=(doc, query, P("dp"), P()) + weights,
        out_specs=(P(), doc, query, doc, query) + weights,
        check_vma=False,
    )
```

time: 2520 us -> 1090 us (0.43)
  waiting for transfers between devices: 1330 us -> 535 us
  matrix products: 580 us -> 0 us
  Pallas kernels: 0 us -> 300 us
  local copies, waits for them, and re-layouts: 188 us -> 39.4 us
  other arithmetic: 155 us -> 19.8 us
  blocking collectives: 229 us -> 148 us
    reduce_scatter x10 -> x9, waiting for transfers between devices: 1210 us -> 392 us  [the longest x1 141 us: shards(): dwu_own = lax.psum_scatter(dwu, 'dp', scatter_dimension=0, tiled=True)]
    dot_general x142 -> x0, matrix products: 580 us -> none  [the longest x32 130 us: group_scores(): jnp.einsum('rhd,khd->hrk', query_heads, key_heads, preferred_element_type...]
    pallas_call x0 -> x7, Pallas kernels: none -> 300 us  [the longest x1 98.6 us: attend_back(): pl.pallas_call(functools.partial(attend_back_kernel, doc_rows, parts), gr...]
    reduce_sum x50 -> x0, other arithmetic: 99.6 us -> none  [the longest x16 85.2 us: attend_group(): row_total = jnp.sum(powers, axis=-1, keepdims=True)]
    all_gather x5 -> x1, blocking collectives: 146 us -> 57.6 us  [shards(): wv = lax.all_gather(vector_weight, AXES, axis=0, tiled=True)]
    dynamic_slice x106 -> x3, local copies, waits for them, and re-layouts: 86.4 us -> 0.22 us  [shards(): lax.dynamic_slice(vector(i), (mine * width,), (width,))]
    all_gather x8 -> x5, waiting for transfers between devices: 113 us -> 139 us  [the longest x1 79.1 us: shards(): wu = lax.all_gather(outer_weight, AXES, axis=0, tiled=True)]
  transfers between devices with their start and end apart: 18 -> 19, of which waited for: 13 -> 9; matrix products, arithmetic and copies ran while one was open for 20% -> 4% of each run, Pallas kernels for 0% -> 17%
where the time goes in v1:
time: 1090 us; the launch traced here: 1080 us
  waiting for transfers between devices  535 us (49%)
  Pallas kernels  300 us (28%)
  blocking collectives  148 us (14%)
  local copies, waits for them, and re-layouts  39.4 us (4%)
  other arithmetic  19.8 us (2%)
  starting transfers between devices  17.5 us (2%)
  between operations  15.3 us (1%)
    reduce_scatter x1, waiting for transfers between devices, shards(): dwu_own = lax.psum_scatter(dwu, 'dp', scatter_dimension=0, tiled=True)  141 us
    reduce_scatter x1, waiting for transfers between devices, shards(): dwi_own = lax.psum_scatter(dwi, 'dp', scatter_dimension=0, tiled=True)  100 us
    pallas_call x1, Pallas kernels, attend_back(): pl.pallas_call(functools.partial(attend_back_kernel, doc_rows, parts), gr...  98.6 us
    unnamed x2, blocking collectives  81.9 us
    all_gather x1, waiting for transfers between devices, shards(): wu = lax.all_gather(outer_weight, AXES, axis=0, tiled=True)  79.1 us
    reduce_scatter x1, waiting for transfers between devices, shards(): dw_dp = lax.psum_scatter(dw, 'dp', scatter_dimension=0, tiled=True)  67 us
    all_gather x1, blocking collectives, shards(): wv = lax.all_gather(vector_weight, AXES, axis=0, tiled=True)  57.6 us
    reduce_scatter x1, waiting for transfers between devices, shards(): dwv_own = lax.psum_scatter(dwv, 'dp', scatter_dimension=0, tiled=True)  53.2 us
  transfers between devices with their start and end apart: 19, of which 9 were waited for; matrix products, arithmetic and copies ran while one was open for 4% of the time, Pallas kernels for 17%

profile of v1, /device:TPU:1, one launch (start us, length us, event | category | flops | bytes accessed | tf_op | source)
XLA Modules:
  0.0 1075.2 jit_solution(17850785990702794122)
XLA Ops:
  7.2 0.7 constant_dynamic-update-slice_fusion.11
  8.0 0.7 constant_dynamic-update-slice_fusion.10
  8.7 0.7 constant_dynamic-update-slice_fusion.9
  9.4 0.7 constant_dynamic-update-slice_fusion.8
  10.1 0.7 constant_dynamic-update-slice_fusion.7
  10.8 0.7 constant_dynamic-update-slice_fusion.6
  11.6 0.7 constant_dynamic-update-slice_fusion.5
  12.3 0.7 constant_dynamic-update-slice_fusion.4
  13.0 0.7 constant_dynamic-update-slice_fusion.3
  13.7 0.7 constant_dynamic-update-slice_fusion.2
  14.4 0.7 constant_dynamic-update-slice_fusion.1
  15.1 0.7 constant_dynamic-update-slice_fusion
  15.9 8.8 all_to_all.42
  24.9 2.8 pad_maximum_fusion.x_ref
  27.7 0.7 all-gather.10.cloned.1.call-update
  30.1 40.2 %all-reduce.1 = bf16[13312]{0:T(1024)(128)(2,1)S(1)} all-reduce(bf16[13312]{0:T(1024)(128)(2,1)S(1)} %dynamic-update-slice), channel_id=3, replica_groups=mesh['dp'=8,'fsdp'=4] {'dp','fsdp'}, use_global_device_ids=true, to_apply=%add.1 | all-reduce | flops 13312 | bytes 53248
  72.2 46.4 %all-gather.16.cloned.1.call-done = bf16[3200,1024]{1,0:T(8,128)(2,1)} async-done(((bf16[800,1024]{1,0:T(8,128)(2,1)}), bf16[3200,1024]{1,0:T(8,128)(2,1)}) %all-gather.16.cloned.1.call-update) | async-done | bytes 6553616 | tf_op jit(solution)/shard_map/all_gather | solution.py:902
  118.7 12.4 %project_heads.1 = (bf16[4,3200,128]{2,1,0:T(8,128)(2,1)}, bf16[4,3200,128]{2,1,0:T(8,128)(2,1)}, bf16[4,3200,128]{2,1,0:T(8,128)(2,1)}) custom-call(s32[1]{0:T(128)} %copy.104.len_ref, bf16[4,800,1024]{2,1,0:T(8,128)(2,1)} %bitcast.63, bf16[1024,768]{1,0:T(8,128)(2,1)} %all-gather.8.cloned.1.call-done.w_ref, f32[1,768]{1,0:T(1,128)} %reshape.155.b_ref, ...), custom_call_target="tpu_custom_call" | custom-call | tf_op jit(solution)/shard_map/project_heads/pallas_call | solution.py:115
  131.0 51.4 %attend.1 = (bf16[4,800,256]{2,1,0:T(8,128)(2,1)}, f32[4,800,256]{2,1,0:T(8,128)}, bf16[4,3200,128]{2,1,0:T(8,128)(2,1)}) custom-call(bf16[4,3200,128]{2,1,0:T(8,128)(2,1)} %get-tuple-element.54.q_ref, bf16[4,3200,128]{2,1,0:T(8,128)(2,1)} %get-tuple-element.55.k_ref.ko_ref, bf16[4,3200,128]{2,1,0:T(8,128)(2,1)} %get-tuple-element.56.v_ref.vo_ref, ...), custom_call_target="tpu_custom_call" | custom-call | flops 41943040000 | bytes 16777216 | tf_op jit(solution)/shard_map/attend/pallas_call | solution.py:187
  182.4 3.9 all-to-all-start.1
  188.3 57.6 %all_gather.35.wv_ref = bf16[1024,128]{1,0:T(8,128)(2,1)} all-gather(bf16[32,128]{1,0:T(8,128)(2,1)S(1)} %copy-done.7), channel_id=1, replica_groups=mesh['dp'=8,'fsdp'=4] {'dp','fsdp'}, dimensions={0}, use_global_device_ids=true | all-gather | bytes 270336 | tf_op jit(solution)/shard_map/all_gather | solution.py:906
  246.0 13.3 %all-gather.12.cloned.1.call-done.wi_ref = bf16[1024,4096]{1,0:T(8,128)(2,1)} async-done(((bf16[32,4096]{1,0:T(8,128)(2,1)}), bf16[1024,4096]{1,0:T(8,128)(2,1)}) %all-gather.12.cloned.1.call-update) | async-done | bytes 8388624 | tf_op jit(solution)/shard_map/all_gather | solution.py:904
  259.3 79.1 %all-gather.14.cloned.1.call-done.wu_ref = bf16[4096,1024]{1,0:T(8,128)(2,1)} async-done(((bf16[128,1024]{1,0:T(8,128)(2,1)}), bf16[4096,1024]{1,0:T(8,128)(2,1)}) %all-gather.14.cloned.1.call-update) | async-done | bytes 8388624 | tf_op jit(solution)/shard_map/all_gather | solution.py:905
  338.4 30.2 %rows_forward.1 = (bf16[800,1024]{1,0:T(8,128)(2,1)}, f32[800,128]{1,0:T(8,128)}, bf16[800,1024]{1,0:T(8,128)(2,1)}, bf16[800,4096]{1,0:T(8,128)(2,1)}, bf16[800...) custom-call(bf16[4,800,256]{2,1,0:T(8,128)(2,1)} %copy-done.3, ...), custom_call_target="tpu_custom_call" | custom-call | flops 15099494400 | bytes 33554432 | tf_op jit(solution)/shard_map/rows_forward/pallas_call | solution.py:392
  368.6 1.8 slice.185.pd_ref
  370.4 1.3 slice.184.pq_ref
  371.7 0.9 broadcast_in_dim.42.mask_ref
  373.2 38.4 %maxsim.1 = (f32[8,128]{1,0:T(8,128)}, bf16[32,128]{1,0:T(8,128)(2,1)}, bf16[768,128]{1,0:T(8,128)(2,1)}) custom-call(f32[32,128]{1,0:T(8,128)} %slice.184.pq_ref, f32[768,128]{1,0:T(8,128)} %slice.185.pd_ref, f32[768,128]{1,0:T(8,128)} %broadcast_in_dim.42.mask_ref, s32[8,128]{1,0:T(8,128)} %broadcast_in_dim.44.label_ref), custom_call_target="tpu_custom_call" | custom-call | tf_op jit(solution)/shard_map/maxsim/pallas_call | solution.py:802
  411.6 1.6 pad_maximum_fusion.2.dproj_ref
  413.3 51.4 %rows_backward.1 = (bf16[1024,128]{1,0:T(8,128)(2,1)}, bf16[4096,1024]{1,0:T(8,128)(2,1)}, bf16[1024,4096]{1,0:T(8,128)(2,1)}, f32[1,4096]{1,0:T(1,128)}, bf16[1...) custom-call(bf16[800,128]{1,0:T(8,128)(2,1)} %pad_maximum_fusion.2.dproj_ref, ...), custom_call_target="tpu_custom_call" | custom-call | flops 30198988800 | bytes 67108864 | tf_op jit(solution)/shard_map/rows_backward/pallas_call | solution.py:516
  464.8 0.7 reduce-scatter.13.cloned.1.call-update
  465.5 0.7 reduce-scatter.17.cloned.1.call-update
  466.3 0.7 reduce-scatter.21.cloned.1.call-update
  467.0 3.6 all-to-all-start.2
  470.6 53.2 %reduce-scatter.25.cloned.1.call-done = bf16[128,128]{1,0:T(8,128)(2,1)} async-done(((bf16[1024,128]{1,0:T(8,128)(2,1)}), bf16[128,128]{1,0:T(8,128)(2,1)}) %reduce-scatter.25.cloned.1.call-update) | async-done | bytes 32784 | tf_op jit(solution)/shard_map/reduce_scatter | solution.py:954
  523.9 1.2 copy-done.4
  525.1 98.6 %attend_back.1 = (bf16[4,800,256]{2,1,0:T(8,128)(2,1)}, bf16[4,800,256]{2,1,0:T(8,128)(2,1)}, bf16[4,800,256]{2,1,0:T(8,128)(2,1)}) custom-call(bf16[4,3200,128]{2,1,0:T(8,128)(2,1)} %get-tuple-element.71.q_ref, bf16[4,3200,128]{2,1,0:T(8,128)(2,1)} %get-tuple-element.55.k_ref.ko_ref, bf16[4,3200,128]{2,1,0:T(8,128)(2,1)} %get-tuple-element.56.v_ref.vo_ref, ...), custom_call_target="tpu_custom_call" | custom-call | flops 104857600000 | bytes 16777216 | tf_op jit(solution)/shard_map/attend_back/pallas_call | solution.py:303
  623.7 17.4 %heads_backward.1 = (bf16[4,800,1024]{2,1,0:T(8,128)(2,1)}, bf16[1024,768]{1,0:T(8,128)(2,1)}, f32[1,768]{1,0:T(1,128)}) custom-call(bf16[4,800,1024]{2,1,0:T(8,128)(2,1)} %bitcast.64, bf16[4,800,256]{2,1,0:T(8,128)(2,1)} %get-tuple-element.74.dq_ref, bf16[4,800,256]{2,1,0:T(8,128)(2,1)} %get-tuple-element.75.dk_ref, ...), custom_call_target="tpu_custom_call" | custom-call | tf_op jit(solution)/shard_map/heads_backward/pallas_call | solution.py:577
  641.2 4.1 dynamic-slice_bitcast_fusion
  645.3 2.5 collective-permute-start
  647.9 100.0 %reduce-scatter.17.cloned.1.call-done = bf16[128,4096]{1,0:T(8,128)(2,1)} async-done(((bf16[1024,4096]{1,0:T(8,128)(2,1)}), bf16[128,4096]{1,0:T(8,128)(2,1)}) %reduce-scatter.17.cloned.1.call-update) | async-done | bytes 1048592 | tf_op jit(solution)/shard_map/reduce_scatter | solution.py:950
  748.0 3.4 convert_add_fusion
  751.5 2.8 copy-done
  754.2 1.5 fusion.2
  755.7 1.2 collective-permute-start.1
  758.2 1.3 slice_bitcast_fusion.1
  759.5 140.6 %reduce-scatter.21.cloned.1.call-done = bf16[512,1024]{1,0:T(8,128)(2,1)} async-done(((bf16[4096,1024]{1,0:T(8,128)(2,1)}), bf16[512,1024]{1,0:T(8,128)(2,1)}) %reduce-scatter.21.cloned.1.call-update) | async-done | bytes 1048592 | tf_op jit(solution)/shard_map/reduce_scatter | solution.py:952
  900.7 19.5 %reduce-scatter.27.cloned.1.call-done = bf16[32,128]{1,0:T(8,128)(2,1)} async-done(((bf16[128,128]{1,0:T(8,128)(2,1)}), bf16[32,128]{1,0:T(8,128)(2,1)}) %reduce-scatter.27.cloned.1.call-update) | async-done | bytes 8208 | tf_op jit(solution)/shard_map/reduce_scatter | solution.py:955
  920.1 1.3 convert_element_type.61
  921.7 67.0 %reduce-scatter.11.cloned.1.call-done = bf16[128,768]{1,0:T(8,128)(2,1)} async-done(((bf16[1024,768]{1,0:T(8,128)(2,1)}), bf16[128,768]{1,0:T(8,128)(2,1)}) %reduce-scatter.11.cloned.1.call-update) | async-done | bytes 196624 | tf_op jit(solution)/shard_map/reduce_scatter | solution.py:945
  988.7 5.8 all-to-all-start.3
  994.6 41.7 %all-reduce.2 = f32[32,416]{0,1:T(8,128)S(1)} all-reduce(f32[32,416]{0,1:T(8,128)S(1)} %pad_maximum_fusion.1), channel_id=5, replica_groups=mesh['dp'=8,'fsdp'=4] {'dp','fsdp'}, use_global_device_ids=true, to_apply=%region_1.2.clone | all-reduce | flops 13312 | bytes 106496
  1036.3 0.7 dynamic-slice_reduce_fusion
  1037.0 0.9 dynamic-slice_reduce_fusion.1
  1037.8 1.8 convert_bitcast_fusion
  1039.7 2.0 reshape.168
  1041.7 2.0 fusion.4
  1044.6 0.7 copy.88
  1046.0 1.5 convert_element_type.58
  1047.5 3.6 fusion.1
  1051.8 1.3 slice_bitcast_fusion
  1053.0 1.8 convert_element_type.59
  1054.8 11.8 %reduce-scatter.23.cloned.1.call-done = bf16[128,1024]{1,0:T(8,128)(2,1)} async-done(((bf16[512,1024]{1,0:T(8,128)(2,1)}), bf16[128,1024]{1,0:T(8,128)(2,1)}) %reduce-scatter.23.cloned.1.call-update) | async-done | bytes 262160 | tf_op jit(solution)/shard_map/reduce_scatter | solution.py:953
  1066.6 1.8 convert_element_type.60
  (126 shorter events, 10.4 us)
Async XLA Ops:
  7.2 65.0 %all-gather.8.cloned.1.call-start = ((), (), s32[]{:S(2)}) async-start(), calls=%async_computation.13 | async-start | bytes 1769472 | tf_op jit(solution)/shard_map/all_gather | solution.py:876
  24.7 94.0 %all-gather.16.cloned.1.call-start = ((), (), s32[]{:S(2)}) async-start(), calls=%async_computation.26 | async-start | bytes 8192000 | tf_op jit(solution)/shard_map/all_gather | solution.py:902
  24.7 4.9 copy-start.11
  24.8 4.9 copy-start.12
  24.8 4.9 copy-start.13
  24.8 4.9 copy-start.14
  24.8 4.9 copy-start.15
  24.8 4.9 copy-start.16
  24.8 4.8 copy-start.17
  24.8 4.8 copy-start.18
  24.8 4.8 copy-start.19
  24.9 4.8 copy-start.20
  27.7 218.2 %all-gather.10.cloned.1.call-start = ((), (), s32[]{:S(2)}) async-start(), calls=%async_computation.14 | async-start | bytes 2162688 | tf_op jit(solution)/shard_map/all_gather | solution.py:903
  28.4 230.8 %all-gather.12.cloned.1.call-start = ((), (), s32[]{:S(2)}) async-start(), calls=%async_computation.15 | async-start | bytes 8650752 | tf_op jit(solution)/shard_map/all_gather | solution.py:904
  29.0 309.4 %all-gather.14.cloned.1.call-start = ((), (), s32[]{:S(2)}) async-start(), calls=%async_computation.16 | async-start | bytes 8650752 | tf_op jit(solution)/shard_map/all_gather | solution.py:905
  182.4 5.1 copy-start.9
  182.4 5.9 copy-start.7
  182.4 63.5 %all-to-all-start.1 = ((bf16[4,800,256]{2,1,0:T(8,128)(2,1)}), bf16[4,800,256]{2,1,0:T(8,128)(2,1)S(1)}, u32[]{:S(2)}, u32[]{:S(2)}) async-start(bf16[4,800,256]{2,1,0:T(8,128)(2,1)} %get-tuple-element.57), calls=%async_computation.1 | async-start | bytes 3276800 | tf_op jit(solution)/shard_map/all_to_all | solution.py:914
  186.4 337.5 %reduce-scatter.25.cloned.1.call-start = ((), (), s32[]{:S(2)}) async-start(), calls=%async_computation.24 | async-start | bytes 294912 | tf_op jit(solution)/shard_map/reduce_scatter | solution.py:954
  245.9 92.5 %copy-start.3 = (bf16[4,800,256]{2,1,0:T(8,128)(2,1)}, bf16[4,800,256]{2,1,0:T(8,128)(2,1)S(1)}, u32[]{:S(2)}) copy-start(bf16[4,800,256]{2,1,0:T(8,128)(2,1)S(1)} %all-to-all-done.1.att_ref) | copy-start | bytes 4915204
  464.7 183.1 %reduce-scatter.13.cloned.1.call-start = ((), (), s32[]{:S(2)}) async-start(), calls=%async_computation.18 | async-start | bytes 2359296 | tf_op jit(solution)/shard_map/reduce_scatter | solution.py:948
  465.5 282.4 %reduce-scatter.17.cloned.1.call-start = ((), (), s32[]{:S(2)}) async-start(), calls=%async_computation.20 | async-start | bytes 9437184 | tf_op jit(solution)/shard_map/reduce_scatter | solution.py:950
  466.2 433.8 %reduce-scatter.21.cloned.1.call-start = ((), (), s32[]{:S(2)}) async-start(), calls=%async_computation.22 | async-start | bytes 9437184 | tf_op jit(solution)/shard_map/reduce_scatter | solution.py:952
  467.0 56.9 %all-to-all-start.2 = ((bf16[4,800,256]{2,1,0:T(8,128)(2,1)}), bf16[4,800,256]{2,1,0:T(8,128)(2,1)S(1)}, u32[]{:S(2)}, u32[]{:S(2)}) async-start(bf16[4,800,256]{2,1,0:T(8,128)(2,1)} %get-tuple-element.72), calls=%async_computation.2 | async-start | bytes 3276800 | tf_op jit(solution)/shard_map/all_to_all | solution.py:928
  470.5 449.6 %reduce-scatter.27.cloned.1.call-start = ((), (), s32[]{:S(2)}) async-start(), calls=%async_computation.25 | async-start | bytes 40960 | tf_op jit(solution)/shard_map/reduce_scatter | solution.py:955
  523.9 464.9 %reduce-scatter.11.cloned.1.call-start = ((), (), s32[]{:S(2)}) async-start(), calls=%async_computation.17 | async-start | bytes 1769472 | tf_op jit(solution)/shard_map/reduce_scatter | solution.py:945
  523.9 1.2 copy-start.4
  641.1 404.9 %reduce-scatter.15.cloned.1.call-start = ((), (), s32[]{:S(2)}) async-start(), calls=%async_computation.19 | async-start | bytes 327680 | tf_op jit(solution)/shard_map/reduce_scatter | solution.py:949
  645.3 102.7 %collective-permute-start = (bf16[2,800,1024]{2,1,0:T(8,128)(2,1)}, bf16[2,800,1024]{2,1,0:T(8,128)(2,1)S(1)}, u32[]{:S(2)}, u32[]{:S(2)}) collective-permute-start(bf16[2,800,1024]{2,1,0:T(8,128)(2,1)} %dynamic-slice_bitcast_fusion), channel_id=1, source_target_pairs={{0,1},{1,0},{2,3},{3,2},{4,5},{5,4},{6,7},{7,6},{8,9},{9,8},{10,11... | collective-permute-start | bytes 9830408 | tf_op jit(solution)/shard_map/ppermute | solution.py:936
  647.8 405.2 %reduce-scatter.19.cloned.1.call-start = ((), (), s32[]{:S(2)}) async-start(), calls=%async_computation.21 | async-start | bytes 1310720 | tf_op jit(solution)/shard_map/reduce_scatter | solution.py:951
  747.9 318.7 %reduce-scatter.23.cloned.1.call-start = ((), (), s32[]{:S(2)}) async-start(), calls=%async_computation.23 | async-start | bytes 1310720 | tf_op jit(solution)/shard_map/reduce_scatter | solution.py:953
  751.5 2.8 copy-start
  754.2 2.8 copy-start.5
  754.2 3.0 copy-start.6
  754.2 3.1 copy-start.10
  754.2 4.0 copy-start.2
  755.7 291.8 %collective-permute-start.1 = (bf16[800,1024]{1,0:T(8,128)(2,1)}, bf16[800,1024]{1,0:T(8,128)(2,1)}, u32[]{:S(2)}, u32[]{:S(2)}) collective-permute-start(bf16[800,1024]{1,0:T(8,128)(2,1)} %fusion.2), channel_id=1, source_target_pairs={{0,2},{1,3},{2,0},{3,1},{4,6},{5,7},{6,4},{7,5},{8,10},{9,11},{10,... | collective-permute-start | bytes 4915208 | tf_op jit(solution)/shard_map/ppermute | solution.py:941
  758.2 163.2 %copy-start.8 = (f32[1,768]{1,0:T(1,128)S(1)}, f32[1,768]{1,0:T(1,128)}, u32[]{:S(2)}) copy-start(f32[1,768]{1,0:T(1,128)} %get-tuple-element.79) | copy-start | bytes 9220
  988.7 49.1 %all-to-all-start.3 = ((bf16[4,32,768]{2,1,0:T(8,128)(2,1)}), bf16[4,32,768]{2,1,0:T(8,128)(2,1)}, u32[]{:S(2)}, u32[]{:S(2)}) async-start(bf16[4,32,768]{2,1,0:T(8,128)(2,1)} %bitcast.76), calls=%async_computation.4 | async-start | bytes 393216 | tf_op jit(solution)/shard_map/all_to_all | solution.py:946
  1037.0 10.6 copy-start.1
Sparse Core Ops, SparseCore 0:
  24.8 44.4 all-gather.7
  70.8 47.7 all-gather.15
  121.5 56.3 all-gather.9
  180.7 78.5 all-gather.11
  262.0 76.3 all-gather.13
  464.8 58.9 reduce-scatter.24
  527.4 66.9 reduce-scatter.12
  598.0 149.8 reduce-scatter.16
  752.0 147.9 reduce-scatter.20
  902.3 17.8 reduce-scatter.26
  924.5 64.1 reduce-scatter.10
  991.1 20.0 reduce-scatter.14
  1013.9 26.1 reduce-scatter.18
  1042.4 24.1 reduce-scatter.22

commit v2 on v1

--- a/solution.py
+++ b/solution.py
@@ -215,18 +215,20 @@
     dq_ref,
     dk_ref,
     dv_ref,
+    sums_ref,
     dk_doc,
     dv_doc,
     dk_own,
     dv_own,
 ):
     rows = doc_rows + QLEN
-    at = pl.program_id(1)
+    at = pl.program_id(0)
 
     @pl.when(at == 0)
     def _():
         dk_doc[...] = jnp.zeros_like(dk_doc)
         dv_doc[...] = jnp.zeros_like(dv_doc)
+        sums_ref[...] = jnp.zeros_like(sums_ref)
 
     for span, own in ((slice(0, doc_rows), False), (slice(doc_rows, rows), True)):
         grad_pair = do_ref[0, span, :]
@@ -269,7 +271,9 @@
                 grad_query += dot_nn(grad_scores, key)
             pieces.append(grad_query)
         joined = jnp.where(lane < 64, pieces[0], pltpu.roll(pieces[1], 64, 1)) * HEAD_DIM**-0.5
-        dq_ref[0, span, :] = turn(joined, cos_ref[at, span, :], -sin_ref[at, span, :]).astype(BF)
+        low = turn(joined, cos_ref[at, span, :], -sin_ref[at, span, :]).astype(BF)
+        dq_ref[0, span, :] = low
+        sums_ref[0:1, :] += column_sum(low.astype(F32))
 
     @pl.when(at == parts - 1)
     def _():
@@ -283,29 +287,36 @@
                 (slice(doc_rows, rows), dk_own, dv_own),
             ):
                 grad_key = both(keys, part) * (1.0 / log2e)
-                dk_ref[part, span, :] = turn(
-                    grad_key, cos_ref[part, span, :], -sin_ref[part, span, :]
-                ).astype(BF)
-                dv_ref[part, span, :] = both(values, part).astype(BF)
-
-
-def attend_back(query, key, value, grad, mixed, cosine, sine, doc_rows):
+                low = turn(grad_key, cos_ref[part, span, :], -sin_ref[part, span, :]).astype(BF)
+                dk_ref[part, span, :] = low
+                sums_ref[1:2, :] += column_sum(low.astype(F32))
+                low = both(values, part).astype(BF)
+                dv_ref[part, span, :] = low
+                sums_ref[2:3, :] += column_sum(low.astype(F32))
+
+
+def attend_back(pair, query, key, value, grad, mixed, cosine, sine, doc_rows):
     heads, total, _ = query.shape
     parts, rows, width = grad.shape
     own_at = rows // QLEN
-    mine = pl.BlockSpec((2, rows, LANES), lambda pair, part: (pair, part, 0))
-    whole = pl.BlockSpec((2, total, LANES), lambda pair, part: (pair, 0, 0))
-    own = pl.BlockSpec((2, QLEN, LANES), lambda pair, part: (pair, part * own_at + own_at - 1, 0))
-    flat = pl.BlockSpec((1, rows, LANES), lambda pair, part: (part, 0, pair))
-    full = pl.BlockSpec((parts, rows, LANES), lambda pair, part: (0, 0, pair))
-    table = pl.BlockSpec((parts, rows, LANES), lambda pair, part: (0, 0, 0))
-    shape = jax.ShapeDtypeStruct(grad.shape, BF)
+    mine = pl.BlockSpec((2, rows, LANES), lambda part: (pair, part, 0))
+    whole = pl.BlockSpec((2, total, LANES), lambda part: (pair, 0, 0))
+    own = pl.BlockSpec((2, QLEN, LANES), lambda part: (pair, part * own_at + own_at - 1, 0))
+    flat = pl.BlockSpec((1, rows, LANES), lambda part: (part, 0, pair))
+    table = pl.BlockSpec((parts, rows, LANES), lambda part: (0, 0, 0))
+    full = pl.BlockSpec((parts, rows, LANES), lambda part: (0, 0, 0))
+    shape = jax.ShapeDtypeStruct((parts, rows, LANES), BF)
     return pl.pallas_call(
         functools.partial(attend_back_kernel, doc_rows, parts),
-        grid=(heads // 2, parts),
+        grid=(parts,),
         in_specs=[mine, whole, whole, own, own, flat, flat, table, table],
-        out_specs=[flat, full, full],
-        out_shape=[shape] * 3,
+        out_specs=[
+            pl.BlockSpec((1, rows, LANES), lambda part: (part, 0, 0)),
+            full,
+            full,
+            pl.BlockSpec((8, LANES), lambda part: (0, 0)),
+        ],
+        out_shape=[shape] * 3 + [jax.ShapeDtypeStruct((8, LANES), F32)],
         scratch_shapes=[
             pltpu.VMEM((2, parts, LANES, doc_rows), F32),
             pltpu.VMEM((2, parts, LANES, doc_rows), F32),
@@ -314,7 +325,7 @@
         ],
         compiler_params=params(),
         cost_estimate=pl.CostEstimate(
-            flops=10 * heads * total * total * 256, bytes_accessed=1 << 24, transcendentals=0
+            flops=10 * 2 * total * total * 256, bytes_accessed=1 << 24, transcendentals=0
         ),
         name="attend_back",
     )(query, key, value, key, value, grad, mixed, cosine, sine)
@@ -325,6 +336,30 @@
     variance = jnp.mean(centered * centered, axis=-1, keepdims=True)
     inverse = lax.rsqrt(variance + norm_eps)
     return centered * inverse, inverse
+
+
+GROUPS = 4
+CHUNK = 512
+
+
+def joined_up(up_ref):
+    size = up_ref.shape[0] // (CHUNK // (QLEN * GROUPS))
+    pieces = [
+        up_ref[at : at + size, group * D : (group + 1) * D]
+        for at in range(0, up_ref.shape[0], size)
+        for group in range(GROUPS)
+    ]
+    return jnp.concatenate(pieces, axis=0)
+
+
+def packed_specs():
+    hidden = GROUPS * D
+    return {
+        "up": pl.BlockSpec((CHUNK // GROUPS, hidden), lambda step: (step, 0)),
+        "down": pl.BlockSpec((D, CHUNK), lambda step: (0, hidden // CHUNK + step)),
+        "out": pl.BlockSpec((D, D), lambda step: (0, 2 * hidden // D)),
+        "vector": pl.BlockSpec((D, LANES), lambda step: (0, (2 * hidden + D) // LANES)),
+    }
 
 
 def rows_kernel(
@@ -362,13 +397,14 @@
         low1_ref[...] = out.astype(BF)
         sum_ref[...] = out + vec_ref[3:4, :]
 
+    up = joined_up(wu_ref)
     inner = dot_nn(low1_ref[...], wi_ref[...]) + bi_ref[...]
     share = 0.5 * lax.erf(inner * math.sqrt(0.5)) + 0.5
     act = (inner * share).astype(BF)
     act_ref[...] = act
     density = jnp.exp(inner * inner * -0.5) * (1.0 / math.sqrt(2.0 * math.pi))
     slope_ref[...] = (share + inner * density).astype(BF)
-    sum_ref[...] += dot_nn(act, wu_ref[...])
+    sum_ref[...] += dot_nn(act, up)
 
     @pl.when(step == pl.num_programs(0) - 1)
     def _():
@@ -380,10 +416,11 @@
         proj_ref[...] = dot_nn(low, wv_ref[...])
 
 
-def rows_forward(att, rows_in, wo, wi, wu, wv, inner_bias, vectors):
+def rows_forward(att, rows_in, packed, inner_bias, vectors):
     rows = rows_in.shape[0]
-    hidden = wi.shape[1]
-    chunk = 512
+    hidden = inner_bias.shape[1]
+    chunk = CHUNK
+    weights = packed_specs()
     keep = lambda shape: pl.BlockSpec(shape, lambda step: (0,) * len(shape))
     columns = pl.BlockSpec((rows, chunk), lambda step: (0, step))
     wide = jax.ShapeDtypeStruct((rows, D), BF)
@@ -395,10 +432,10 @@
         in_specs=[
             keep(att.shape),
             keep(rows_in.shape),
-            keep(wo.shape),
-            pl.BlockSpec((D, chunk), lambda step: (0, step)),
-            pl.BlockSpec((chunk, D), lambda step: (step, 0)),
-            keep(wv.shape),
+            weights["out"],
+            weights["down"],
+            weights["up"],
+            weights["vector"],
             pl.BlockSpec((1, chunk), lambda step: (0, step)),
             keep(vectors.shape),
         ],
@@ -420,7 +457,7 @@
             flops=2 * rows * D * (D + 2 * hidden), bytes_accessed=1 << 25, transcendentals=0
         ),
         name="rows_forward",
-    )(att, rows_in, wo, wi, wu, wv, inner_bias, vectors)
+    )(att, rows_in, packed, packed, packed, packed, inner_bias, vectors)
 
 
 def norm_back(grad, hat, inverse, gain):
@@ -450,24 +487,51 @@
     att_ref,
     wo_ref,
     vec_ref,
-    dwv_ref,
-    dwu_ref,
-    dwi_ref,
+    grads_ref,
     dbi_ref,
-    dwo_ref,
     datt_ref,
     dsum_ref,
     dvec_ref,
     low_ref,
     total_ref,
+    dwv_ref,
+    dwo_ref,
+    dwu_ref,
+    dwi_ref,
+    once_sem,
+    up_sem,
+    down_sem,
 ):
     step = pl.program_id(0)
+    steps = pl.num_programs(0)
     parts, _, width = att_ref.shape
+    hidden = GROUPS * D
+    slot = lax.rem(step, 2)
+
+    def up_copy(at, place):
+        here = pl.ds(pl.multiple_of(at * (CHUNK // GROUPS), CHUNK // GROUPS), CHUNK // GROUPS)
+        return pltpu.make_async_copy(
+            dwu_ref.at[place], grads_ref.at[here, pl.ds(0, hidden)], up_sem.at[place]
+        )
+
+    def down_copy(at, place):
+        here = pl.ds(pl.multiple_of(hidden + at * CHUNK, CHUNK), CHUNK)
+        return pltpu.make_async_copy(
+            dwi_ref.at[place], grads_ref.at[:, here], down_sem.at[place]
+        )
+
+    vector_copy = pltpu.make_async_copy(
+        dwv_ref, grads_ref.at[:, pl.ds(2 * hidden + D, LANES)], once_sem.at[0]
+    )
+    out_copy = pltpu.make_async_copy(
+        dwo_ref, grads_ref.at[:, pl.ds(2 * hidden, D)], once_sem.at[1]
+    )
 
     @pl.when(step == 0)
     def _():
         dproj = dproj_ref[...]
         dwv_ref[...] = dot_tn(enc_ref[...], dproj).astype(BF)
+        vector_copy.start()
         grad = dot_nt(dproj, wv_ref[...])
         hat = hat2_ref[...].astype(F32)
         dvec_ref[4:5, :] = column_sum(grad * hat)
@@ -478,11 +542,23 @@
         total_ref[...] = back
         dvec_ref[3:4, :] = column_sum(low.astype(F32))
 
+    @pl.when(step >= 2)
+    def _():
+        up_copy(step - 2, slot).wait()
+        down_copy(step - 2, slot).wait()
+
     low = low_ref[...]
-    dinner = (dot_nt(low, wu_ref[...]) * slope_ref[...].astype(F32)).astype(BF)
+    dinner = (dot_nt(low, joined_up(wu_ref)) * slope_ref[...].astype(F32)).astype(BF)
     dbi_ref[...] = column_sum(dinner.astype(F32))
-    dwu_ref[...] = dot_tn(act_ref[...], low).astype(BF)
-    dwi_ref[...] = dot_tn(low1_ref[...], dinner).astype(BF)
+    up_grad = dot_tn(act_ref[...], low).astype(BF)
+    for at in range(0, CHUNK, QLEN):
+        own, group = at // (QLEN * GROUPS), at // QLEN % GROUPS
+        dwu_ref[slot, own * QLEN : (own + 1) * QLEN, group * D : (group + 1) * D] = up_grad[
+            at : at + QLEN
+        ]
+    up_copy(step, slot).start()
+    dwi_ref[slot] = dot_tn(low1_ref[...], dinner).astype(BF)
+    down_copy(step, slot).start()
     total_ref[...] += dot_nt(dinner, wi_ref[...])
 
     @pl.when(step == pl.num_programs(0) - 1)
@@ -499,99 +575,72 @@
             here = slice(part * width, (part + 1) * width)
             dwo_ref[here, :] = dot_tn(att_ref[part], attn_low).astype(BF)
             datt_ref[part] = dot_nt(attn_low, wo_ref[here, :]).astype(BF)
-
-
-def rows_backward(
-    dproj, enc, hat2, inv2, wv, act, slope, wu, wi, low1, hat1, inv1, att, wo, vectors
-):
+        out_copy.start()
+        vector_copy.wait()
+        for place in range(2):
+            up_copy(steps - 2 + place, place).wait()
+            down_copy(steps - 2 + place, place).wait()
+        out_copy.wait()
+
+
+def rows_backward(dproj, enc, hat2, inv2, packed, act, slope, low1, hat1, inv1, att, vectors):
     rows, hidden = act.shape
-    chunk = 512
     keep = lambda shape: pl.BlockSpec(shape, lambda step: (0,) * len(shape))
-    columns = pl.BlockSpec((rows, chunk), lambda step: (0, step))
-    up = pl.BlockSpec((chunk, D), lambda step: (step, 0))
-    down = pl.BlockSpec((D, chunk), lambda step: (0, step))
-    bias = pl.BlockSpec((1, chunk), lambda step: (0, step))
-    operands = (dproj, enc, hat2, inv2, wv, act, slope, wu, wi, low1, hat1, inv1, att, wo, vectors)
-    special = {5: columns, 6: columns, 7: up, 8: down}
+    columns = pl.BlockSpec((rows, CHUNK), lambda step: (0, step))
+    bias = pl.BlockSpec((1, CHUNK), lambda step: (0, step))
+    weights = packed_specs()
+    operands = (
+        (dproj, None),
+        (enc, None),
+        (hat2, None),
+        (inv2, None),
+        (packed, weights["vector"]),
+        (act, columns),
+        (slope, columns),
+        (packed, weights["up"]),
+        (packed, weights["down"]),
+        (low1, None),
+        (hat1, None),
+        (inv1, None),
+        (att, None),
+        (packed, weights["out"]),
+        (vectors, None),
+    )
     return pl.pallas_call(
         rows_back_kernel,
-        grid=(hidden // chunk,),
-        in_specs=[special.get(i, keep(entry.shape)) for i, entry in enumerate(operands)],
+        grid=(hidden // CHUNK,),
+        in_specs=[keep(entry.shape) if spec is None else spec for entry, spec in operands],
         out_specs=[
-            keep(wv.shape),
-            up,
-            down,
+            pl.BlockSpec(memory_space=pl.ANY),
             bias,
-            keep(wo.shape),
             keep(att.shape),
             keep((rows, D)),
             keep((8, D)),
         ],
         out_shape=[
-            jax.ShapeDtypeStruct(wv.shape, BF),
-            jax.ShapeDtypeStruct(wu.shape, BF),
-            jax.ShapeDtypeStruct(wi.shape, BF),
+            jax.ShapeDtypeStruct(packed.shape, BF),
             jax.ShapeDtypeStruct((1, hidden), F32),
-            jax.ShapeDtypeStruct(wo.shape, BF),
             jax.ShapeDtypeStruct(att.shape, BF),
             jax.ShapeDtypeStruct((rows, D), F32),
             jax.ShapeDtypeStruct((8, D), F32),
         ],
-        scratch_shapes=[pltpu.VMEM((rows, D), BF), pltpu.VMEM((rows, D), F32)],
+        scratch_shapes=[
+            pltpu.VMEM((rows, D), BF),
+            pltpu.VMEM((rows, D), F32),
+            pltpu.VMEM((D, LANES), BF),
+            pltpu.VMEM((D, D), BF),
+            pltpu.VMEM((2, CHUNK // GROUPS, hidden), BF),
+            pltpu.VMEM((2, D, CHUNK), BF),
+            pltpu.SemaphoreType.DMA((2,)),
+            pltpu.SemaphoreType.DMA((2,)),
+            pltpu.SemaphoreType.DMA((2,)),
+        ],
         compiler_params=params(),
         cost_estimate=pl.CostEstimate(
             flops=4 * rows * D * (D + 2 * hidden), bytes_accessed=1 << 26, transcendentals=0
         ),
         name="rows_backward",
-    )(*operands)
-
-
-def heads_back_kernel(x_ref, dq_ref, dk_ref, dv_ref, w_ref, dx_ref, dw_ref, db_ref, acc_ref):
-    part = pl.program_id(0)
-    width = dq_ref.shape[2]
-
-    @pl.when(part == 0)
-    def _():
-        acc_ref[...] = jnp.zeros_like(acc_ref)
-        db_ref[...] = jnp.zeros_like(db_ref)
-
-    total = None
-    for index, ref in enumerate((dq_ref, dk_ref, dv_ref)):
-        here = slice(index * width, (index + 1) * width)
-        grad = ref[0]
-        term = dot_nt(grad, w_ref[:, here])
-        total = term if total is None else total + term
-        acc_ref[:, here] += dot_tn(x_ref[0], grad)
-        db_ref[:, here] += column_sum(grad.astype(F32))
-    dx_ref[0] = total.astype(BF)
-
-    @pl.when(part == pl.num_programs(0) - 1)
-    def _():
-        dw_ref[...] = acc_ref[...].astype(BF)
-
-
-def heads_backward(x_all, dq, dk, dv, w_heads):
-    parts, rows, width = dq.shape
-    flat = pl.BlockSpec((1, rows, width), lambda part: (part, 0, 0))
-    wide = pl.BlockSpec((1, rows, D), lambda part: (part, 0, 0))
-    return pl.pallas_call(
-        heads_back_kernel,
-        grid=(parts,),
-        in_specs=[wide, flat, flat, flat, pl.BlockSpec(w_heads.shape, lambda part: (0, 0))],
-        out_specs=[
-            wide,
-            pl.BlockSpec(w_heads.shape, lambda part: (0, 0)),
-            pl.BlockSpec((1, 3 * width), lambda part: (0, 0)),
-        ],
-        out_shape=[
-            jax.ShapeDtypeStruct(x_all.shape, BF),
-            jax.ShapeDtypeStruct(w_heads.shape, BF),
-            jax.ShapeDtypeStruct((1, 3 * width), F32),
-        ],
-        scratch_shapes=[pltpu.VMEM(w_heads.shape, F32)],
-        compiler_params=params(),
-        name="heads_backward",
-    )(x_all, dq, dk, dv, w_heads)
+    )(*(entry for entry, _ in operands))
 
 
 class Exchange:
@@ -641,6 +690,184 @@
                 device_id_type=pl.DeviceIdType.MESH,
             )
     pl.semaphore_wait(barrier, sum(size - 1 for size in sizes.values()))
+
+
+class Sent:
+    def __init__(self, source, target, axis, index, send, recv):
+        self.copy = pltpu.make_async_remote_copy(
+            src_ref=source,
+            dst_ref=target,
+            send_sem=send,
+            recv_sem=recv,
+            device_id={axis: index},
+            device_id_type=pl.DeviceIdType.MESH,
+        )
+
+    def start(self):
+        self.copy.start()
+        return self
+
+
+pieces_along_y = 5
+
+
+def heads_back_kernel(n_dp, n_fs, pairs, *refs):
+    x_ref, w_ref, dsum_ref, vec_ref = refs[:4]
+    grad_refs = refs[4 : 4 + 3 * pairs]
+    dx_ref, dw_ref, dvec_ref = refs[4 + 3 * pairs : 7 + 3 * pairs]
+    (
+        first_out,
+        second_out,
+        first_in,
+        second_in,
+        chip_out,
+        chip_in,
+        kept_ref,
+        dw_out,
+        dw_in,
+        dw_sum,
+        vec_in,
+        vec_sum,
+        vec_last,
+        core_send,
+        core_recv,
+        chip_send,
+        chip_recv,
+        *sems,
+    ) = refs[7 + 3 * pairs :]
+    me, my_dp = lax.axis_index("fsdp"), lax.axis_index("dp")
+    core, chip = lax.rem(me, 2), me // 2
+    other_core = chip * 2 + 1 - core
+    other_chip = (1 - chip) * 2 + core
+    over = [
+        Exchange(axis, n_dp if axis == "dp" else n_fs, sems[2 * i], sems[2 * i + 1])
+        for i, axis in enumerate(("fsdp", "dp", "dp", "fsdp"))
+    ]
+    greet({"dp": n_dp, "fsdp": n_fs})
+    width = w_ref.shape[1] // 3
+    rows = x_ref.shape[1]
+    piece = rows // pieces_along_y
+
+    over[0].start(lambda partner: vec_ref.at[partner], lambda offset: vec_in.at[offset - 1])
+
+    def back(part):
+        total = jnp.zeros((rows, D), F32)
+        for index in range(3):
+            for pair in range(pairs):
+                here = index * width + pair * LANES
+                total += dot_nt(
+                    grad_refs[pair * 3 + index][part], w_ref[:, here : here + LANES]
+                )
+        return total
+
+    def to_core(source, target, at):
+        return Sent(source, target, "fsdp", other_core, core_send.at[at], core_recv.at[at]).start()
+
+    first_out[...] = back((1 - chip) * 2 + 1 - core).astype(BF)
+    first = to_core(first_out, first_in, 0)
+    away = back(other_chip)
+    first.copy.wait_recv()
+    chip_out[...] = (away + first_in[...].astype(F32)).astype(BF)
+    along_y = []
+    for at in range(pieces_along_y):
+        here = pl.ds(at * piece, piece)
+        along_y.append(
+            Sent(
+                chip_out.at[here],
+                chip_in.at[here],
+                "fsdp",
+                other_chip,
+                chip_send.at[at],
+                chip_recv.at[at],
+            ).start()
+        )
+
+    block = D // n_dp
+    for index in range(3):
+        for pair in range(pairs):
+            here = index * width + pair * LANES
+            total = jnp.zeros((D, LANES), F32)
+            for part in range(n_fs):
+                total += dot_tn(x_ref[part], grad_refs[pair * 3 + index][part])
+            dw_out[:, :, here : here + LANES] = total.astype(BF).reshape(n_dp, block, LANES)
+    over[1].start(lambda partner: dw_out.at[partner], lambda offset: dw_in.at[offset - 1])
+
+    over[0].arrived()
+    vec_total = vec_ref[me]
+    for offset in range(n_fs - 1):
+        vec_total = vec_total + vec_in[offset]
+    vec_sum[...] = vec_total
+    over[2].start(lambda partner: vec_sum.at[partner], lambda offset: vec_last.at[offset - 1])
+
+    second_out[...] = back(other_core).astype(BF)
+    second = to_core(second_out, second_in, 1)
+    kept_ref[...] = back(me) + dsum_ref[...]
+    second.copy.wait_recv()
+    kept_ref[...] += second_in[...].astype(F32)
+
+    over[2].arrived()
+    vec_total = vec_sum[my_dp]
+    for offset in range(n_dp - 1):
+        vec_total = vec_total + vec_last[offset]
+    dvec_ref[...] = vec_total
+
+    over[1].arrived()
+    dw_total = dw_out[my_dp].astype(F32)
+    for offset in range(n_dp - 1):
+        dw_total = dw_total + dw_in[offset].astype(F32)
+    each = block // n_fs
+    dw_sum[...] = dw_total.reshape(n_fs, each, 3 * width)
+    mine = dw_ref.at[me]
+    dw_ref[me] = dw_sum[me]
+    over[3].start(lambda partner: dw_sum.at[partner], lambda offset: mine)
+    for at in range(pieces_along_y):
+        here = slice(at * piece, (at + 1) * piece)
+        along_y[at].copy.wait_recv()
+        dx_ref[here, :] = (kept_ref[here, :] + chip_in[here, :].astype(F32)).astype(BF)
+    over[3].arrived()
+    for exchange in over:
+        exchange.sent()
+    for one in [first, second] + along_y:
+        one.copy.wait_send()
+
+
+def heads_backward(x_all, w_heads, dsum, vector_grads, grads):
+    n_dp, n_fs = lax.axis_size("dp"), lax.axis_size("fsdp")
+    _, rows, _ = x_all.shape
+    pairs = len(grads) // 3
+    whole = pl.BlockSpec(memory_space=pltpu.VMEM)
+    block = D // n_dp
+    columns = w_heads.shape[1]
+    tile = vector_grads.shape[2:]
+    line = pltpu.VMEM((rows, D), BF)
+    dma = lambda axis: [pltpu.SemaphoreType.DMA(((n_dp if axis == "dp" else n_fs) - 1,))] * 2
+    return pl.pallas_call(
+        functools.partial(heads_back_kernel, n_dp, n_fs, pairs),
+        in_specs=[whole] * (4 + 3 * pairs),
+        out_specs=[whole] * 3,
+        out_shape=[
+            jax.ShapeDtypeStruct((rows, D), BF),
+            jax.ShapeDtypeStruct((n_fs, block // n_fs, columns), F32),
+            jax.ShapeDtypeStruct(tile, F32),
+        ],
+        scratch_shapes=[line] * 6
+        + [
+            pltpu.VMEM((rows, D), F32),
+            pltpu.VMEM((n_dp, block, columns), BF),
+            pltpu.VMEM((n_dp - 1, block, columns), BF),
+            pltpu.VMEM((n_fs, block // n_fs, columns), F32),
+            pltpu.VMEM((n_fs - 1, n_dp) + tile, F32),
+            pltpu.VMEM((n_dp,) + tile, F32),
+            pltpu.VMEM((n_dp - 1,) + tile, F32),
+            pltpu.SemaphoreType.DMA((2,)),
+            pltpu.SemaphoreType.DMA((2,)),
+            pltpu.SemaphoreType.DMA((pieces_along_y,)),
+            pltpu.SemaphoreType.DMA((pieces_along_y,)),
+        ]
+        + [sem for axis in ("fsdp", "dp", "dp", "fsdp") for sem in dma(axis)],
+        compiler_params=params(collective_id=2, has_side_effects=True),
+        name="heads_backward",
+    )(x_all, w_heads, dsum, vector_grads, *grads)
 
 
 widths = (PROJ, PROJ * 3 // 4, PROJ // 2)
@@ -900,10 +1127,9 @@
 
     rows_in = jnp.concatenate([doc_tokens.reshape(doc_rows, D), query_tokens.reshape(QLEN, D)])
     x_all = lax.all_gather(rows_in, "fsdp")
-    wo = lax.all_gather(out_weight, AXES, axis=0, tiled=True)
-    wi = lax.all_gather(inner_weight, AXES, axis=0, tiled=True)
-    wu = lax.all_gather(outer_weight, AXES, axis=0, tiled=True)
-    wv = lax.all_gather(vector_weight, AXES, axis=0, tiled=True)
+    own_up = [outer_weight[group * split : (group + 1) * split] for group in range(GROUPS)]
+    packed_own = jnp.concatenate(own_up + [inner_weight, out_weight, vector_weight], axis=1)
+    packed_w = lax.all_gather(packed_own, AXES, axis=0, tiled=True)
 
     tables = rope_tables(parts, doc_rows)
     cosine, sine = jnp.asarray(tables[0]), jnp.asarray(tables[1])
@@ -913,7 +1139,7 @@
     mixed, mixed_full, query_log = attend(query, key, value, parts, doc_rows)
     att = lax.all_to_all(mixed, "fsdp", 0, 0, tiled=True)
     hat1, inv1, low1, act, slope, hat2, inv2, enc, proj = rows_forward(
-        att, rows_in, wo, wi, wu, wv, inner_vec, vectors
+        att, rows_in, packed_w, inner_vec, vectors
     )
 
     positions = mine * doc_rows + jnp.arange(doc_rows, dtype=jnp.int32)
@@ -922,46 +1148,74 @@
     )
     dproj = jnp.concatenate([grad_doc, grad_query])
 
-    dwv, dwu, dwi, dbi, dwo, datt, dsum, dvec = rows_backward(
-        dproj, enc, hat2, inv2, wv, act, slope, wu, wi, low1, hat1, inv1, att, wo, vectors
+    grads, dbi, datt, dsum, dvec = rows_backward(
+        dproj, enc, hat2, inv2, packed_w, act, slope, low1, hat1, inv1, att, vectors
     )
     grad_mixed = lax.all_to_all(datt, "fsdp", 0, 0, tiled=True)
-    dq, dk, dv = attend_back(query_log, key, value, grad_mixed, mixed_full, cosine, sine, doc_rows)
-    dx, dw, db = heads_backward(x_all, dq, dk, dv, w_heads)
-
-    core, chip = mine % 2, mine // 2
-    by_core = dx.reshape(parts // 2, 2, rows, D)
-    kept = lax.dynamic_index_in_dim(by_core, core, 1, False)
-    sent = lax.dynamic_index_in_dim(by_core, 1 - core, 1, False)
-    half = kept.astype(F32) + lax.ppermute(sent, "fsdp", other_core(parts)).astype(F32)
-    away = lax.dynamic_index_in_dim(half, 1 - chip, 0, False).astype(BF)
-    grad_rows = (
-        dsum
-        + lax.dynamic_index_in_dim(half, chip, 0, False)
-        + lax.ppermute(away, "fsdp", other_chip(parts)).astype(F32)
-    )
-    grad_low = grad_rows.astype(BF)
-
-    dw_dp = lax.psum_scatter(dw, "dp", scatter_dimension=0, tiled=True)
-    dw_own = lax.all_to_all(dw_dp, "fsdp", 0, 1, tiled=True).astype(F32)
-    dw_own = dw_own.reshape(split, parts, 3, width).transpose(2, 0, 1, 3).reshape(3, split, D)
-    dwo_own = lax.psum_scatter(dwo, "dp", scatter_dimension=0, tiled=True)
-    dwo_own = lax.psum_scatter(dwo_own, "fsdp", scatter_dimension=0, tiled=True).astype(F32)
-    dwi_own = lax.psum_scatter(dwi, "dp", scatter_dimension=0, tiled=True)
-    dwi_own = lax.psum_scatter(dwi_own, "fsdp", scatter_dimension=0, tiled=True).astype(F32)
-    dwu_own = lax.psum_scatter(dwu, "dp", scatter_dimension=0, tiled=True)
-    dwu_own = lax.psum_scatter(dwu_own, "fsdp", scatter_dimension=0, tiled=True).astype(F32)
-    dwv_own = lax.psum_scatter(dwv, "dp", scatter_dimension=0, tiled=True)
-    dwv_own = lax.psum_scatter(dwv_own, "fsdp", scatter_dimension=0, tiled=True).astype(F32)
+    pair_args = (query_log, key, value, grad_mixed, mixed_full, cosine, sine)
+
+    n_dp = lax.axis_size("dp")
+    z, x = lax.axis_index("dp") // 2, lax.axis_index("dp") % 2
+    core, y = mine % 2, mine // 2
+    pick = lambda value, index, axis: lax.dynamic_index_in_dim(value, index, axis, False)
+    middle = grads.shape[1] // 2 // LANES * LANES
+    by_device = grads.reshape(n_dp // 2, 2, 2, 2, split, -1)
+    across = [(d, d ^ 1) for d in range(n_dp)]
+    add = lambda one, two: one.astype(F32) + two.astype(F32)
+    from_core = lax.ppermute(pick(by_device, 1 - core, 3), "fsdp", other_core(parts))
+    own = lambda columns: pick(by_device, core, 3)[..., columns]
+    left, right = slice(0, middle), slice(middle, None)
+    sum_left = add(own(left), from_core[..., left])
+    sum_right = add(own(right), from_core[..., right])
+    out_x = pick(sum_left, 1 - x, 1).astype(BF)
+    out_y = pick(sum_right, 1 - y, 2).astype(BF)
+    out_x, out_y, *pair_args = lax.optimization_barrier((out_x, out_y) + pair_args)
+    left_x = lax.ppermute(out_x, "dp", across)
+    right_y = lax.ppermute(out_y, "fsdp", other_chip(parts))
+    grads_pair = list(attend_back(0, *pair_args, doc_rows))
+    left_x, right_y, grads_pair[0] = lax.optimization_barrier((left_x, right_y, grads_pair[0]))
+    sum_left = add(pick(sum_left, x, 1), left_x)
+    sum_right = add(pick(sum_right, y, 2), right_y)
+    out_y = pick(sum_left, 1 - y, 1).astype(BF)
+    out_x = pick(sum_right, 1 - x, 1).astype(BF)
+    out_x, out_y, grads_pair[0], *pair_args = lax.optimization_barrier(
+        (out_x, out_y, grads_pair[0], *pair_args)
+    )
+    left_y = lax.ppermute(out_y, "fsdp", other_chip(parts))
+    right_x = lax.ppermute(out_x, "dp", across)
+    pairs = [grads_pair, list(attend_back(1, *pair_args, doc_rows))]
+    left_y, right_x, pairs[1][0] = lax.optimization_barrier((left_y, right_x, pairs[1][0]))
+    by_z = jnp.concatenate(
+        [add(pick(sum_left, y, 1), left_y), add(pick(sum_right, x, 1), right_x)], axis=-1
+    ).astype(BF)
+    n_z = n_dp // 2
+    grads_own = pick(by_z, z, 0).astype(F32)
+    for shift in range(1, n_z):
+        along = [(d, (d + 2 * shift) % n_dp) for d in range(n_dp)]
+        grads_own += lax.ppermute(pick(by_z, (z + shift) % n_z, 0), "dp", along).astype(F32)
+
     place = jnp.arange(parts, dtype=jnp.int32)[None, :, None] == mine
-    db_all = jnp.where(place, db.reshape(3, 1, width), 0.0).reshape(3, D)
+    db = jnp.stack([jnp.concatenate([pair[3][i] for pair in pairs]) for i in range(3)])
+    db_all = jnp.where(place, db[:, None, :], 0.0).reshape(3, D)
     vector_grads = jnp.concatenate([db_all, dvec[:6]]).reshape(9, -1, split).transpose(1, 0, 2)
     vector_grads = jnp.concatenate(
         [vector_grads.reshape(-1, 9 * split), dbi.reshape(-1, hidden_split)], axis=1
     )
-    summed = lax.psum_scatter(vector_grads, AXES, scatter_dimension=0, tiled=False)
+    used = vector_grads.shape[1]
+    vector_grads = jnp.pad(vector_grads, ((0, 0), (0, -used % (8 * LANES))))
+    vector_grads = vector_grads.reshape(n_dp, parts, 8, -1).transpose(1, 0, 2, 3)
+    grad_low, dw, summed = heads_backward(
+        x_all, w_heads, dsum, vector_grads, [entry for pair in pairs for entry in pair[:3]]
+    )
+    dw_own = dw.reshape(parts, split, 3, width).transpose(2, 1, 0, 3).reshape(3, split, D)
+    summed = summed.reshape(-1)
+    up_own = jnp.concatenate([grads_own[:, i * D : (i + 1) * D] for i in range(GROUPS)])
+    hidden = GROUPS * D
+    dwi_own = grads_own[:, hidden : 2 * hidden]
+    dwo_own = grads_own[:, 2 * hidden : 2 * hidden + D]
+    dwv_own = grads_own[:, 2 * hidden + D :]
     vec_own = [summed[index * split : (index + 1) * split] for index in range(9)]
-    dbi_own = summed[9 * split :]
+    dbi_own = summed[9 * split : 9 * split + hidden_split]
     return (
         losses,
         enc[:doc_rows].reshape(1, doc_rows, D),
@@ -980,7 +1234,7 @@
         vec_own[5],
         dwi_own,
         dbi_own,
-        dwu_own,
+        up_own,
         vec_own[6],
         vec_own[7],
         vec_own[8],

time: 1090 us -> 708 us (0.65)
  waiting for transfers between devices: 535 us -> 123 us
  blocking collectives: 148 us -> 49.5 us
  Pallas kernels: 300 us -> 381 us
  local copies, waits for them, and re-layouts: 39.4 us -> 77.2 us
  other arithmetic: 19.8 us -> 36.4 us
    reduce_scatter x9 -> x0, waiting for transfers between devices: 392 us -> none  [the longest x1 141 us: shards(): dwu_own = lax.psum_scatter(dwu, 'dp', scatter_dimension=0, tiled=True)]
    pallas_call x2, Pallas kernels: 68.8 us -> 146 us  [the longest x1 94.7 us: heads_backward(): pl.pallas_call(functools.partial(heads_back_kernel, n_dp, n_fs, pairs), i...]
    all_gather x1 -> x0, blocking collectives: 57.6 us -> none  [shards(): wv = lax.all_gather(vector_weight, AXES, axis=0, tiled=True)]
    all_gather x3 -> x1, waiting for transfers between devices: 92.5 us -> 41.4 us  [shards(): packed_w = lax.all_gather(packed_own, AXES, axis=0, tiled=True)]
    unnamed x2 -> x1, blocking collectives: 81.9 us -> 40.7 us
    all_to_all x1, waiting for transfers between devices: 0.01 us -> 35.2 us  [shards(): att = lax.all_to_all(mixed, 'fsdp', 0, 0, tiled=True)]
    dynamic_slice x0 -> x3, local copies, waits for them, and re-layouts: none -> 31.3 us  [shards(): lax.dynamic_index_in_dim(value, index, axis, False)]
    add x1 -> x5, other arithmetic: 3.44 us -> 25.2 us  [the longest x4 23.5 us: shards(): add = lambda one, two: one.astype(F32) + two.astype(F32)]
  transfers between devices with their start and end apart: 19 -> 13, of which waited for: 9 -> 3; matrix products, arithmetic and copies ran while one was open for 4% -> 7% of each run, Pallas kernels for 17% -> 37%
where the time goes in v2:
time: 708 us; the launch traced here: 699 us
  Pallas kernels  381 us (54%)
  waiting for transfers between devices  123 us (17%)
  local copies, waits for them, and re-layouts  77.2 us (11%)
  blocking collectives  49.5 us (7%)
  other arithmetic  36.4 us (5%)
  starting transfers between devices  17.1 us (2%)
  between operations  15.2 us (2%)
    pallas_call x2, Pallas kernels, attend_back(): pl.pallas_call(functools.partial(attend_back_kernel, doc_rows, parts), gr...  104 us
    pallas_call x1, Pallas kernels, heads_backward(): pl.pallas_call(functools.partial(heads_back_kernel, n_dp, n_fs, pairs), i...  94.7 us
    pallas_call x1, Pallas kernels, attend(): pl.pallas_call(functools.partial(attend_kernel, doc_rows, parts), grid=(h...  51.6 us
    pallas_call x1, Pallas kernels, rows_backward(): pl.pallas_call(rows_back_kernel, grid=(hidden // CHUNK,), in_specs=[keep(...  51.1 us
    all_gather x1, waiting for transfers between devices, shards(): x_all = lax.all_gather(rows_in, 'fsdp')  46.4 us
    all_gather x1, waiting for transfers between devices, shards(): packed_w = lax.all_gather(packed_own, AXES, axis=0, tiled=True)  41.4 us
    unnamed x1, blocking collectives  40.7 us
    pallas_call x1, Pallas kernels, maxsim(): pl.pallas_call(functools.partial(maxsim_kernel, n_dp, n_fs), in_specs=[wh...  37.4 us
  transfers between devices with their start and end apart: 13, of which 3 were waited for; matrix products, arithmetic and copies ran while one was open for 7% of the time, Pallas kernels for 37%

profile of v2, /device:TPU:1, one launch (start us, length us, event | category | flops | bytes accessed | tf_op | source)
XLA Modules:
  0.0 699.2 jit_solution(8366875881414308423)
XLA Ops:
  7.2 0.7 constant_dynamic-update-slice_fusion.11
  8.0 0.7 constant_dynamic-update-slice_fusion.10
  8.7 0.7 constant_dynamic-update-slice_fusion.9
  9.4 0.7 constant_dynamic-update-slice_fusion.8
  10.1 0.7 constant_dynamic-update-slice_fusion.7
  10.8 0.7 constant_dynamic-update-slice_fusion.6
  11.6 0.7 constant_dynamic-update-slice_fusion.5
  12.3 0.7 constant_dynamic-update-slice_fusion.4
  13.0 0.7 constant_dynamic-update-slice_fusion.3
  13.7 0.7 constant_dynamic-update-slice_fusion.2
  14.4 0.7 constant_dynamic-update-slice_fusion.1
  15.9 8.8 %all_to_all.29 = bf16[32,4,768]{2,0,1:T(8,128)(2,1)} all-to-all(bf16[32,4,768]{2,0,1:T(8,128)(2,1)S(1)} %bitcast.110), channel_id=1, replica_groups=mesh['dp'=8,'fsdp'=4] {'fsdp'}, dimensions={1} | all-to-all | bytes 393216 | tf_op jit(solution)/shard_map/all_to_all | solution.py:1102
  24.8 2.8 pad_maximum_fusion.x_ref
  28.0 0.8 copy-done.8
  29.3 40.7 %all-reduce.2 = bf16[13312]{0:T(1024)(128)(2,1)S(1)} all-reduce(bf16[13312]{0:T(1024)(128)(2,1)S(1)} %dynamic-update-slice), channel_id=3, replica_groups=mesh['dp'=8,'fsdp'=4] {'dp','fsdp'}, use_global_device_ids=true, to_apply=%add.2 | all-reduce | flops 13312 | bytes 53248
  71.9 46.4 %all-gather.10.cloned.1.call-done = bf16[3200,1024]{1,0:T(8,128)(2,1)} async-done(((bf16[800,1024]{1,0:T(8,128)(2,1)}), bf16[3200,1024]{1,0:T(8,128)(2,1)}) %all-gather.10.cloned.1.call-update) | async-done | bytes 6553616 | tf_op jit(solution)/shard_map/all_gather | solution.py:1129
  118.3 12.4 %project_heads.1 = (bf16[4,3200,128]{2,1,0:T(8,128)(2,1)}, bf16[4,3200,128]{2,1,0:T(8,128)(2,1)}, bf16[4,3200,128]{2,1,0:T(8,128)(2,1)}) custom-call(s32[1]{0:T(128)} %copy.114.len_ref, bf16[4,800,1024]{2,1,0:T(8,128)(2,1)} %bitcast.103, bf16[1024,768]{1,0:T(8,128)(2,1)} %all-gather.6.cloned.1.call-done.w_ref.refs_1_, f32[1,768]{1,0:T(1,128)} %reshape.149.b_ref, ...), custom_call_target="tpu_custom_call" | custom-call | tf_op jit(solution)/shard_map/project_heads/pallas_call | solution.py:115
  130.6 51.6 %attend.1 = (bf16[4,800,256]{2,1,0:T(8,128)(2,1)}, f32[4,800,256]{2,1,0:T(8,128)}, bf16[4,3200,128]{2,1,0:T(8,128)(2,1)}) custom-call(bf16[4,3200,128]{2,1,0:T(8,128)(2,1)} %get-tuple-element.81.q_ref, bf16[4,3200,128]{2,1,0:T(8,128)(2,1)} %get-tuple-element.117.k_ref.ko_ref, bf16[4,3200,128]{2,1,0:T(8,128)(2,1)} %get-tuple-element.118.v_ref.vo_ref, ...), custom_call_target="tpu_custom_call" | custom-call | flops 41943040000 | bytes 16777216 | tf_op jit(solution)/shard_map/attend/pallas_call | solution.py:187
  182.2 4.4 all-to-all-start.1
  188.5 35.2 %all-to-all-done.1.att_ref = bf16[4,800,256]{2,1,0:T(8,128)(2,1)S(1)} async-done(((bf16[4,800,256]{2,1,0:T(8,128)(2,1)}), bf16[4,800,256]{2,1,0:T(8,128)(2,1)S(1)}, u32[]{:S(2)}, u32[]{:S(2)}) %all-to-all-start.1) | async-done | bytes 1638432 | tf_op jit(solution)/shard_map/all_to_all | solution.py:1140
  223.7 41.4 %all-gather.8.cloned.1.call-done.wo_ref.wi_ref.wu_ref.wv_ref = bf16[1024,9344]{1,0:T(8,128)(2,1)} async-done(((bf16[32,9344]{1,0:T(8,128)(2,1)}), bf16[1024,9344]{1,0:T(8,128)(2,1)}) %all-gather.8.cloned.1.call-update) | async-done | bytes 19136528 | tf_op jit(solution)/shard_map/all_gather | solution.py:1132
  265.0 30.1 %rows_forward.1 = (bf16[800,1024]{1,0:T(8,128)(2,1)}, f32[800,128]{1,0:T(8,128)}, bf16[800,1024]{1,0:T(8,128)(2,1)}, bf16[800,4096]{1,0:T(8,128)(2,1)}, bf16[800...) custom-call(bf16[4,800,256]{2,1,0:T(8,128)(2,1)} %copy-done.4, ...), custom_call_target="tpu_custom_call" | custom-call | flops 15099494400 | bytes 33554432 | tf_op jit(solution)/shard_map/rows_forward/pallas_call | solution.py:429
  295.2 1.8 slice.222.pd_ref
  297.0 1.3 slice.221.pq_ref
  298.3 0.9 broadcast_in_dim.41.mask_ref
  299.8 37.4 %maxsim.1 = (f32[8,128]{1,0:T(8,128)}, bf16[32,128]{1,0:T(8,128)(2,1)}, bf16[768,128]{1,0:T(8,128)(2,1)}) custom-call(f32[32,128]{1,0:T(8,128)} %slice.221.pq_ref, f32[768,128]{1,0:T(8,128)} %slice.222.pd_ref, f32[768,128]{1,0:T(8,128)} %broadcast_in_dim.41.mask_ref, s32[8,128]{1,0:T(8,128)} %broadcast_in_dim.43.label_ref), custom_call_target="tpu_custom_call" | custom-call | tf_op jit(solution)/shard_map/maxsim/pallas_call | solution.py:1029
  337.2 1.6 pad_maximum_fusion.2.dproj_ref
  338.8 51.1 %rows_backward.1 = (bf16[1024,9344]{1,0:T(8,128)(2,1)}, f32[1,4096]{1,0:T(1,128)}, bf16[4,800,256]{2,1,0:T(8,128)(2,1)}, f32[800,1024]{1,0:T(8,128)}, f32[8,1024]{1,0:T(8,128)}) custom-call(bf16[800,128]{1,0:T(8,128)(2,1)} %pad_maximum_fusion.2.dproj_ref, bf16[800,1024]{1,0:T(8,128)(2,1)} %get-tuple-element.87.enc_ref, ...), custom_call_target="tpu_custom_call" | custom-call | flops 30198988800 | bytes 67108864 | tf_op jit(solution)/shard_map/rows_backward/pallas_call | solution.py:609
  389.9 14.8 %constant_dynamic-slice_fusion.1 = (bf16[4,2,2,1,32,9344]{5,4,3,2,1,0:T(8,128)(2,1)}, bf16[4,2,2,1,32,9344]{5,4,3,2,1,0:T(8,128)(2,1)}) fusion(bf16[4,2,2,2,32,9344]{5,4,3,2,1,0:T(8,128)(2,1)} %bitcast.105, s32[]{:T(128)S(6)} %select_n.84, s32[]{:T(128)S(6)} %select_n.85), kind=kLoop, calls=%fused_computation.71 | loop fusion | bytes 38273032 | tf_op jit(solution)/shard_map/jit(dynamic_index_in_dim)/dynamic_slice | solution.py:1160
  404.6 8.3 %copy.92 = bf16[4,2,2,1,32,9344]{5,4,0,1,2,3:T(8,128)(2,1)} copy(bf16[4,2,2,1,32,9344]{5,4,3,2,1,0:T(8,128)(2,1)} %get-tuple-element.141) | data formatting | bytes 19136512 | tf_op jit(solution)/shard_map/jit(dynamic_index_in_dim)/dynamic_slice | solution.py:1160
  413.1 8.2 %copy.93 = bf16[4,2,2,1,32,9344]{5,4,0,1,2,3:T(8,128)(2,1)} copy(bf16[4,2,2,1,32,9344]{5,4,3,2,1,0:T(8,128)(2,1)} %get-tuple-element.140) | data formatting | bytes 19136512 | tf_op jit(solution)/shard_map/jit(dynamic_index_in_dim)/dynamic_slice | solution.py:1160
  421.4 5.0 all-to-all-start.2
  428.0 1.3 slice_bitcast_fusion.1
  429.3 5.2 convert_add_fusion
  434.4 12.4 %convert_add_fusion.1 = f32[4,2,2,32,4608]{4,3,0,1,2:T(8,128)} fusion(bf16[4,2,2,32,9344]{4,3,0,1,2:T(8,128)(2,1)} %collective-permute-done, bf16[4,2,2,32,9344]{4,3,0,1,2:T(8,128)(2,1)} %bitcast.102), kind=kLoop, calls=%fused_computation.3 | loop fusion | flops 7077888 | bytes 18874368 | tf_op jit(solution)/shard_map/add | solution.py:1164
  447.1 4.0 fusion.2
  451.1 1.4 collective-permute-start.2
  452.5 1.3 collective-permute-start.1
  453.8 51.9 %attend_back.2 = (bf16[4,800,128]{2,1,0:T(8,128)(2,1)}, bf16[4,800,128]{2,1,0:T(8,128)(2,1)}, bf16[4,800,128]{2,1,0:T(8,128)(2,1)}, f32[8,128]{1,0:T(8,128)}) custom-call(bf16[4,3200,128]{2,1,0:T(8,128)(2,1)} %get-tuple-element.116.q_ref, bf16[4,3200,128]{2,1,0:T(8,128)(2,1)} %get-tuple-element.117.k_ref.ko_ref, ...), custom_call_target="tpu_custom_call" | custom-call | flops 52428800000 | bytes 16777216 | tf_op jit(solution)/shard_map/attend_back/pallas_call | solution.py:309
  505.7 0.8 slice_bitcast_fusion.9
  506.5 3.7 bitcast_add_fusion.1
  510.2 2.4 copy-done.3
  512.6 1.1 fusion.7
  514.4 2.2 bitcast_add_fusion
  516.7 2.2 copy-done.2
  519.3 1.0 collective-permute-start.3
  520.4 51.7 %attend_back.3 = (bf16[4,800,128]{2,1,0:T(8,128)(2,1)}, bf16[4,800,128]{2,1,0:T(8,128)(2,1)}, bf16[4,800,128]{2,1,0:T(8,128)(2,1)}, f32[8,128]{1,0:T(8,128)}) custom-call(bf16[4,3200,128]{2,1,0:T(8,128)(2,1)} %get-tuple-element.116.q_ref, bf16[4,3200,128]{2,1,0:T(8,128)(2,1)} %get-tuple-element.117.k_ref.ko_ref, ...), custom_call_target="tpu_custom_call" | custom-call | flops 52428800000 | bytes 16777216 | tf_op jit(solution)/shard_map/attend_back/pallas_call | solution.py:309
  572.1 0.8 slice_bitcast_fusion.8
  574.1 1.0 copy-done.7
  575.1 2.2 fusion.3
  577.4 2.3 fusion.1
  579.6 1.2 fusion.13
  580.8 0.8 collective-permute-start.5
  581.6 2.0 collective-permute-start.6
  583.6 0.8 collective-permute-start.7
  584.4 94.7 %heads_backward.1 = (bf16[800,1024]{1,0:T(8,128)(2,1)}, f32[4,32,768]{2,1,0:T(8,128)}, f32[8,128]{1,0:T(8,128)}) custom-call(bf16[4,800,1024]{2,1,0:T(8,128)(2,1)} %bitcast.104, bf16[1024,768]{1,0:T(8,128)(2,1)} %all-gather.6.cloned.1.call-done.w_ref.refs_1_, f32[800,1024]{1,0:T(8,128)} %get-tuple-element.97.refs_2_, f32[4,8,8,128]{3,2,1,0:T(8,128)} %bitcast.112, ...), custom_call_target="tpu_custom_call" | custom-call | tf_op jit(solution)/shard_map/heads_backward/pallas_call | solution.py:844
  679.1 1.2 reshape.162
  680.6 1.6 fusion.21
  682.3 1.3 slice.250
  686.5 1.3 slice_bitcast_fusion
  687.7 1.7 fusion.6
  689.5 0.7 fusion.18
  690.2 0.8 slice.277
  691.6 0.8 pad_maximum_fusion.1
  (136 shorter events, 13.4 us)
Async XLA Ops:
  7.2 64.7 %all-gather.6.cloned.1.call-start = ((), (), s32[]{:S(2)}) async-start(), calls=%async_computation.3 | async-start | bytes 1769472 | tf_op jit(solution)/shard_map/all_gather | solution.py:1103
  24.7 93.6 %all-gather.10.cloned.1.call-start = ((), (), s32[]{:S(2)}) async-start(), calls=%async_computation.5 | async-start | bytes 8192000 | tf_op jit(solution)/shard_map/all_gather | solution.py:1129
  24.8 3.1 copy-start.9
  24.8 3.1 copy-start.10
  24.8 3.1 copy-start.11
  24.8 3.2 copy-start.14
  27.6 1.2 copy-start.17
  27.7 1.2 copy-start.18
  27.7 1.2 copy-start.19
  27.7 1.2 copy-start.20
  27.7 1.2 copy-start.21
  27.7 1.2 copy-start.22
  27.7 1.2 copy-start.23
  27.7 1.2 copy-start.24
  27.7 1.2 copy-start.25
  27.7 1.2 copy-start.26
  27.8 237.3 %all-gather.8.cloned.1.call-start = ((), (), s32[]{:S(2)}) async-start(), calls=%async_computation.4 | async-start | bytes 19734528 | tf_op jit(solution)/shard_map/all_gather | solution.py:1132
  28.0 0.8 copy-start.8
  182.2 5.5 copy-start.15
  182.2 41.5 %all-to-all-start.1 = ((bf16[4,800,256]{2,1,0:T(8,128)(2,1)}), bf16[4,800,256]{2,1,0:T(8,128)(2,1)S(1)}, u32[]{:S(2)}, u32[]{:S(2)}) async-start(bf16[4,800,256]{2,1,0:T(8,128)(2,1)} %get-tuple-element.84), calls=%async_computation.1 | async-start | bytes 3276800 | tf_op jit(solution)/shard_map/all_to_all | solution.py:1140
  223.6 41.4 %copy-start.4 = (bf16[4,800,256]{2,1,0:T(8,128)(2,1)}, bf16[4,800,256]{2,1,0:T(8,128)(2,1)S(1)}, u32[]{:S(2)}) copy-start(bf16[4,800,256]{2,1,0:T(8,128)(2,1)S(1)} %all-to-all-done.1.att_ref) | copy-start | bytes 4915204
  412.9 16.3 %collective-permute-start = (bf16[4,2,2,32,9344]{4,3,0,1,2:T(8,128)(2,1)}, bf16[4,2,2,32,9344]{4,3,0,1,2:T(8,128)(2,1)}, u32[]{:S(2)}, u32[]{:S(2)}) collective-permute-start(bf16[4,2,2,32,9344]{4,3,0,1,2:T(8,128)(2,1)} %bitcast.106), channel_id=1, source_target_pairs={{0,1},{1,0},{2,3},{3,2},{4,5},{5,4},{6,7},{7,6},{8,9},{9,8},{10,11... | collective-permute-start | bytes 28704776 | tf_op jit(solution)/shard_map/ppermute | solution.py:1165
  421.3 5.0 copy-start.12
  421.3 5.2 copy-start.16
  421.3 6.0 copy-start.5
  421.4 29.7 %all-to-all-start.2 = ((bf16[4,800,256]{2,1,0:T(8,128)(2,1)}), bf16[4,800,256]{2,1,0:T(8,128)(2,1)}, u32[]{:S(2)}, u32[]{:S(2)}) async-start(bf16[4,800,256]{2,1,0:T(8,128)(2,1)} %get-tuple-element.100), calls=%async_computation.2 | async-start | bytes 3276800 | tf_op jit(solution)/shard_map/all_to_all | solution.py:1154
  434.4 12.4 %copy-start = (f32[4,2,2,32,4736]{4,3,0,1,2:T(8,128)}, f32[4,2,2,32,4736]{4,3,0,1,2:T(8,128)S(1)}, u32[]{:S(2)}) copy-start(f32[4,2,2,32,4736]{4,3,0,1,2:T(8,128)S(1)} %convert_add_fusion) | copy-start | bytes 29097988
  451.1 55.4 %collective-permute-start.2 = (bf16[4,2,32,4736]{3,2,0,1:T(8,128)(2,1)S(1)}, bf16[4,2,32,4736]{3,2,0,1:T(8,128)(2,1)}, u32[]{:S(2)}, u32[]{:S(2)}) collective-permute-start(bf16[4,2,32,4736]{3,2,0,1:T(8,128)(2,1)S(1)} %fusion), channel_id=1, source_target_pairs={{0,2},{1,3},{2,0},{3,1},{4,6},{5,7},{6,4},{7,5},{8,10},{9,11},{10,... | collective-permute-start | bytes 7274504 | tf_op jit(solution)/shard_map/ppermute | solution.py:1174
  452.5 54.0 %collective-permute-start.1 = (bf16[4,2,32,4608]{3,2,0,1:T(8,128)(2,1)}, bf16[4,2,32,4608]{3,2,0,1:T(8,128)(2,1)}, u32[]{:S(2)}, u32[]{:S(2)}) collective-permute-start(bf16[4,2,32,4608]{3,2,0,1:T(8,128)(2,1)} %fusion.2), channel_id=1, source_target_pairs={{0,4},{4,0},{8,12},{12,8},{16,20},{20,16},{24,28},{28,24},{1,5},{5... | collective-permute-start | bytes 7077896 | tf_op jit(solution)/shard_map/ppermute | solution.py:1173
  506.5 7.9 %copy-start.1 = (f32[4,2,2,32,4736]{4,3,0,1,2:T(8,128)S(1)}, f32[4,2,2,32,4736]{4,3,0,1,2:T(8,128)}, u32[]{:S(2)}) copy-start(f32[4,2,2,32,4736]{4,3,0,1,2:T(8,128)} %copy-done) | copy-start | bytes 29097988
  510.2 2.4 copy-start.3
  516.7 2.2 copy-start.2
  519.0 54.3 %copy-start.13 = (f32[1,4096]{1,0:T(1,128)S(1)}, f32[1,4096]{1,0:T(1,128)}, u32[]{:S(2)}) copy-start(f32[1,4096]{1,0:T(1,128)} %get-tuple-element.125) | copy-start | bytes 49156
  519.0 55.1 %collective-permute-start.4 = (bf16[4,32,4736]{2,1,0:T(8,128)(2,1)S(1)}, bf16[4,32,4736]{2,1,0:T(8,128)(2,1)S(1)}, u32[]{:S(2)}, u32[]{:S(2)}) collective-permute-start(bf16[4,32,4736]{2,1,0:T(8,128)(2,1)S(1)} %fusion.4), channel_id=1, source_target_pairs={{0,4},{4,0},{8,12},{12,8},{16,20},{20,16},{24,28},{28,24},{1,5},{5... | collective-permute-start | bytes 3637256 | tf_op jit(solution)/shard_map/ppermute | solution.py:1185
  519.3 54.8 %collective-permute-start.3 = (bf16[4,32,4608]{2,1,0:T(8,128)(2,1)}, bf16[4,32,4608]{2,1,0:T(8,128)(2,1)}, u32[]{:S(2)}, u32[]{:S(2)}) collective-permute-start(bf16[4,32,4608]{2,1,0:T(8,128)(2,1)} %fusion.7), channel_id=1, source_target_pairs={{0,2},{1,3},{2,0},{3,1},{4,6},{5,7},{6,4},{7,5},{8,10},{9,11},{10,... | collective-permute-start | bytes 3538952 | tf_op jit(solution)/shard_map/ppermute | solution.py:1184
  574.1 1.0 copy-start.7
  580.8 106.9 %collective-permute-start.5 = (bf16[32,9344]{1,0:T(8,128)(2,1)}, bf16[32,9344]{1,0:T(8,128)(2,1)}, u32[]{:S(2)}, u32[]{:S(2)}) collective-permute-start(bf16[32,9344]{1,0:T(8,128)(2,1)} %get-tuple-element.142), channel_id=1, source_target_pairs={{0,8},{4,12},{8,16},{12,20},{16,24},{20,28},{24,0},{28,4},{1,9},{5... | collective-permute-start | bytes 1794056 | tf_op jit(solution)/shard_map/ppermute | solution.py:1195
  581.6 106.1 %collective-permute-start.6 = (bf16[32,9344]{1,0:T(8,128)(2,1)}, bf16[32,9344]{1,0:T(8,128)(2,1)}, u32[]{:S(2)}, u32[]{:S(2)}) collective-permute-start(bf16[32,9344]{1,0:T(8,128)(2,1)} %get-tuple-element.143), channel_id=1, source_target_pairs={{0,16},{4,20},{8,24},{12,28},{16,0},{20,4},{24,8},{28,12},{1,17},{... | collective-permute-start | bytes 1794056 | tf_op jit(solution)/shard_map/ppermute | solution.py:1195
  583.6 104.2 %collective-permute-start.7 = (bf16[32,9344]{1,0:T(8,128)(2,1)S(1)}, bf16[32,9344]{1,0:T(8,128)(2,1)}, u32[]{:S(2)}, u32[]{:S(2)}) collective-permute-start(bf16[32,9344]{1,0:T(8,128)(2,1)S(1)} %get-tuple-element.144), channel_id=1, source_target_pairs={{0,24},{4,28},{8,0},{12,4},{16,8},{20,12},{24,16},{28,20},{1,25},{... | collective-permute-start | bytes 1794056 | tf_op jit(solution)/shard_map/ppermute | solution.py:1195
  680.3 5.5 copy-start.6
Sparse Core Ops, SparseCore 0:
  24.8 44.0 all-gather.5
  70.5 47.7 all-gather.9
  121.7 143.2 all-gather.7

commit v3 on v2

--- a/solution.py
+++ b/solution.py
@@ -75,6 +75,175 @@
     first = lanes_of(tile.shape) % HEAD_DIM < HEAD_DIM // 2
     partner = jnp.where(first, pltpu.roll(tile, LANES - 32, 1), pltpu.roll(tile, 32, 1))
     return tile * cosine + partner * sine
+
+
+class Exchange:
+    def __init__(self, axis, size, send, recv):
+        self.axis, self.size, self.send, self.recv = axis, size, send, recv
+        self.me = lax.axis_index(axis)
+        self.going = []
+
+    def to(self, offset):
+        return lax.rem(self.me + offset, self.size)
+
+    def source(self, offset):
+        return lax.rem(self.me - offset + self.size, self.size)
+
+    def start(self, source_of, target_of):
+        for offset in range(1, self.size):
+            partner = self.to(offset)
+            copy = pltpu.make_async_remote_copy(
+                src_ref=source_of(partner),
+                dst_ref=target_of(offset),
+                send_sem=self.send.at[offset - 1],
+                recv_sem=self.recv.at[offset - 1],
+                device_id={self.axis: partner},
+                device_id_type=pl.DeviceIdType.MESH,
+            )
+            copy.start()
+            self.going.append(copy)
+
+    def arrived(self):
+        for copy in self.going:
+            copy.wait_recv()
+
+    def sent(self):
+        for copy in self.going:
+            copy.wait_send()
+
+
+def greet(sizes):
+    barrier = pltpu.get_barrier_semaphore()
+    for axis, size in sizes.items():
+        for offset in range(1, size):
+            partner = lax.rem(lax.axis_index(axis) + offset, size)
+            pl.semaphore_signal(
+                barrier,
+                inc=1,
+                device_id={axis: partner},
+                device_id_type=pl.DeviceIdType.MESH,
+            )
+    pl.semaphore_wait(barrier, sum(size - 1 for size in sizes.values()))
+
+
+class Sent:
+    def __init__(self, source, target, axis, index, send, recv):
+        self.copy = pltpu.make_async_remote_copy(
+            src_ref=source,
+            dst_ref=target,
+            send_sem=send,
+            recv_sem=recv,
+            device_id={axis: index},
+            device_id_type=pl.DeviceIdType.MESH,
+        )
+
+    def start(self):
+        self.copy.start()
+        return self
+
+
+pieces_along_y = 5
+
+
+def start_kernel(n_dp, n_fs, x_ref, w_ref, v_ref, x_all, w_all, v_all, *sems):
+    (
+        chip_send,
+        chip_recv,
+        core_send,
+        core_recv,
+        own_sem,
+        *sems,
+    ) = sems
+    me, my_dp = lax.axis_index("fsdp"), lax.axis_index("dp")
+    core, chip = lax.rem(me, 2), me // 2
+    other_core = chip * 2 + 1 - core
+    other_chip = (1 - chip) * 2 + core
+    over = [
+        Exchange(axis, n_dp if axis == "dp" else n_fs, sems[2 * i], sems[2 * i + 1])
+        for i, axis in enumerate(("fsdp", "fsdp", "dp", "dp"))
+    ]
+    greet({"dp": n_dp, "fsdp": n_fs})
+    over[0].start(lambda partner: w_ref.at[partner], lambda offset: w_all.at[my_dp, me])
+    over[1].start(lambda partner: v_ref, lambda offset: v_all.at[my_dp, me])
+    piece = x_ref.shape[0] // pieces_along_y
+    spans = [pl.ds(at * piece, piece) for at in range(pieces_along_y)]
+    along_y = [
+        Sent(
+            x_ref.at[span],
+            x_all.at[me, span],
+            "fsdp",
+            other_chip,
+            chip_send.at[at],
+            chip_recv.at[at],
+        ).start()
+        for at, span in enumerate(spans)
+    ]
+    own = [
+        pltpu.make_async_copy(w_ref.at[me], w_all.at[my_dp, me], own_sem.at[0]),
+        pltpu.make_async_copy(v_ref, v_all.at[my_dp, me], own_sem.at[1]),
+        pltpu.make_async_copy(x_ref, x_all.at[me], own_sem.at[2]),
+    ]
+    for copy in own:
+        copy.start()
+    last = pieces_along_y
+    to_core = [
+        Sent(
+            x_ref, x_all.at[me], "fsdp", other_core, core_send.at[last], core_recv.at[last]
+        ).start()
+    ]
+    own[0].wait()
+    own[1].wait()
+    over[0].arrived()
+    over[1].arrived()
+    over[2].start(lambda partner: w_all.at[my_dp], lambda offset: w_all.at[my_dp])
+    over[3].start(lambda partner: v_all.at[my_dp], lambda offset: v_all.at[my_dp])
+    for at, span in enumerate(spans):
+        along_y[at].copy.wait_recv()
+        to_core.append(
+            Sent(
+                x_all.at[other_chip, span],
+                x_all.at[other_chip, span],
+                "fsdp",
+                other_core,
+                core_send.at[at],
+                core_recv.at[at],
+            ).start()
+        )
+    for one in to_core:
+        one.copy.wait_recv()
+    over[2].arrived()
+    over[3].arrived()
+    own[2].wait()
+    for exchange in over:
+        exchange.sent()
+    for one in along_y + to_core:
+        one.copy.wait_send()
+
+
+def gather_start(rows_in, w_split, vector_tile):
+    n_dp, n_fs = lax.axis_size("dp"), lax.axis_size("fsdp")
+    anywhere = pl.BlockSpec(memory_space=pl.ANY)
+    dma = lambda axis: [pltpu.SemaphoreType.DMA(((n_dp if axis == "dp" else n_fs) - 1,))] * 2
+    return pl.pallas_call(
+        functools.partial(start_kernel, n_dp, n_fs),
+        in_specs=[anywhere] * 3,
+        out_specs=[anywhere] * 3,
+        out_shape=[
+            jax.ShapeDtypeStruct((n_fs,) + rows_in.shape, BF),
+            jax.ShapeDtypeStruct((n_dp,) + w_split.shape, BF),
+            jax.ShapeDtypeStruct((n_dp, n_fs) + vector_tile.shape, F32),
+        ],
+        scratch_shapes=[
+            pltpu.SemaphoreType.DMA((pieces_along_y,)),
+            pltpu.SemaphoreType.DMA((pieces_along_y,)),
+            pltpu.SemaphoreType.DMA((pieces_along_y + 1,)),
+            pltpu.SemaphoreType.DMA((pieces_along_y + 1,)),
+            pltpu.SemaphoreType.DMA((3,)),
+        ]
+        + [sem for axis in ("fsdp", "fsdp", "dp", "dp") for sem in dma(axis)],
+        compiler_params=params(collective_id=3, has_side_effects=True),
+        name="gather_start",
+    )(rows_in, w_split, vector_tile)
 
 
 def heads_kernel(doc_rows, len_ref, x_ref, w_ref, b_ref, cos_ref, sin_ref, q_ref, k_ref, v_ref):
@@ -201,6 +370,7 @@
 
 
 def attend_back_kernel(
+    halves,
     doc_rows,
     parts,
     q_ref,
@@ -235,8 +405,8 @@
         lane = lanes_of(grad_pair.shape)
         product = grad_pair.astype(F32) * o_ref[0, span, :]
         turned = pltpu.roll(grad_pair.astype(F32), 64, 1).astype(BF)
-        pieces = []
-        for head in range(2):
+        joined = jnp.zeros(grad_pair.shape, F32)
+        for head in halves:
             query = q_ref[head, span, :]
             inside = lane < 64 if head == 0 else lane >= 64
             row_dot = jnp.sum(jnp.where(inside, product, 0.0), axis=1, keepdims=True)
@@ -269,8 +439,8 @@
                     dv_doc[head, part] += dot_nn(grad_t, powers.astype(BF))
                     dk_doc[head, part] += dot_nn(query_t, grad_scores)
                 grad_query += dot_nn(grad_scores, key)
-            pieces.append(grad_query)
-        joined = jnp.where(lane < 64, pieces[0], pltpu.roll(pieces[1], 64, 1)) * HEAD_DIM**-0.5
+            joined = jnp.where(inside, pltpu.roll(grad_query, 64, 1) if head else grad_query, joined)
+        joined = joined * HEAD_DIM**-0.5
         low = turn(joined, cos_ref[at, span, :], -sin_ref[at, span, :]).astype(BF)
         dq_ref[0, span, :] = low
         sums_ref[0:1, :] += column_sum(low.astype(F32))
@@ -278,8 +448,13 @@
     @pl.when(at == parts - 1)
     def _():
         def both(kept, part):
-            first, second = kept[0, part].T, kept[1, part].T
-            return jnp.where(lanes_of(first.shape) < 64, first, pltpu.roll(second, 64, 1))
+            sides = [kept[head, part].T for head in halves]
+            lane = lanes_of(sides[0].shape)
+            if len(halves) == 2:
+                return jnp.where(lane < 64, sides[0], pltpu.roll(sides[1], 64, 1))
+            if halves[0]:
+                return jnp.where(lane < 64, 0.0, pltpu.roll(sides[0], 64, 1))
+            return jnp.where(lane < 64, sides[0], 0.0)
 
         for part in range(parts):
             for span, keys, values in (
@@ -295,7 +470,7 @@
                 sums_ref[2:3, :] += column_sum(low.astype(F32))
 
 
-def attend_back(pair, query, key, value, grad, mixed, cosine, sine, doc_rows):
+def attend_back(pair, halves, query, key, value, grad, mixed, cosine, sine, doc_rows):
     heads, total, _ = query.shape
     parts, rows, width = grad.shape
     own_at = rows // QLEN
@@ -307,7 +482,7 @@
     full = pl.BlockSpec((parts, rows, LANES), lambda part: (0, 0, 0))
     shape = jax.ShapeDtypeStruct((parts, rows, LANES), BF)
     return pl.pallas_call(
-        functools.partial(attend_back_kernel, doc_rows, parts),
+        functools.partial(attend_back_kernel, halves, doc_rows, parts),
         grid=(parts,),
         in_specs=[mine, whole, whole, own, own, flat, flat, table, table],
         out_specs=[
@@ -325,7 +500,7 @@
         ],
         compiler_params=params(),
         cost_estimate=pl.CostEstimate(
-            flops=10 * 2 * total * total * 256, bytes_accessed=1 << 24, transcendentals=0
+            flops=10 * len(halves) * total * total * 256, bytes_accessed=1 << 24, transcendentals=0
         ),
         name="attend_back",
     )(query, key, value, key, value, grad, mixed, cosine, sine)
@@ -340,10 +515,11 @@
 
 GROUPS = 4
 CHUNK = 512
+OWN_ROWS = 32
 
 
 def joined_up(up_ref):
-    size = up_ref.shape[0] // (CHUNK // (QLEN * GROUPS))
+    size = OWN_ROWS
     pieces = [
         up_ref[at : at + size, group * D : (group + 1) * D]
         for at in range(0, up_ref.shape[0], size)
@@ -487,7 +663,8 @@
     att_ref,
     wo_ref,
     vec_ref,
-    grads_ref,
+    keep_ref,
+    send_ref,
     dbi_ref,
     datt_ref,
     dsum_ref,
@@ -508,30 +685,50 @@
     hidden = GROUPS * D
     slot = lax.rem(step, 2)
 
+    core = lax.rem(lax.axis_index("fsdp"), 2)
+
+    def both(source, rows_at, columns, sem):
+        return [
+            pltpu.make_async_copy(
+                source.at[:, which], target.at[rows_at, :, columns], sem.at[index]
+            )
+            for index, (which, target) in enumerate(((1 - core, send_ref), (core, keep_ref)))
+        ]
+
+    count = dwu_ref.shape[1]
+    every = pl.ds(0, keep_ref.shape[0])
+
     def up_copy(at, place):
-        here = pl.ds(pl.multiple_of(at * (CHUNK // GROUPS), CHUNK // GROUPS), CHUNK // GROUPS)
-        return pltpu.make_async_copy(
-            dwu_ref.at[place], grads_ref.at[here, pl.ds(0, hidden)], up_sem.at[place]
+        return both(
+            dwu_ref.at[place], pl.ds(at * count, count), pl.ds(0, hidden), up_sem.at[place]
         )
 
     def down_copy(at, place):
         here = pl.ds(pl.multiple_of(hidden + at * CHUNK, CHUNK), CHUNK)
-        return pltpu.make_async_copy(
-            dwi_ref.at[place], grads_ref.at[:, here], down_sem.at[place]
-        )
-
-    vector_copy = pltpu.make_async_copy(
-        dwv_ref, grads_ref.at[:, pl.ds(2 * hidden + D, LANES)], once_sem.at[0]
-    )
-    out_copy = pltpu.make_async_copy(
-        dwo_ref, grads_ref.at[:, pl.ds(2 * hidden, D)], once_sem.at[1]
-    )
+        return both(dwi_ref.at[place], every, here, down_sem.at[place])
+
+    def vector_copy():
+        return both(dwv_ref, every, pl.ds(2 * hidden + D, LANES), once_sem.at[0])
+
+    def out_copy():
+        return both(dwo_ref, every, pl.ds(2 * hidden, D), once_sem.at[1])
+
+    def start(copies):
+        for copy in copies:
+            copy.start()
+
+    def wait(copies):
+        for copy in copies:
+            copy.wait()
+
+    def by_device(value):
+        return value.astype(BF).reshape(-1, 2, OWN_ROWS, value.shape[1])
 
     @pl.when(step == 0)
     def _():
         dproj = dproj_ref[...]
-        dwv_ref[...] = dot_tn(enc_ref[...], dproj).astype(BF)
-        vector_copy.start()
+        dwv_ref[...] = by_device(dot_tn(enc_ref[...], dproj))
+        start(vector_copy())
         grad = dot_nt(dproj, wv_ref[...])
         hat = hat2_ref[...].astype(F32)
         dvec_ref[4:5, :] = column_sum(grad * hat)
@@ -544,21 +741,19 @@
 
     @pl.when(step >= 2)
     def _():
-        up_copy(step - 2, slot).wait()
-        down_copy(step - 2, slot).wait()
+        wait(up_copy(step - 2, slot))
+        wait(down_copy(step - 2, slot))
 
     low = low_ref[...]
     dinner = (dot_nt(low, joined_up(wu_ref)) * slope_ref[...].astype(F32)).astype(BF)
     dbi_ref[...] = column_sum(dinner.astype(F32))
     up_grad = dot_tn(act_ref[...], low).astype(BF)
-    for at in range(0, CHUNK, QLEN):
-        own, group = at // (QLEN * GROUPS), at // QLEN % GROUPS
-        dwu_ref[slot, own * QLEN : (own + 1) * QLEN, group * D : (group + 1) * D] = up_grad[
-            at : at + QLEN
-        ]
-    up_copy(step, slot).start()
-    dwi_ref[slot] = dot_tn(low1_ref[...], dinner).astype(BF)
-    down_copy(step, slot).start()
+    for at in range(0, CHUNK, OWN_ROWS):
+        own, group = at // (OWN_ROWS * GROUPS), at // OWN_ROWS % GROUPS
+        dwu_ref[slot, own // 2, own % 2, :, group * D : (group + 1) * D] = up_grad[at : at + OWN_ROWS]
+    start(up_copy(step, slot))
+    dwi_ref[slot] = by_device(dot_tn(low1_ref[...], dinner))
+    start(down_copy(step, slot))
     total_ref[...] += dot_nt(dinner, wi_ref[...])
 
     @pl.when(step == pl.num_programs(0) - 1)
@@ -573,14 +768,15 @@
         dvec_ref[0:1, :] = column_sum(attn_low.astype(F32))
         for part in range(parts):
             here = slice(part * width, (part + 1) * width)
-            dwo_ref[here, :] = dot_tn(att_ref[part], attn_low).astype(BF)
+            size = width // (2 * OWN_ROWS)
+            dwo_ref[part * size : (part + 1) * size] = by_device(dot_tn(att_ref[part], attn_low))
             datt_ref[part] = dot_nt(attn_low, wo_ref[here, :]).astype(BF)
-        out_copy.start()
-        vector_copy.wait()
+        start(out_copy())
+        wait(vector_copy())
         for place in range(2):
-            up_copy(steps - 2 + place, place).wait()
-            down_copy(steps - 2 + place, place).wait()
-        out_copy.wait()
+            wait(up_copy(steps - 2 + place, place))
+            wait(down_copy(steps - 2 + place, place))
+        wait(out_copy())
 
 
 def rows_backward(dproj, enc, hat2, inv2, packed, act, slope, low1, hat1, inv1, att, vectors):
@@ -589,6 +785,8 @@
     columns = pl.BlockSpec((rows, CHUNK), lambda step: (0, step))
     bias = pl.BlockSpec((1, CHUNK), lambda step: (0, step))
     weights = packed_specs()
+    pairs = packed.shape[0] // (2 * OWN_ROWS)
+    half = jax.ShapeDtypeStruct((pairs, OWN_ROWS, packed.shape[1]), BF)
     operands = (
         (dproj, None),
         (enc, None),
@@ -612,13 +810,15 @@
         in_specs=[keep(entry.shape) if spec is None else spec for entry, spec in operands],
         out_specs=[
             pl.BlockSpec(memory_space=pl.ANY),
+            pl.BlockSpec(memory_space=pl.ANY),
             bias,
             keep(att.shape),
             keep((rows, D)),
             keep((8, D)),
         ],
         out_shape=[
-            jax.ShapeDtypeStruct(packed.shape, BF),
+            half,
+            half,
             jax.ShapeDtypeStruct((1, hidden), F32),
             jax.ShapeDtypeStruct(att.shape, BF),
             jax.ShapeDtypeStruct((rows, D), F32),
@@ -627,13 +827,13 @@
         scratch_shapes=[
             pltpu.VMEM((rows, D), BF),
             pltpu.VMEM((rows, D), F32),
-            pltpu.VMEM((D, LANES), BF),
-            pltpu.VMEM((D, D), BF),
-            pltpu.VMEM((2, CHUNK // GROUPS, hidden), BF),
-            pltpu.VMEM((2, D, CHUNK), BF),
-            pltpu.SemaphoreType.DMA((2,)),
-            pltpu.SemaphoreType.DMA((2,)),
-            pltpu.SemaphoreType.DMA((2,)),
+            pltpu.VMEM((pairs, 2, OWN_ROWS, LANES), BF),
+            pltpu.VMEM((pairs, 2, OWN_ROWS, D), BF),
+            pltpu.VMEM((2, CHUNK // (2 * GROUPS * OWN_ROWS), 2, OWN_ROWS, hidden), BF),
+            pltpu.VMEM((2, pairs, 2, OWN_ROWS, CHUNK), BF),
+            pltpu.SemaphoreType.DMA((2, 2)),
+            pltpu.SemaphoreType.DMA((2, 2)),
+            pltpu.SemaphoreType.DMA((2, 2)),
         ],
         compiler_params=params(),
         cost_estimate=pl.CostEstimate(
@@ -643,78 +843,11 @@
     )(*(entry for entry, _ in operands))
 
 
-class Exchange:
-    def __init__(self, axis, size, send, recv):
-        self.axis, self.size, self.send, self.recv = axis, size, send, recv
-        self.me = lax.axis_index(axis)
-        self.going = []
-
-    def to(self, offset):
-        return lax.rem(self.me + offset, self.size)
-
-    def source(self, offset):
-        return lax.rem(self.me - offset + self.size, self.size)
-
-    def start(self, source_of, target_of):
-        for offset in range(1, self.size):
-            partner = self.to(offset)
-            copy = pltpu.make_async_remote_copy(
-                src_ref=source_of(partner),
-                dst_ref=target_of(offset),
-                send_sem=self.send.at[offset - 1],
-                recv_sem=self.recv.at[offset - 1],
-                device_id={self.axis: partner},
-                device_id_type=pl.DeviceIdType.MESH,
-            )
-            copy.start()
-            self.going.append(copy)
-
-    def arrived(self):
-        for copy in self.going:
-            copy.wait_recv()
-
-    def sent(self):
-        for copy in self.going:
-            copy.wait_send()
-
-
-def greet(sizes):
-    barrier = pltpu.get_barrier_semaphore()
-    for axis, size in sizes.items():
-        for offset in range(1, size):
-            partner = lax.rem(lax.axis_index(axis) + offset, size)
-            pl.semaphore_signal(
-                barrier,
-                inc=1,
-                device_id={axis: partner},
-                device_id_type=pl.DeviceIdType.MESH,
-            )
-    pl.semaphore_wait(barrier, sum(size - 1 for size in sizes.values()))
-
-
-class Sent:
-    def __init__(self, source, target, axis, index, send, recv):
-        self.copy = pltpu.make_async_remote_copy(
-            src_ref=source,
-            dst_ref=target,
-            send_sem=send,
-            recv_sem=recv,
-            device_id={axis: index},
-            device_id_type=pl.DeviceIdType.MESH,
-        )
-
-    def start(self):
-        self.copy.start()
-        return self
-
-
-pieces_along_y = 5
-
-
-def heads_back_kernel(n_dp, n_fs, pairs, *refs):
+def heads_back_kernel(n_dp, n_fs, pair_of, *refs):
+    calls, pairs = len(pair_of), max(pair_of) + 1
     x_ref, w_ref, dsum_ref, vec_ref = refs[:4]
-    grad_refs = refs[4 : 4 + 3 * pairs]
-    dx_ref, dw_ref, dvec_ref = refs[4 + 3 * pairs : 7 + 3 * pairs]
+    call_refs = refs[4 : 4 + 3 * calls]
+    dx_ref, dw_ref, dvec_ref = refs[4 + 3 * calls : 7 + 3 * calls]
     (
         first_out,
         second_out,
@@ -724,6 +857,8 @@
         chip_in,
         kept_ref,
         dw_out,
+        dw_across,
+        dw_line,
         dw_in,
         dw_sum,
         vec_in,
@@ -733,15 +868,19 @@
         core_recv,
         chip_send,
         chip_recv,
+        across_send,
+        across_recv,
+        along_send,
+        along_recv,
         *sems,
-    ) = refs[7 + 3 * pairs :]
+    ) = refs[7 + 3 * calls :]
     me, my_dp = lax.axis_index("fsdp"), lax.axis_index("dp")
     core, chip = lax.rem(me, 2), me // 2
     other_core = chip * 2 + 1 - core
     other_chip = (1 - chip) * 2 + core
     over = [
         Exchange(axis, n_dp if axis == "dp" else n_fs, sems[2 * i], sems[2 * i + 1])
-        for i, axis in enumerate(("fsdp", "dp", "dp", "fsdp"))
+        for i, axis in enumerate(("fsdp", "dp", "fsdp"))
     ]
     greet({"dp": n_dp, "fsdp": n_fs})
     width = w_ref.shape[1] // 3
@@ -750,14 +889,18 @@
 
     over[0].start(lambda partner: vec_ref.at[partner], lambda offset: vec_in.at[offset - 1])
 
+    def gradient(index, pair, part):
+        found = [
+            call_refs[call * 3 + index][part] for call in range(calls) if pair_of[call] == pair
+        ]
+        return functools.reduce(lambda one, two: one + two, found)
+
     def back(part):
         total = jnp.zeros((rows, D), F32)
         for index in range(3):
             for pair in range(pairs):
                 here = index * width + pair * LANES
-                total += dot_nt(
-                    grad_refs[pair * 3 + index][part], w_ref[:, here : here + LANES]
-                )
+                total += dot_nt(gradient(index, pair, part), w_ref[:, here : here + LANES])
         return total
 
     def to_core(source, target, at):
@@ -783,58 +926,88 @@
         )
 
     block = D // n_dp
+    n_z, z, x = n_dp // 2, my_dp // 2, lax.rem(my_dp, 2)
+    across, along_z = [], []
     for index in range(3):
         for pair in range(pairs):
-            here = index * width + pair * LANES
+            here = slice(pair * LANES, (pair + 1) * LANES)
             total = jnp.zeros((D, LANES), F32)
             for part in range(n_fs):
-                total += dot_tn(x_ref[part], grad_refs[pair * 3 + index][part])
-            dw_out[:, :, here : here + LANES] = total.astype(BF).reshape(n_dp, block, LANES)
-    over[1].start(lambda partner: dw_out.at[partner], lambda offset: dw_in.at[offset - 1])
+                total += dot_tn(x_ref[part], gradient(index, pair, part))
+            dw_out[index, :, :, :, here] = total.astype(BF).reshape(n_z, 2, block, LANES)
+        across.append(
+            Sent(
+                dw_out.at[index, :, 1 - x],
+                dw_across.at[index],
+                "dp",
+                z * 2 + 1 - x,
+                across_send.at[index],
+                across_recv.at[index],
+            ).start()
+        )
+
+    def send_along_z(index):
+        across[index].copy.wait_recv()
+        dw_line[index] = (dw_out[index, :, x].astype(F32) + dw_across[index].astype(F32)).astype(BF)
+        for offset in range(1, n_z):
+            partner = lax.rem(z + offset, n_z)
+            along_z.append(
+                Sent(
+                    dw_line.at[index, partner],
+                    dw_in.at[index, offset - 1],
+                    "dp",
+                    partner * 2 + x,
+                    along_send.at[index, offset - 1],
+                    along_recv.at[index, offset - 1],
+                ).start()
+            )
 
     over[0].arrived()
     vec_total = vec_ref[me]
     for offset in range(n_fs - 1):
         vec_total = vec_total + vec_in[offset]
     vec_sum[...] = vec_total
-    over[2].start(lambda partner: vec_sum.at[partner], lambda offset: vec_last.at[offset - 1])
-
+    over[1].start(lambda partner: vec_sum.at[partner], lambda offset: vec_last.at[offset - 1])
+
+    send_along_z(0)
     second_out[...] = back(other_core).astype(BF)
     second = to_core(second_out, second_in, 1)
+    send_along_z(1)
     kept_ref[...] = back(me) + dsum_ref[...]
+    send_along_z(2)
     second.copy.wait_recv()
     kept_ref[...] += second_in[...].astype(F32)
 
-    over[2].arrived()
+    over[1].arrived()
     vec_total = vec_sum[my_dp]
     for offset in range(n_dp - 1):
         vec_total = vec_total + vec_last[offset]
     dvec_ref[...] = vec_total
 
-    over[1].arrived()
-    dw_total = dw_out[my_dp].astype(F32)
-    for offset in range(n_dp - 1):
-        dw_total = dw_total + dw_in[offset].astype(F32)
     each = block // n_fs
-    dw_sum[...] = dw_total.reshape(n_fs, each, 3 * width)
     mine = dw_ref.at[me]
+    for index in range(3):
+        total = dw_out[index, z, x].astype(F32) + dw_across[index, z].astype(F32)
+        for offset in range(n_z - 1):
+            along_z[index * (n_z - 1) + offset].copy.wait_recv()
+            total = total + dw_in[index, offset].astype(F32)
+        dw_sum[:, :, index * width : (index + 1) * width] = total.reshape(n_fs, each, width)
     dw_ref[me] = dw_sum[me]
-    over[3].start(lambda partner: dw_sum.at[partner], lambda offset: mine)
+    over[2].start(lambda partner: dw_sum.at[partner], lambda offset: mine)
     for at in range(pieces_along_y):
         here = slice(at * piece, (at + 1) * piece)
         along_y[at].copy.wait_recv()
         dx_ref[here, :] = (kept_ref[here, :] + chip_in[here, :].astype(F32)).astype(BF)
-    over[3].arrived()
+    over[2].arrived()
     for exchange in over:
         exchange.sent()
-    for one in [first, second] + along_y:
+    for one in [first, second] + across + along_y + along_z:
         one.copy.wait_send()
 
 
-def heads_backward(x_all, w_heads, dsum, vector_grads, grads):
+def heads_backward(x_all, w_heads, dsum, vector_grads, pair_of, grads):
     n_dp, n_fs = lax.axis_size("dp"), lax.axis_size("fsdp")
     _, rows, _ = x_all.shape
-    pairs = len(grads) // 3
     whole = pl.BlockSpec(memory_space=pltpu.VMEM)
     block = D // n_dp
     columns = w_heads.shape[1]
@@ -842,8 +1015,8 @@
     line = pltpu.VMEM((rows, D), BF)
     dma = lambda axis: [pltpu.SemaphoreType.DMA(((n_dp if axis == "dp" else n_fs) - 1,))] * 2
     return pl.pallas_call(
-        functools.partial(heads_back_kernel, n_dp, n_fs, pairs),
-        in_specs=[whole] * (4 + 3 * pairs),
+        functools.partial(heads_back_kernel, n_dp, n_fs, pair_of),
+        in_specs=[whole] * (4 + len(grads)),
         out_specs=[whole] * 3,
         out_shape=[
             jax.ShapeDtypeStruct((rows, D), BF),
@@ -853,8 +1026,10 @@
         scratch_shapes=[line] * 6
         + [
             pltpu.VMEM((rows, D), F32),
-            pltpu.VMEM((n_dp, block, columns), BF),
-            pltpu.VMEM((n_dp - 1, block, columns), BF),
+            pltpu.VMEM((3, n_dp // 2, 2, block, columns // 3), BF),
+            pltpu.VMEM((3, n_dp // 2, block, columns // 3), BF),
+            pltpu.VMEM((3, n_dp // 2, block, columns // 3), BF),
+            pltpu.VMEM((3, n_dp // 2 - 1, block, columns // 3), BF),
             pltpu.VMEM((n_fs, block // n_fs, columns), F32),
             pltpu.VMEM((n_fs - 1, n_dp) + tile, F32),
             pltpu.VMEM((n_dp,) + tile, F32),
@@ -863,8 +1038,12 @@
             pltpu.SemaphoreType.DMA((2,)),
             pltpu.SemaphoreType.DMA((pieces_along_y,)),
             pltpu.SemaphoreType.DMA((pieces_along_y,)),
+            pltpu.SemaphoreType.DMA((3,)),
+            pltpu.SemaphoreType.DMA((3,)),
+            pltpu.SemaphoreType.DMA((3, n_dp // 2 - 1)),
+            pltpu.SemaphoreType.DMA((3, n_dp // 2 - 1)),
         ]
-        + [sem for axis in ("fsdp", "dp", "dp", "fsdp") for sem in dma(axis)],
+        + [sem for axis in ("fsdp", "dp", "fsdp") for sem in dma(axis)],
         compiler_params=params(collective_id=2, has_side_effects=True),
         name="heads_backward",
     )(x_all, w_heads, dsum, vector_grads, *grads)
@@ -1091,16 +1270,18 @@
     width = D // parts
     split = query_weight.shape[0]
 
-    w_split = jnp.concatenate(
+    w_split = jnp.stack(
         [
-            entry[:, part * width : (part + 1) * width]
+            jnp.concatenate(
+                [
+                    entry[:, part * width : (part + 1) * width]
+                    for entry in (query_weight, key_weight, value_weight)
+                ],
+                axis=1,
+            )
             for part in range(parts)
-            for entry in (query_weight, key_weight, value_weight)
-        ],
-        axis=1,
+        ]
     )
-    w_split = lax.all_to_all(w_split, "fsdp", 1, 0, tiled=True)
-    w_heads = lax.all_gather(w_split, "dp", axis=0, tiled=True)
     small = [
         query_bias,
         key_bias,
@@ -1113,23 +1294,26 @@
         second_shift,
     ]
     hidden_split = inner_bias.shape[0]
-    packed = lax.all_gather(jnp.concatenate(small + [inner_bias]), AXES, axis=0, tiled=False)
-    packed = packed.astype(F32)
+    line = jnp.concatenate(small + [inner_bias]).astype(F32)
+    line = jnp.pad(line, (0, -line.shape[0] % (8 * LANES))).reshape(8, -1)
+    rows_in = jnp.concatenate([doc_tokens.reshape(doc_rows, D), query_tokens.reshape(QLEN, D)])
+    own_up = [outer_weight[group * split : (group + 1) * split] for group in range(GROUPS)]
+    packed_own = jnp.concatenate(own_up + [inner_weight, out_weight, vector_weight], axis=1)
+    x_all, w_heads, packed = gather_start(rows_in, w_split, line)
+    packed_own, x_all = lax.optimization_barrier((packed_own, x_all))
+    packed_w = lax.all_gather(packed_own, AXES, axis=0, tiled=True)
+    w_heads = w_heads.reshape(D, 3 * width)
+    packed = packed.reshape(lax.axis_size("dp") * parts, -1)
 
     def vector(index):
         return packed[:, index * split : (index + 1) * split].reshape(-1)
 
-    inner_vec = packed[:, len(small) * split :].reshape(1, -1)
+    inner_at = len(small) * split
+    inner_vec = packed[:, inner_at : inner_at + hidden_split].reshape(1, -1)
     vectors = jnp.stack([vector(i) for i in (3, 4, 5, 6, 7, 8)] + [jnp.zeros((D,), F32)] * 2)
     b_heads = jnp.concatenate(
         [lax.dynamic_slice(vector(i), (mine * width,), (width,)) for i in range(3)]
     ).reshape(1, -1)
-
-    rows_in = jnp.concatenate([doc_tokens.reshape(doc_rows, D), query_tokens.reshape(QLEN, D)])
-    x_all = lax.all_gather(rows_in, "fsdp")
-    own_up = [outer_weight[group * split : (group + 1) * split] for group in range(GROUPS)]
-    packed_own = jnp.concatenate(own_up + [inner_weight, out_weight, vector_weight], axis=1)
-    packed_w = lax.all_gather(packed_own, AXES, axis=0, tiled=True)
 
     tables = rope_tables(parts, doc_rows)
     cosine, sine = jnp.asarray(tables[0]), jnp.asarray(tables[1])
@@ -1148,7 +1332,7 @@
     )
     dproj = jnp.concatenate([grad_doc, grad_query])
 
-    grads, dbi, datt, dsum, dvec = rows_backward(
+    keep, send, dbi, datt, dsum, dvec = rows_backward(
         dproj, enc, hat2, inv2, packed_w, act, slope, low1, hat1, inv1, att, vectors
     )
     grad_mixed = lax.all_to_all(datt, "fsdp", 0, 0, tiled=True)
@@ -1158,44 +1342,58 @@
     z, x = lax.axis_index("dp") // 2, lax.axis_index("dp") % 2
     core, y = mine % 2, mine // 2
     pick = lambda value, index, axis: lax.dynamic_index_in_dim(value, index, axis, False)
-    middle = grads.shape[1] // 2 // LANES * LANES
-    by_device = grads.reshape(n_dp // 2, 2, 2, 2, split, -1)
+    middle = keep.shape[2] // 2 // LANES * LANES
+    n_z = n_dp // 2
+    whole = (n_z, 2, 2, split, keep.shape[2])
     across = [(d, d ^ 1) for d in range(n_dp)]
     add = lambda one, two: one.astype(F32) + two.astype(F32)
-    from_core = lax.ppermute(pick(by_device, 1 - core, 3), "fsdp", other_core(parts))
-    own = lambda columns: pick(by_device, core, 3)[..., columns]
+    keep = keep.reshape(whole)
+    from_core = lax.ppermute(send, "fsdp", other_core(parts)).reshape(whole)
     left, right = slice(0, middle), slice(middle, None)
-    sum_left = add(own(left), from_core[..., left])
-    sum_right = add(own(right), from_core[..., right])
+    sum_left = add(keep[..., left], from_core[..., left])
+    sum_right = add(keep[..., right], from_core[..., right])
     out_x = pick(sum_left, 1 - x, 1).astype(BF)
     out_y = pick(sum_right, 1 - y, 2).astype(BF)
     out_x, out_y, *pair_args = lax.optimization_barrier((out_x, out_y) + pair_args)
     left_x = lax.ppermute(out_x, "dp", across)
     right_y = lax.ppermute(out_y, "fsdp", other_chip(parts))
-    grads_pair = list(attend_back(0, *pair_args, doc_rows))
-    left_x, right_y, grads_pair[0] = lax.optimization_barrier((left_x, right_y, grads_pair[0]))
+    calls = [list(attend_back(0, (0, 1), *pair_args, doc_rows))]
+    left_x, right_y, calls[0][0] = lax.optimization_barrier((left_x, right_y, calls[0][0]))
     sum_left = add(pick(sum_left, x, 1), left_x)
     sum_right = add(pick(sum_right, y, 2), right_y)
     out_y = pick(sum_left, 1 - y, 1).astype(BF)
     out_x = pick(sum_right, 1 - x, 1).astype(BF)
-    out_x, out_y, grads_pair[0], *pair_args = lax.optimization_barrier(
-        (out_x, out_y, grads_pair[0], *pair_args)
+    out_x, out_y, calls[0][0], *pair_args = lax.optimization_barrier(
+        (out_x, out_y, calls[0][0], *pair_args)
     )
     left_y = lax.ppermute(out_y, "fsdp", other_chip(parts))
     right_x = lax.ppermute(out_x, "dp", across)
-    pairs = [grads_pair, list(attend_back(1, *pair_args, doc_rows))]
-    left_y, right_x, pairs[1][0] = lax.optimization_barrier((left_y, right_x, pairs[1][0]))
-    by_z = jnp.concatenate(
+    calls.append(list(attend_back(1, (0,), *pair_args, doc_rows)))
+    left_y, right_x, calls[1][0] = lax.optimization_barrier((left_y, right_x, calls[1][0]))
+    grads_own = jnp.concatenate(
         [add(pick(sum_left, y, 1), left_y), add(pick(sum_right, x, 1), right_x)], axis=-1
-    ).astype(BF)
-    n_z = n_dp // 2
-    grads_own = pick(by_z, z, 0).astype(F32)
-    for shift in range(1, n_z):
-        along = [(d, (d + 2 * shift) % n_dp) for d in range(n_dp)]
-        grads_own += lax.ppermute(pick(by_z, (z + shift) % n_z, 0), "dp", along).astype(F32)
+    )
+    bits = n_z.bit_length() - 1
+    for bit in range(bits):
+        grads_own = grads_own.reshape(-1, 2, split, grads_own.shape[-1])
+        mine_bit = z // 2**bit % 2
+        out_z = pick(grads_own, 1 - mine_bit, 1).astype(BF)
+        if bit == 0:
+            out_z, calls[1][0], *pair_args = lax.optimization_barrier(
+                (out_z, calls[1][0], *pair_args)
+            )
+        along = [(d, d ^ (2 << bit)) for d in range(n_dp)]
+        from_z = lax.ppermute(out_z, "dp", along)
+        if bit == 0:
+            calls.append(list(attend_back(1, (1,), *pair_args, doc_rows)))
+            from_z, calls[2][0] = lax.optimization_barrier((from_z, calls[2][0]))
+        grads_own = add(pick(grads_own, mine_bit, 1), from_z)
+    grads_own = grads_own.reshape(split, -1)
 
     place = jnp.arange(parts, dtype=jnp.int32)[None, :, None] == mine
-    db = jnp.stack([jnp.concatenate([pair[3][i] for pair in pairs]) for i in range(3)])
+    db = jnp.stack(
+        [jnp.concatenate([calls[0][3][i], calls[1][3][i] + calls[2][3][i]]) for i in range(3)]
+    )
     db_all = jnp.where(place, db[:, None, :], 0.0).reshape(3, D)
     vector_grads = jnp.concatenate([db_all, dvec[:6]]).reshape(9, -1, split).transpose(1, 0, 2)
     vector_grads = jnp.concatenate(
@@ -1205,7 +1403,12 @@
     vector_grads = jnp.pad(vector_grads, ((0, 0), (0, -used % (8 * LANES))))
     vector_grads = vector_grads.reshape(n_dp, parts, 8, -1).transpose(1, 0, 2, 3)
     grad_low, dw, summed = heads_backward(
-        x_all, w_heads, dsum, vector_grads, [entry for pair in pairs for entry in pair[:3]]
+        x_all,
+        w_heads,
+        dsum,
+        vector_grads,
+        (0, 1, 1),
+        [entry for call in calls for entry in call[:3]],
     )
     dw_own = dw.reshape(parts, split, 3, width).transpose(2, 1, 0, 3).reshape(3, split, D)
     summed = summed.reshape(-1)

time: 708 us -> 616 us (0.87)
  blocking collectives: 49.5 us -> 0 us
  waiting for transfers between devices: 123 us -> 75 us
  Pallas kernels: 381 us -> 416 us
  local copies, waits for them, and re-layouts: 77.2 us -> 53.3 us
    all_gather x2 -> x0, waiting for transfers between devices: 46.4 us -> none  [the longest x1 46.4 us: shards(): x_all = lax.all_gather(rows_in, 'fsdp')]
    unnamed x1 -> x0, blocking collectives: 40.7 us -> none
    dynamic_slice x3 -> x0, local copies, waits for them, and re-layouts: 31.3 us -> none  [shards(): lax.dynamic_index_in_dim(value, index, axis, False)]
    pallas_call x3 -> x5, Pallas kernels: 198 us -> 229 us  [the longest x3 112 us: attend_back(): pl.pallas_call(functools.partial(attend_back_kernel, halves, doc_rows, pa...]
    all_gather x1, waiting for transfers between devices: 41.4 us -> 31.9 us  [shards(): packed_w = lax.all_gather(packed_own, AXES, axis=0, tiled=True)]
    all_to_all x1 -> x0, blocking collectives: 8.79 us -> none  [shards(): w_split = lax.all_to_all(w_split, 'fsdp', 1, 0, tiled=True)]
    ppermute x4 -> x3, waiting for transfers between devices: 0.01 us -> 7.23 us  [the longest x1 7.22 us: shards(): from_core = lax.ppermute(send, 'fsdp', other_core(parts)).reshape(whole)]
    unnamed x77 -> x49, local copies, waits for them, and re-layouts: 17.5 us -> 19.8 us
  transfers between devices with their start and end apart: 13 -> 10, of which waited for: 3 -> 3; matrix products, arithmetic and copies ran while one was open for 7% -> 5% of each run, Pallas kernels for 37% -> 39%
where the time goes in v3:
time: 616 us; the launch traced here: 608 us
  Pallas kernels  416 us (68%)
  waiting for transfers between devices  75 us (12%)
  local copies, waits for them, and re-layouts  53.3 us (9%)
  other arithmetic  31.4 us (5%)
  starting transfers between devices  16.9 us (3%)
  between operations  15.5 us (3%)
    pallas_call x3, Pallas kernels, attend_back(): pl.pallas_call(functools.partial(attend_back_kernel, halves, doc_rows, pa...  112 us
    pallas_call x1, Pallas kernels, heads_backward(): pl.pallas_call(functools.partial(heads_back_kernel, n_dp, n_fs, pair_of),...  59.1 us
    pallas_call x1, Pallas kernels, gather_start(): pl.pallas_call(functools.partial(start_kernel, n_dp, n_fs), in_specs=[any...  58.1 us
    pallas_call x1, Pallas kernels, rows_backward(): pl.pallas_call(rows_back_kernel, grid=(hidden // CHUNK,), in_specs=[keep(...  55.2 us
    pallas_call x1, Pallas kernels, attend(): pl.pallas_call(functools.partial(attend_kernel, doc_rows, parts), grid=(h...  51.5 us
    pallas_call x1, Pallas kernels, maxsim(): pl.pallas_call(functools.partial(maxsim_kernel, n_dp, n_fs), in_specs=[wh...  37.4 us
    all_to_all x1, waiting for transfers between devices, shards(): att = lax.all_to_all(mixed, 'fsdp', 0, 0, tiled=True)  35.9 us
    all_gather x1, waiting for transfers between devices, shards(): packed_w = lax.all_gather(packed_own, AXES, axis=0, tiled=True)  31.9 us
  transfers between devices with their start and end apart: 10, of which 3 were waited for; matrix products, arithmetic and copies ran while one was open for 5% of the time, Pallas kernels for 39%

profile of v3, /device:TPU:1, one launch (start us, length us, event | category | flops | bytes accessed | tf_op | source)
XLA Modules:
  0.0 608.1 jit_solution(7059017074472564088)
XLA Ops:
  7.3 0.8 fusion.10
  8.1 0.8 fusion.11
  8.9 0.8 fusion.12
  9.6 6.8 %concatenate.57 = bf16[416]{0:T(512)(128)(2,1)S(1)} concatenate(bf16[32]{0:T(256)(128)(2,1)} %param.28, bf16[32]{0:T(256)(128)(2,1)} %param.30, bf16[32]{0:T(256)(128)(2,1)} %param.32, bf16[32]{0:T(256)(128)(2,1)} %param.34, bf16[32]{0:T(256)(128)(2,1)} %param.35, bf16[32]{0:T(256)(128)(2,1)} %param.36, bf16[32]{0:T(256)(128)(2,1)} %param.40, bf16[32]{0:T(256)(128)(2,1)} %param.41, ...), dimensions={0} | concatenate | bytes 1664 | tf_op jit(solution)/shard_map/concatenate | solution.py:1297
  17.0 0.8 slice_dynamic-update-slice_fusion.3
  17.8 0.8 slice_dynamic-update-slice_fusion.2
  18.7 0.8 slice_dynamic-update-slice_fusion.1
  19.5 0.8 slice_dynamic-update-slice_fusion
  20.4 2.8 pad_maximum_fusion.1.x_ref
  23.3 0.8 pad_maximum_fusion.4.w_ref
  24.1 58.1 %gather_start.1 = (bf16[4,800,1024]{2,1,0:T(8,128)(2,1)}, bf16[8,4,32,768]{3,2,1,0:T(8,128)(2,1)}, f32[8,4,8,128]{3,2,1,0:T(8,128)}) custom-call(bf16[800,1024]{1,0:T(8,128)(2,1)} %pad_maximum_fusion.1.x_ref, bf16[4,32,768]{2,1,0:T(8,128)(2,1)} %pad_maximum_fusion.4.w_ref, f32[8,128]{1,0:T(8,128)} %bitcast_convert_fusion.v_ref), custom_call_target="tpu_custom_call" | custom-call | tf_op jit(solution)/shard_map/gather_start/pallas_call | solution.py:227
  82.2 0.9 copy.100
  84.9 12.4 %project_heads.1 = (bf16[4,3200,128]{2,1,0:T(8,128)(2,1)}, bf16[4,3200,128]{2,1,0:T(8,128)(2,1)}, bf16[4,3200,128]{2,1,0:T(8,128)(2,1)}) custom-call(s32[1]{0:T(128)} %copy.108.len_ref, bf16[4,800,1024]{2,1,0:T(8,128)(2,1)} %get-tuple-element.103.x_ref.refs_0_, bf16[1024,768]{1,0:T(8,128)(2,1)} %bitcast.101, f32[1,768]{1,0:T(1,128)} %reshape.179.b_ref, ...), custom_call_target="tpu_custom_call" | custom-call | tf_op jit(solution)/shard_map/project_heads/pallas_call | solution.py:284
  97.3 51.5 %attend.1 = (bf16[4,800,256]{2,1,0:T(8,128)(2,1)}, f32[4,800,256]{2,1,0:T(8,128)}, bf16[4,3200,128]{2,1,0:T(8,128)(2,1)}) custom-call(bf16[4,3200,128]{2,1,0:T(8,128)(2,1)} %get-tuple-element.106.q_ref, bf16[4,3200,128]{2,1,0:T(8,128)(2,1)} %get-tuple-element.158.k_ref.ko_ref, bf16[4,3200,128]{2,1,0:T(8,128)(2,1)} %get-tuple-element.159.v_ref.vo_ref, ...), custom_call_target="tpu_custom_call" | custom-call | flops 41943040000 | bytes 16777216 | tf_op jit(solution)/shard_map/attend/pallas_call | solution.py:356
  148.8 5.1 all-to-all-start
  153.9 0.7 slice.274
  155.8 35.9 %all-to-all-done.att_ref = bf16[4,800,256]{2,1,0:T(8,128)(2,1)S(1)} async-done(((bf16[4,800,256]{2,1,0:T(8,128)(2,1)}), bf16[4,800,256]{2,1,0:T(8,128)(2,1)S(1)}, u32[]{:S(2)}, u32[]{:S(2)}) %all-to-all-start) | async-done | bytes 1638432 | tf_op jit(solution)/shard_map/all_to_all | solution.py:1324
  191.7 31.9 %all-gather.2.cloned.1.call-done.wo_ref.wi_ref.wu_ref.wv_ref = bf16[1024,9344]{1,0:T(8,128)(2,1)} async-done(((bf16[32,9344]{1,0:T(8,128)(2,1)}), bf16[1024,9344]{1,0:T(8,128)(2,1)}) %all-gather.2.cloned.1.call-update) | async-done | bytes 19136528 | tf_op jit(solution)/shard_map/all_gather | solution.py:1304
  223.6 30.1 %rows_forward.1 = (bf16[800,1024]{1,0:T(8,128)(2,1)}, f32[800,128]{1,0:T(8,128)}, bf16[800,1024]{1,0:T(8,128)(2,1)}, bf16[800,4096]{1,0:T(8,128)(2,1)}, bf16[800...) custom-call(bf16[4,800,256]{2,1,0:T(8,128)(2,1)} %copy-done.7, ...), custom_call_target="tpu_custom_call" | custom-call | flops 15099494400 | bytes 33554432 | tf_op jit(solution)/shard_map/rows_forward/pallas_call | solution.py:605
  253.7 1.8 slice.231.pd_ref
  255.5 1.3 slice.230.pq_ref
  256.8 0.9 broadcast_in_dim.41.mask_ref
  258.3 37.4 %maxsim.1 = (f32[8,128]{1,0:T(8,128)}, bf16[32,128]{1,0:T(8,128)(2,1)}, bf16[768,128]{1,0:T(8,128)(2,1)}) custom-call(f32[32,128]{1,0:T(8,128)} %slice.230.pq_ref, f32[768,128]{1,0:T(8,128)} %slice.231.pd_ref, f32[768,128]{1,0:T(8,128)} %broadcast_in_dim.41.mask_ref, s32[8,128]{1,0:T(8,128)} %broadcast_in_dim.43.label_ref), custom_call_target="tpu_custom_call" | custom-call | tf_op jit(solution)/shard_map/maxsim/pallas_call | solution.py:1208
  295.8 1.6 pad_maximum_fusion.3.dproj_ref
  297.4 55.2 %rows_backward.1 = (bf16[16,32,9344]{2,1,0:T(8,128)(2,1)}, bf16[16,32,9344]{2,1,0:T(8,128)(2,1)}, f32[1,4096]{1,0:T(1,128)}, bf16[4,800,256]{2,1,0:T(8,128)(2,1)...) custom-call(bf16[800,128]{1,0:T(8,128)(2,1)} %pad_maximum_fusion.3.dproj_ref, bf16[800,1024]{1,0:T(8,128)(2,1)} %get-tuple-element.113.enc_ref, ...), custom_call_target="tpu_custom_call" | custom-call | flops 30198988800 | bytes 67108864 | tf_op jit(solution)/shard_map/rows_backward/pallas_call | solution.py:807
  353.0 4.7 all-to-all-start.1
  359.4 1.3 slice_bitcast_fusion.1
  360.7 7.2 %collective-permute-done = bf16[16,32,9344]{2,1,0:T(8,128)(2,1)} collective-permute-done((bf16[16,32,9344]{2,1,0:T(8,128)(2,1)}, bf16[16,32,9344]{2,1,0:T(8,128)(2,1)}, u32[]{:S(2)}, u32[]{:S(2)}) %collective-permute-start) | collective-permute-done | bytes 9568288 | tf_op jit(solution)/shard_map/ppermute | solution.py:1351
  367.9 4.4 convert_add_fusion
  372.3 8.0 %convert_add_fusion.1 = f32[4,2,2,32,4608]{4,3,0,2,1:T(8,128)S(1)} fusion(bf16[4,2,2,32,9344]{4,3,2,1,0:T(8,128)(2,1)} %bitcast.100, bf16[4,2,2,32,9344]{4,3,2,1,0:T(8,128)(2,1)} %bitcast.16), kind=kLoop, calls=%fused_computation.1 | loop fusion | flops 7077888 | bytes 18874368 | tf_op jit(solution)/shard_map/add | solution.py:1349
  380.5 3.3 copy-done.2
  383.8 1.7 fusion.1
  385.5 1.1 collective-permute-start.2
  386.6 1.5 collective-permute-start.1
  388.1 51.9 %attend_back.3 = (bf16[4,800,128]{2,1,0:T(8,128)(2,1)}, bf16[4,800,128]{2,1,0:T(8,128)(2,1)}, bf16[4,800,128]{2,1,0:T(8,128)(2,1)}, f32[8,128]{1,0:T(8,128)}) custom-call(bf16[4,3200,128]{2,1,0:T(8,128)(2,1)} %get-tuple-element.157.q_ref, bf16[4,3200,128]{2,1,0:T(8,128)(2,1)} %get-tuple-element.158.k_ref.ko_ref, ...), custom_call_target="tpu_custom_call" | custom-call | flops 52428800000 | bytes 16777216 | tf_op jit(solution)/shard_map/attend_back/pallas_call | solution.py:484
  440.0 0.8 slice_bitcast_fusion.6
  440.9 3.7 bitcast_add_fusion.1
  444.6 2.4 copy-done.6
  447.1 1.2 copy-done.1
  448.4 2.2 bitcast_add_fusion
  450.6 2.2 copy-done.3
  453.3 1.2 collective-permute-start.3
  454.5 29.0 %attend_back.4 = (bf16[4,800,128]{2,1,0:T(8,128)(2,1)}, bf16[4,800,128]{2,1,0:T(8,128)(2,1)}, bf16[4,800,128]{2,1,0:T(8,128)(2,1)}, f32[8,128]{1,0:T(8,128)}) custom-call(bf16[4,3200,128]{2,1,0:T(8,128)(2,1)} %get-tuple-element.157.q_ref, bf16[4,3200,128]{2,1,0:T(8,128)(2,1)} %get-tuple-element.158.k_ref.ko_ref, ...), custom_call_target="tpu_custom_call" | custom-call | flops 26214400000 | bytes 16777216 | tf_op jit(solution)/shard_map/attend_back/pallas_call | solution.py:484
  483.5 2.4 bitcast_add_fusion.4
  485.9 1.0 copy-done.4
  487.6 2.2 copy-done.5
  489.9 0.8 collective-permute-start.5
  490.8 31.3 %attend_back.5 = (bf16[4,800,128]{2,1,0:T(8,128)(2,1)}, bf16[4,800,128]{2,1,0:T(8,128)(2,1)}, bf16[4,800,128]{2,1,0:T(8,128)(2,1)}, f32[8,128]{1,0:T(8,128)}) custom-call(bf16[4,3200,128]{2,1,0:T(8,128)(2,1)} %get-tuple-element.157.q_ref, bf16[4,3200,128]{2,1,0:T(8,128)(2,1)} %get-tuple-element.158.k_ref.ko_ref, ...), custom_call_target="tpu_custom_call" | custom-call | flops 26214400000 | bytes 16777216 | tf_op jit(solution)/shard_map/attend_back/pallas_call | solution.py:484
  522.1 0.8 add_bitcast_fusion.3
  524.1 1.0 copy-done.10
  525.1 2.2 bitcast_add_fusion.3
  527.4 0.9 dynamic-slice_convert_fusion.5
  528.3 1.9 collective-permute-start.6
  530.2 59.1 %heads_backward.1 = (bf16[800,1024]{1,0:T(8,128)(2,1)}, f32[4,32,768]{2,1,0:T(8,128)}, f32[8,128]{1,0:T(8,128)}) custom-call(bf16[4,800,1024]{2,1,0:T(8,128)(2,1)} %get-tuple-element.103.x_ref.refs_0_, bf16[1024,768]{1,0:T(8,128)(2,1)} %bitcast.102, f32[800,1024]{1,0:T(8,128)} %get-tuple-element.123.refs_2_, f32[4,8,8,128]{3,2,1,0:T(8,128)} %bitcast.108, ...), custom_call_target="tpu_custom_call" | custom-call | tf_op jit(solution)/shard_map/heads_backward/pallas_call | solution.py:1017
  589.4 1.2 reshape.194
  590.9 1.6 fusion.13
  592.5 1.3 slice.262
  593.9 0.7 copy.91
  594.6 0.7 copy.92
  595.4 0.7 copy.93
  596.7 1.3 slice_bitcast_fusion
  598.1 0.7 fusion.7
  598.8 0.8 slice.289
  600.2 0.8 pad_maximum_fusion.2
  (105 shorter events, 10.3 us)
Async XLA Ops:
  7.2 16.0 %copy-start.12 = (bf16[32,4096]{1,0:T(8,128)(2,1)S(1)}, bf16[32,4096]{1,0:T(8,128)(2,1)}, u32[]{:S(2)}) copy-start(bf16[32,4096]{1,0:T(8,128)(2,1)} %param.37) | copy-start | bytes 786436
  7.2 16.0 %copy-start.13 = (bf16[32,1024]{1,0:T(8,128)(2,1)S(1)}, bf16[32,1024]{1,0:T(8,128)(2,1)}, u32[]{:S(2)}) copy-start(bf16[32,1024]{1,0:T(8,128)(2,1)} %param.33) | copy-start | bytes 196612
  7.2 16.0 %copy-start.16 = (bf16[32,128]{1,0:T(8,128)(2,1)S(1)}, bf16[32,128]{1,0:T(8,128)(2,1)}, u32[]{:S(2)}) copy-start(bf16[32,128]{1,0:T(8,128)(2,1)} %param.43) | copy-start | bytes 24580
  7.2 216.3 %all-gather.2.cloned.1.call-start = ((), (), s32[]{:S(2)}) async-start(), calls=%async_computation.2 | async-start | bytes 19734528 | tf_op jit(solution)/shard_map/all_gather | solution.py:1304
  23.2 58.9 %copy-start.11 = (bf16[32,9344]{1,0:T(8,128)(2,1)}, bf16[32,9344]{1,0:T(8,128)(2,1)S(1)}, u32[]{:S(2)}) copy-start(bf16[32,9344]{1,0:T(8,128)(2,1)S(1)} %constant_dynamic-update-slice_fusion) | copy-start | bytes 1794052
  148.8 6.3 %copy-start.17 = (s32[8,4]{0,1:T(4,128)S(1)}, s32[8,4]{0,1:T(4,128)}, u32[]{:S(2)}) copy-start(s32[8,4]{0,1:T(4,128)} %param.26) | copy-start | bytes 388
  148.8 42.9 %all-to-all-start = ((bf16[4,800,256]{2,1,0:T(8,128)(2,1)}), bf16[4,800,256]{2,1,0:T(8,128)(2,1)S(1)}, u32[]{:S(2)}, u32[]{:S(2)}) async-start(bf16[4,800,256]{2,1,0:T(8,128)(2,1)} %get-tuple-element.109), calls=%async_computation | async-start | bytes 3276800 | tf_op jit(solution)/shard_map/all_to_all | solution.py:1324
  191.7 31.9 %copy-start.7 = (bf16[4,800,256]{2,1,0:T(8,128)(2,1)}, bf16[4,800,256]{2,1,0:T(8,128)(2,1)S(1)}, u32[]{:S(2)}) copy-start(bf16[4,800,256]{2,1,0:T(8,128)(2,1)S(1)} %all-to-all-done.att_ref) | copy-start | bytes 4915204
  352.6 5.1 copy-start.14
  352.6 5.3 copy-start.18
  352.6 6.1 %copy-start.8 = (bf16[800,1024]{1,0:T(8,128)(2,1)S(1)}, bf16[800,1024]{1,0:T(8,128)(2,1)}, u32[]{:S(2)}) copy-start(bf16[800,1024]{1,0:T(8,128)(2,1)} %get-tuple-element.113.enc_ref) | copy-start | bytes 4915204
  352.6 15.3 %collective-permute-start = (bf16[16,32,9344]{2,1,0:T(8,128)(2,1)}, bf16[16,32,9344]{2,1,0:T(8,128)(2,1)}, u32[]{:S(2)}, u32[]{:S(2)}) collective-permute-start(bf16[16,32,9344]{2,1,0:T(8,128)(2,1)} %get-tuple-element.125), channel_id=1, source_target_pairs={{0,1},{1,0},{2,3},{3,2},{4,5},{5,4},{6,7},{7,6},{8,9},{9,8},{10,11... | collective-permute-start | bytes 28704776 | tf_op jit(solution)/shard_map/ppermute | solution.py:1351
  353.0 32.5 %all-to-all-start.1 = ((bf16[4,800,256]{2,1,0:T(8,128)(2,1)}), bf16[4,800,256]{2,1,0:T(8,128)(2,1)}, u32[]{:S(2)}, u32[]{:S(2)}) async-start(bf16[4,800,256]{2,1,0:T(8,128)(2,1)} %get-tuple-element.127), calls=%async_computation.1 | async-start | bytes 3276800 | tf_op jit(solution)/shard_map/all_to_all | solution.py:1338
  372.3 8.0 %copy-start = (f32[4,2,2,32,4736]{4,3,0,1,2:T(8,128)}, f32[4,2,2,32,4736]{4,3,0,1,2:T(8,128)S(1)}, u32[]{:S(2)}) copy-start(f32[4,2,2,32,4736]{4,3,0,1,2:T(8,128)S(1)} %convert_add_fusion) | copy-start | bytes 29097988
  380.3 3.5 copy-start.2
  385.5 55.4 %collective-permute-start.2 = (bf16[4,2,32,4736]{3,2,0,1:T(8,128)(2,1)S(1)}, bf16[4,2,32,4736]{3,2,0,1:T(8,128)(2,1)}, u32[]{:S(2)}, u32[]{:S(2)}) collective-permute-start(bf16[4,2,32,4736]{3,2,0,1:T(8,128)(2,1)S(1)} %fusion), channel_id=1, source_target_pairs={{0,2},{1,3},{2,0},{3,1},{4,6},{5,7},{6,4},{7,5},{8,10},{9,11},{10,... | collective-permute-start | bytes 7274504 | tf_op jit(solution)/shard_map/ppermute | solution.py:1359
  386.6 54.2 %collective-permute-start.1 = (bf16[4,2,32,4608]{3,2,0,1:T(8,128)(2,1)}, bf16[4,2,32,4608]{3,2,0,1:T(8,128)(2,1)}, u32[]{:S(2)}, u32[]{:S(2)}) collective-permute-start(bf16[4,2,32,4608]{3,2,0,1:T(8,128)(2,1)} %fusion.1), channel_id=1, source_target_pairs={{0,4},{4,0},{8,12},{12,8},{16,20},{20,16},{24,28},{28,24},{1,5},{5... | collective-permute-start | bytes 7077896 | tf_op jit(solution)/shard_map/ppermute | solution.py:1358
  440.8 7.5 %copy-start.1 = (f32[4,2,2,32,4736]{4,3,0,1,2:T(8,128)S(1)}, f32[4,2,2,32,4736]{4,3,0,1,2:T(8,128)}, u32[]{:S(2)}) copy-start(f32[4,2,2,32,4736]{4,3,0,1,2:T(8,128)} %copy-done) | copy-start | bytes 29097988
  444.6 2.4 copy-start.6
  450.6 2.2 copy-start.3
  452.9 30.6 %collective-permute-start.4 = (bf16[4,32,4736]{2,1,0:T(8,128)(2,1)S(1)}, bf16[4,32,4736]{2,1,0:T(8,128)(2,1)S(1)}, u32[]{:S(2)}, u32[]{:S(2)}) collective-permute-start(bf16[4,32,4736]{2,1,0:T(8,128)(2,1)S(1)} %fusion.2), channel_id=1, source_target_pairs={{0,4},{4,0},{8,12},{12,8},{16,20},{20,16},{24,28},{28,24},{1,5},{5... | collective-permute-start | bytes 3637256 | tf_op jit(solution)/shard_map/ppermute | solution.py:1370
  453.3 30.2 %collective-permute-start.3 = (bf16[4,32,4608]{2,1,0:T(8,128)(2,1)S(1)}, bf16[4,32,4608]{2,1,0:T(8,128)(2,1)}, u32[]{:S(2)}, u32[]{:S(2)}) collective-permute-start(bf16[4,32,4608]{2,1,0:T(8,128)(2,1)S(1)} %fusion.4), channel_id=1, source_target_pairs={{0,2},{1,3},{2,0},{3,1},{4,6},{5,7},{6,4},{7,5},{8,10},{9,11},{10,... | collective-permute-start | bytes 3538952 | tf_op jit(solution)/shard_map/ppermute | solution.py:1369
  483.5 3.4 copy-start.4
  487.6 2.2 copy-start.5
  489.9 33.4 %copy-start.15 = (f32[1,4096]{1,0:T(1,128)S(1)}, f32[1,4096]{1,0:T(1,128)}, u32[]{:S(2)}) copy-start(f32[1,4096]{1,0:T(1,128)} %get-tuple-element.166) | copy-start | bytes 49156
  489.9 34.2 %collective-permute-start.5 = (bf16[2,32,9344]{2,1,0:T(8,128)(2,1)S(1)}, bf16[2,32,9344]{2,1,0:T(8,128)(2,1)S(1)}, u32[]{:S(2)}, u32[]{:S(2)}) collective-permute-start(bf16[2,32,9344]{2,1,0:T(8,128)(2,1)S(1)} %fusion.3), channel_id=1, source_target_pairs={{0,8},{4,12},{8,0},{12,4},{16,24},{20,28},{24,16},{28,20},{1,9},{5... | collective-permute-start | bytes 3588104 | tf_op jit(solution)/shard_map/ppermute | solution.py:1386
  524.1 1.0 copy-start.10
  528.3 69.7 %collective-permute-start.6 = (bf16[1,32,9344]{2,1,0:T(8,128)(2,1)}, bf16[1,32,9344]{2,1,0:T(8,128)(2,1)S(1)}, u32[]{:S(2)}, u32[]{:S(2)}) collective-permute-start(bf16[1,32,9344]{2,1,0:T(8,128)(2,1)} %dynamic-slice_convert_fusion.5), channel_id=1, source_target_pairs={{0,16},{4,20},{8,24},{12,28},{16,0},{20,4},{24,8},{28,12},{1,17},{... | collective-permute-start | bytes 1794056 | tf_op jit(solution)/shard_map/ppermute | solution.py:1386
  590.6 5.5 copy-start.9
Sparse Core Ops, SparseCore 0:
  82.3 141.1 all-gather.1

commit v4 on v3

--- a/solution.py
+++ b/solution.py
@@ -14,6 +14,9 @@
 PROJ = 128
 QLEN = 32
 LANES = 128
+GROUPS = 4
+CHUNK = 512
+OWN_ROWS = 32
 
 norm_eps = 1e-05
 vector_eps = 1e-06
@@ -143,107 +146,182 @@
 
 
 pieces_along_y = 5
-
-
-def start_kernel(n_dp, n_fs, x_ref, w_ref, v_ref, x_all, w_all, v_all, *sems):
+doc_pieces = 4
+
+
+class Rows:
+    def __init__(self, doc_ref, query_ref, x_all, chosen, sems):
+        me = lax.axis_index("fsdp")
+        core, chip = lax.rem(me, 2), me // 2
+        self.other_core = chip * 2 + 1 - core
+        self.other_chip = (1 - chip) * 2 + core
+        self.sems, self.x_all, self.going = sems, x_all, []
+        piece = doc_ref.shape[0] // doc_pieces
+        self.moved = []
+        for slot, at in enumerate(chosen):
+            if at < doc_pieces:
+                span = pl.ds(at * piece, piece)
+                source = doc_ref.at[span]
+            else:
+                span = pl.ds(doc_ref.shape[0], QLEN)
+                source = query_ref
+            self.moved.append((slot, span, source, x_all.at[me, span]))
+
+    def send(self, source, target, partner, kind, slot):
+        one = Sent(
+            source,
+            target,
+            "fsdp",
+            partner,
+            self.sems[2 * kind].at[slot],
+            self.sems[2 * kind + 1].at[slot],
+        ).start()
+        self.going.append(one)
+        return one
+
+    def start(self):
+        self.along_y = [
+            self.send(source, target, self.other_chip, 0, slot)
+            for slot, span, source, target in self.moved
+        ]
+        self.own = [
+            self.send(source, target, self.other_core, 1, slot)
+            for slot, span, source, target in self.moved
+        ]
+        self.local = []
+        for slot, span, source, target in self.moved:
+            copy = pltpu.make_async_copy(source, target, self.sems[6].at[slot])
+            copy.start()
+            self.local.append(copy)
+
+    def finish(self):
+        passed = []
+        for slot, span, source, target in self.moved:
+            self.along_y[slot].copy.wait_recv()
+            block = self.x_all.at[self.other_chip, span]
+            passed.append(self.send(block, block, self.other_core, 2, slot))
+        for one in self.own + passed:
+            one.copy.wait_recv()
+        for copy in self.local:
+            copy.wait()
+        for one in self.going:
+            one.copy.wait_send()
+
+
+def rows_sems(chosen):
+    return [pltpu.SemaphoreType.DMA((len(chosen),))] * 7
+
+
+def start_kernel(n_dp, n_fs, chosen, *refs):
     (
-        chip_send,
-        chip_recv,
-        core_send,
-        core_recv,
-        own_sem,
+        doc_ref,
+        query_ref,
+        w_ref,
+        v_ref,
+        x_all,
+        w_all,
+        v_all,
         *sems,
-    ) = sems
+    ) = refs
+    moving, (own_sem, line_send, line_recv, cross_send, cross_recv, *sems) = sems[:7], sems[7:]
     me, my_dp = lax.axis_index("fsdp"), lax.axis_index("dp")
-    core, chip = lax.rem(me, 2), me // 2
-    other_core = chip * 2 + 1 - core
-    other_chip = (1 - chip) * 2 + core
+    n_z, z, x = n_dp // 2, my_dp // 2, lax.rem(my_dp, 2)
     over = [
         Exchange(axis, n_dp if axis == "dp" else n_fs, sems[2 * i], sems[2 * i + 1])
-        for i, axis in enumerate(("fsdp", "fsdp", "dp", "dp"))
+        for i, axis in enumerate(("fsdp", "fsdp", "dp"))
     ]
+    rows = Rows(doc_ref, query_ref, x_all, chosen, moving)
     greet({"dp": n_dp, "fsdp": n_fs})
     over[0].start(lambda partner: w_ref.at[partner], lambda offset: w_all.at[my_dp, me])
     over[1].start(lambda partner: v_ref, lambda offset: v_all.at[my_dp, me])
-    piece = x_ref.shape[0] // pieces_along_y
-    spans = [pl.ds(at * piece, piece) for at in range(pieces_along_y)]
-    along_y = [
-        Sent(
-            x_ref.at[span],
-            x_all.at[me, span],
-            "fsdp",
-            other_chip,
-            chip_send.at[at],
-            chip_recv.at[at],
-        ).start()
-        for at, span in enumerate(spans)
+    rows.start()
+
+    moves = [(w_ref.at[me], w_all.at[my_dp, me]), (v_ref, v_all.at[my_dp, me])]
+    local = [
+        pltpu.make_async_copy(source, target, own_sem.at[at])
+        for at, (source, target) in enumerate(moves)
     ]
-    own = [
-        pltpu.make_async_copy(w_ref.at[me], w_all.at[my_dp, me], own_sem.at[0]),
-        pltpu.make_async_copy(v_ref, v_all.at[my_dp, me], own_sem.at[1]),
-        pltpu.make_async_copy(x_ref, x_all.at[me], own_sem.at[2]),
-    ]
-    for copy in own:
+    for copy in local:
         copy.start()
-    last = pieces_along_y
-    to_core = [
-        Sent(
-            x_ref, x_all.at[me], "fsdp", other_core, core_send.at[last], core_recv.at[last]
-        ).start()
-    ]
-    own[0].wait()
-    own[1].wait()
+    local[0].wait()
+    local[1].wait()
     over[0].arrived()
     over[1].arrived()
-    over[2].start(lambda partner: w_all.at[my_dp], lambda offset: w_all.at[my_dp])
-    over[3].start(lambda partner: v_all.at[my_dp], lambda offset: v_all.at[my_dp])
-    for at, span in enumerate(spans):
-        along_y[at].copy.wait_recv()
-        to_core.append(
+
+    block = w_all.at[my_dp]
+    along = []
+    for offset in range(1, n_z):
+        partner = lax.rem(z + offset, n_z) * 2 + x
+        along.append(
             Sent(
-                x_all.at[other_chip, span],
-                x_all.at[other_chip, span],
-                "fsdp",
-                other_core,
-                core_send.at[at],
-                core_recv.at[at],
+                block, block, "dp", partner, line_send.at[offset - 1], line_recv.at[offset - 1]
             ).start()
         )
-    for one in to_core:
+    other = z * 2 + 1 - x
+    cross = [Sent(block, block, "dp", other, cross_send.at[0], cross_recv.at[0]).start()]
+    over[2].start(lambda partner: v_all.at[my_dp], lambda offset: v_all.at[my_dp])
+    for offset in range(1, n_z):
+        along[offset - 1].copy.wait_recv()
+        block = w_all.at[lax.rem(z - offset + n_z, n_z) * 2 + x]
+        cross.append(
+            Sent(block, block, "dp", other, cross_send.at[offset], cross_recv.at[offset]).start()
+        )
+    rows.finish()
+    for one in cross:
         one.copy.wait_recv()
     over[2].arrived()
-    over[3].arrived()
-    own[2].wait()
     for exchange in over:
         exchange.sent()
-    for one in along_y + to_core:
+    for one in along + cross:
         one.copy.wait_send()
 
 
-def gather_start(rows_in, w_split, vector_tile):
+def gather_start(doc, query, w_split, vector_tile):
     n_dp, n_fs = lax.axis_size("dp"), lax.axis_size("fsdp")
+    chosen = tuple(range(doc_pieces - 1))
+    rows = doc.shape[0] + query.shape[0]
     anywhere = pl.BlockSpec(memory_space=pl.ANY)
-    dma = lambda axis: [pltpu.SemaphoreType.DMA(((n_dp if axis == "dp" else n_fs) - 1,))] * 2
+    many = lambda count: [pltpu.SemaphoreType.DMA((count,))] * 2
+    dma = lambda axis: many((n_dp if axis == "dp" else n_fs) - 1)
     return pl.pallas_call(
-        functools.partial(start_kernel, n_dp, n_fs),
-        in_specs=[anywhere] * 3,
+        functools.partial(start_kernel, n_dp, n_fs, chosen),
+        in_specs=[pl.BlockSpec(memory_space=pltpu.VMEM)] * 4,
         out_specs=[anywhere] * 3,
         out_shape=[
-            jax.ShapeDtypeStruct((n_fs,) + rows_in.shape, BF),
+            jax.ShapeDtypeStruct((n_fs, rows, D), BF),
             jax.ShapeDtypeStruct((n_dp,) + w_split.shape, BF),
             jax.ShapeDtypeStruct((n_dp, n_fs) + vector_tile.shape, F32),
         ],
-        scratch_shapes=[
-            pltpu.SemaphoreType.DMA((pieces_along_y,)),
-            pltpu.SemaphoreType.DMA((pieces_along_y,)),
-            pltpu.SemaphoreType.DMA((pieces_along_y + 1,)),
-            pltpu.SemaphoreType.DMA((pieces_along_y + 1,)),
-            pltpu.SemaphoreType.DMA((3,)),
-        ]
-        + [sem for axis in ("fsdp", "fsdp", "dp", "dp") for sem in dma(axis)],
+        scratch_shapes=rows_sems(chosen)
+        + [pltpu.SemaphoreType.DMA((2,))]
+        + many(n_dp // 2 - 1)
+        + many(n_dp // 2)
+        + [sem for axis in ("fsdp", "fsdp", "dp") for sem in dma(axis)],
         compiler_params=params(collective_id=3, has_side_effects=True),
         name="gather_start",
-    )(rows_in, w_split, vector_tile)
+    )(doc, query, w_split, vector_tile)
+
+
+def rest_kernel(n_fs, chosen, doc_ref, query_ref, given_ref, x_all, *sems):
+    rows = Rows(doc_ref, query_ref, x_all, chosen, sems)
+    greet({"fsdp": n_fs})
+    rows.start()
+    rows.finish()
+
+
+def gather_rest(doc, query, x_all):
+    chosen = tuple(range(doc_pieces - 1, pieces_along_y))
+    anywhere = pl.BlockSpec(memory_space=pl.ANY)
+    return pl.pallas_call(
+        functools.partial(rest_kernel, lax.axis_size("fsdp"), chosen),
+        in_specs=[pl.BlockSpec(memory_space=pltpu.VMEM)] * 2 + [anywhere],
+        out_specs=anywhere,
+        out_shape=jax.ShapeDtypeStruct(x_all.shape, BF),
+        scratch_shapes=rows_sems(chosen),
+        input_output_aliases={2: 0},
+        compiler_params=params(collective_id=4, has_side_effects=True),
+        name="gather_rest",
+    )(doc, query, x_all)
 
 
 def heads_kernel(doc_rows, len_ref, x_ref, w_ref, b_ref, cos_ref, sin_ref, q_ref, k_ref, v_ref):
@@ -513,11 +591,6 @@
     return centered * inverse, inverse
 
 
-GROUPS = 4
-CHUNK = 512
-OWN_ROWS = 32
-
-
 def joined_up(up_ref):
     size = OWN_ROWS
     pieces = [
@@ -526,6 +599,15 @@
         for group in range(GROUPS)
     ]
     return jnp.concatenate(pieces, axis=0)
+
+
+def regrouped(packed, old, new):
+    if old == new:
+        return packed
+    hidden = GROUPS * D
+    rows = packed[:, :hidden].reshape(-1, old, GROUPS, D).transpose(0, 2, 1, 3)
+    rows = rows.reshape(-1, GROUPS, new, D).transpose(0, 2, 1, 3).reshape(-1, hidden)
+    return jnp.concatenate([rows, packed[:, hidden:]], axis=1)
 
 
 def packed_specs():
@@ -648,6 +730,7 @@
 
 
 def rows_back_kernel(
+    by_core,
     dproj_ref,
     enc_ref,
     hat2_ref,
@@ -685,7 +768,7 @@
     hidden = GROUPS * D
     slot = lax.rem(step, 2)
 
-    core = lax.rem(lax.axis_index("fsdp"), 2)
+    core = lax.rem(lax.axis_index("fsdp"), 2) if by_core else 0
 
     def both(source, rows_at, columns, sem):
         return [
@@ -779,7 +862,7 @@
         wait(out_copy())
 
 
-def rows_backward(dproj, enc, hat2, inv2, packed, act, slope, low1, hat1, inv1, att, vectors):
+def rows_backward(by_core, dproj, enc, hat2, inv2, packed, act, slope, low1, hat1, inv1, att, vectors):
     rows, hidden = act.shape
     keep = lambda shape: pl.BlockSpec(shape, lambda step: (0,) * len(shape))
     columns = pl.BlockSpec((rows, CHUNK), lambda step: (0, step))
@@ -805,7 +888,7 @@
         (vectors, None),
     )
     return pl.pallas_call(
-        rows_back_kernel,
+        functools.partial(rows_back_kernel, by_core),
         grid=(hidden // CHUNK,),
         in_specs=[keep(entry.shape) if spec is None else spec for entry, spec in operands],
         out_specs=[
@@ -1163,7 +1246,8 @@
             leading, inverse, vector = unit(queries(block), columns)
             power = power_ref[index] if blocks == 1 else powers(index, block)
             dsim = (power * factor[index : index + 1, here]).astype(BF)
-            grad_query += unit_back(leading, inverse, dot_tn(dsim, docs[index][2]))
+            turned = dot_nn(docs[index][2].T, dsim).T
+            grad_query += unit_back(leading, inverse, turned)
             grad_doc[index] += dot_nn(dsim, vector)
         if blocks == 1:
             grad_ref[...] = grad_query.reshape(grad_ref.shape)
@@ -1294,22 +1378,29 @@
         second_shift,
     ]
     hidden_split = inner_bias.shape[0]
-    line = jnp.concatenate(small + [inner_bias]).astype(F32)
-    line = jnp.pad(line, (0, -line.shape[0] % (8 * LANES))).reshape(8, -1)
-    rows_in = jnp.concatenate([doc_tokens.reshape(doc_rows, D), query_tokens.reshape(QLEN, D)])
+    line = [jnp.pad(entry.astype(F32), (0, LANES - split)) for entry in small]
+    inner_rows = -(-hidden_split // LANES)
+    padded = jnp.pad(inner_bias.astype(F32), (0, inner_rows * LANES - hidden_split))
+    line += list(padded.reshape(inner_rows, LANES))
+    line += [jnp.zeros((LANES,), F32)] * (-len(line) % 8)
+    line = jnp.stack(line)
+    doc_in, query_in = doc_tokens.reshape(doc_rows, D), query_tokens.reshape(QLEN, D)
+    x_all, w_heads, packed = gather_start(doc_in, query_in, w_split, line)
     own_up = [outer_weight[group * split : (group + 1) * split] for group in range(GROUPS)]
     packed_own = jnp.concatenate(own_up + [inner_weight, out_weight, vector_weight], axis=1)
-    x_all, w_heads, packed = gather_start(rows_in, w_split, line)
-    packed_own, x_all = lax.optimization_barrier((packed_own, x_all))
+    packed_own, w_heads = lax.optimization_barrier((packed_own, w_heads))
     packed_w = lax.all_gather(packed_own, AXES, axis=0, tiled=True)
+    packed_w = regrouped(packed_w, split, OWN_ROWS)
+    x_all = gather_rest(doc_in, query_in, x_all)
+    rows_in = jnp.concatenate([doc_in, query_in])
     w_heads = w_heads.reshape(D, 3 * width)
-    packed = packed.reshape(lax.axis_size("dp") * parts, -1)
+    packed = packed.reshape((lax.axis_size("dp") * parts,) + line.shape)
 
     def vector(index):
-        return packed[:, index * split : (index + 1) * split].reshape(-1)
-
-    inner_at = len(small) * split
-    inner_vec = packed[:, inner_at : inner_at + hidden_split].reshape(1, -1)
+        return packed[:, index, :split].reshape(-1)
+
+    inner_vec = packed[:, len(small) : len(small) + inner_rows].reshape(packed.shape[0], -1)
+    inner_vec = inner_vec[:, :hidden_split].reshape(1, -1)
     vectors = jnp.stack([vector(i) for i in (3, 4, 5, 6, 7, 8)] + [jnp.zeros((D,), F32)] * 2)
     b_heads = jnp.concatenate(
         [lax.dynamic_slice(vector(i), (mine * width,), (width,)) for i in range(3)]
@@ -1333,7 +1424,7 @@
     dproj = jnp.concatenate([grad_doc, grad_query])
 
     keep, send, dbi, datt, dsum, dvec = rows_backward(
-        dproj, enc, hat2, inv2, packed_w, act, slope, low1, hat1, inv1, att, vectors
+        split == OWN_ROWS, dproj, enc, hat2, inv2, packed_w, act, slope, low1, hat1, inv1, att, vectors
     )
     grad_mixed = lax.all_to_all(datt, "fsdp", 0, 0, tiled=True)
     pair_args = (query_log, key, value, grad_mixed, mixed_full, cosine, sine)
@@ -1342,6 +1433,10 @@
     z, x = lax.axis_index("dp") // 2, lax.axis_index("dp") % 2
     core, y = mine % 2, mine // 2
     pick = lambda value, index, axis: lax.dynamic_index_in_dim(value, index, axis, False)
+    if split != OWN_ROWS:
+        every = jnp.stack([keep, send], axis=1).reshape(D, -1)
+        every = regrouped(every, OWN_ROWS, split).reshape(-1, 2, split, keep.shape[2])
+        keep, send = pick(every, core, 1), pick(every, 1 - core, 1)
     middle = keep.shape[2] // 2 // LANES * LANES
     n_z = n_dp // 2
     whole = (n_z, 2, 2, split, keep.shape[2])

time: 616 us -> 603 us (0.979)
  waiting for transfers between devices: 75 us -> 63.7 us
    all_gather x1, waiting for transfers between devices: 31.9 us -> 22.7 us  [shards(): packed_w = lax.all_gather(packed_own, AXES, axis=0, tiled=True)]
    concatenate x1 -> x0, local copies, waits for them, and re-layouts: 6.77 us -> none  [shards(): line = jnp.concatenate(small + [inner_bias]).astype(F32)]
    pallas_call x2 -> x3, Pallas kernels: 113 us -> 111 us  [the longest x1 55.2 us: rows_backward(): pl.pallas_call(functools.partial(rows_back_kernel, by_core), grid=(hidden...]
    unnamed x49 -> x46, local copies, waits for them, and re-layouts: 19.8 us -> 20.7 us
  transfers between devices with their start and end apart: 10 -> 10, of which waited for: 3 -> 3; matrix products, arithmetic and copies ran while one was open for 5% -> 6% of each run, Pallas kernels for 39% -> 42%
where the time goes in v4:
time: 603 us; the launch traced here: 594 us
  Pallas kernels  414 us (69%)
  waiting for transfers between devices  63.7 us (11%)
  local copies, waits for them, and re-layouts  52.9 us (9%)
  other arithmetic  32.7 us (5%)
  between operations  15.5 us (3%)
  starting transfers between devices  15.2 us (3%)
    pallas_call x3, Pallas kernels, attend_back(): pl.pallas_call(functools.partial(attend_back_kernel, halves, doc_rows, pa...  112 us
    pallas_call x1, Pallas kernels, heads_backward(): pl.pallas_call(functools.partial(heads_back_kernel, n_dp, n_fs, pair_of),...  59.3 us
    pallas_call x1, Pallas kernels, rows_backward(): pl.pallas_call(functools.partial(rows_back_kernel, by_core), grid=(hidden...  55.2 us
    pallas_call x1, Pallas kernels, attend(): pl.pallas_call(functools.partial(attend_kernel, doc_rows, parts), grid=(h...  51.4 us
    pallas_call x1, Pallas kernels, gather_start(): pl.pallas_call(functools.partial(start_kernel, n_dp, n_fs, chosen), in_sp...  39.4 us
    pallas_call x1, Pallas kernels, maxsim(): pl.pallas_call(functools.partial(maxsim_kernel, n_dp, n_fs), in_specs=[wh...  37.5 us
    all_to_all x1, waiting for transfers between devices, shards(): att = lax.all_to_all(mixed, 'fsdp', 0, 0, tiled=True)  33.7 us
    pallas_call x1, Pallas kernels, rows_forward(): pl.pallas_call(rows_kernel, grid=(hidden // chunk,), in_specs=[keep(att.s...  30.2 us
  transfers between devices with their start and end apart: 10, of which 3 were waited for; matrix products, arithmetic and copies ran while one was open for 6% of the time, Pallas kernels for 42%

profile of v4, /device:TPU:1, one launch (start us, length us, event | category | flops | bytes accessed | tf_op | source)
XLA Modules:
  0.0 594.4 jit_solution(119591872327464758)
XLA Ops:
  7.2 0.8 fusion.10
  8.0 0.8 fusion.11
  8.8 0.8 fusion.12
  9.6 0.8 slice_dynamic-update-slice_fusion.3
  10.4 0.8 slice_dynamic-update-slice_fusion.2
  11.2 0.8 slice_dynamic-update-slice_fusion.1
  12.1 0.8 slice_dynamic-update-slice_fusion
  16.3 1.0 constant_dynamic-update-slice_fusion.2
  17.3 0.8 constant_dynamic-update-slice_fusion.1
  18.1 0.7 constant_dynamic-update-slice_fusion
  18.9 0.8 pad_maximum_fusion.4.refs_2_
  19.7 1.2 stack.121.refs_3_
  20.9 39.4 %gather_start.1 = (bf16[4,800,1024]{2,1,0:T(8,128)(2,1)}, bf16[8,4,32,768]{3,2,1,0:T(8,128)(2,1)}, f32[8,4,16,128]{3,2,1,0:T(8,128)}) custom-call(bf16[768,1024]{1,0:T(8,128)(2,1)} %bitcast.143, bf16[32,1024]{1,0:T(8,128)(2,1)} %bitcast.151, bf16[4,32,768]{2,1,0:T(8,128)(2,1)} %pad_maximum_fusion.4.refs_2_, f32[16,128]{1,0:T(8,128)} %stack.121.refs_3_), custom_call_target="tpu_custom_call" | custom-call | tf_op jit(solution)/shard_map/gather_start/pallas_call | solution.py:286
  60.4 2.1 fusion.9
  63.5 16.8 %gather_rest.1.x_ref.refs_0_ = bf16[4,800,1024]{2,1,0:T(8,128)(2,1)} custom-call(bf16[768,1024]{1,0:T(8,128)(2,1)} %bitcast.144, bf16[32,1024]{1,0:T(8,128)(2,1)} %bitcast.152, bf16[4,800,1024]{2,1,0:T(8,128)(2,1)} %get-tuple-element.102.given_ref), custom_call_target="tpu_custom_call", output_to_operand_aliasing={{}: (2, {})} | custom-call | tf_op jit(solution)/shard_map/gather_rest/pallas_call | solution.py:315
  81.0 12.5 %project_heads.1 = (bf16[4,3200,128]{2,1,0:T(8,128)(2,1)}, bf16[4,3200,128]{2,1,0:T(8,128)(2,1)}, bf16[4,3200,128]{2,1,0:T(8,128)(2,1)}) custom-call(s32[1]{0:T(128)} %copy.142.len_ref, bf16[4,800,1024]{2,1,0:T(8,128)(2,1)} %gather_rest.1.x_ref.refs_0_, bf16[1024,768]{1,0:T(8,128)(2,1)} %bitcast.148, f32[1,768]{1,0:T(1,128)} %reshape.165.b_ref, ...), custom_call_target="tpu_custom_call" | custom-call | tf_op jit(solution)/shard_map/project_heads/pallas_call | solution.py:362
  93.4 51.4 %attend.1 = (bf16[4,800,256]{2,1,0:T(8,128)(2,1)}, f32[4,800,256]{2,1,0:T(8,128)}, bf16[4,3200,128]{2,1,0:T(8,128)(2,1)}) custom-call(bf16[4,3200,128]{2,1,0:T(8,128)(2,1)} %get-tuple-element.106.q_ref, bf16[4,3200,128]{2,1,0:T(8,128)(2,1)} %get-tuple-element.158.k_ref.ko_ref, bf16[4,3200,128]{2,1,0:T(8,128)(2,1)} %get-tuple-element.159.v_ref.vo_ref, ...), custom_call_target="tpu_custom_call" | custom-call | flops 41943040000 | bytes 16777216 | tf_op jit(solution)/shard_map/attend/pallas_call | solution.py:434
  144.8 4.3 all-to-all-start
  150.4 1.3 pad_maximum_fusion.1.x_ref
  151.7 1.5 slice_bitcast_fusion.4.bi_ref
  153.2 33.7 %all-to-all-done.att_ref = bf16[4,800,256]{2,1,0:T(8,128)(2,1)S(1)} async-done(((bf16[4,800,256]{2,1,0:T(8,128)(2,1)}), bf16[4,800,256]{2,1,0:T(8,128)(2,1)S(1)}, u32[]{:S(2)}, u32[]{:S(2)}) %all-to-all-start) | async-done | bytes 1638432 | tf_op jit(solution)/shard_map/all_to_all | solution.py:1415
  186.9 22.7 %all-gather.2.cloned.1.call-done.wo_ref.wi_ref.wu_ref.wv_ref = bf16[1024,9344]{1,0:T(8,128)(2,1)} async-done(((bf16[32,9344]{1,0:T(8,128)(2,1)}), bf16[1024,9344]{1,0:T(8,128)(2,1)}) %all-gather.2.cloned.1.call-update) | async-done | bytes 19136528 | tf_op jit(solution)/shard_map/all_gather | solution.py:1392
  209.6 30.2 %rows_forward.1 = (bf16[800,1024]{1,0:T(8,128)(2,1)}, f32[800,128]{1,0:T(8,128)}, bf16[800,1024]{1,0:T(8,128)(2,1)}, bf16[800,4096]{1,0:T(8,128)(2,1)}, bf16[800...) custom-call(bf16[4,800,256]{2,1,0:T(8,128)(2,1)} %copy-done.8, ...), custom_call_target="tpu_custom_call" | custom-call | flops 15099494400 | bytes 33554432 | tf_op jit(solution)/shard_map/rows_forward/pallas_call | solution.py:687
  239.8 1.8 slice.231.pd_ref
  241.5 1.3 slice.230.pq_ref
  242.9 0.9 broadcast_in_dim.41.mask_ref
  244.4 37.5 %maxsim.1 = (f32[8,128]{1,0:T(8,128)}, bf16[32,128]{1,0:T(8,128)(2,1)}, bf16[768,128]{1,0:T(8,128)(2,1)}) custom-call(f32[32,128]{1,0:T(8,128)} %slice.230.pq_ref, f32[768,128]{1,0:T(8,128)} %slice.231.pd_ref, f32[768,128]{1,0:T(8,128)} %broadcast_in_dim.41.mask_ref, s32[8,128]{1,0:T(8,128)} %broadcast_in_dim.43.label_ref), custom_call_target="tpu_custom_call" | custom-call | tf_op jit(solution)/shard_map/maxsim/pallas_call | solution.py:1292
  281.9 1.6 pad_maximum_fusion.3.dproj_ref
  283.5 55.2 %rows_backward.1 = (bf16[16,32,9344]{2,1,0:T(8,128)(2,1)}, bf16[16,32,9344]{2,1,0:T(8,128)(2,1)}, f32[1,4096]{1,0:T(1,128)}, bf16[4,800,256]{2,1,0:T(8,128)(2,1)...) custom-call(bf16[800,128]{1,0:T(8,128)(2,1)} %pad_maximum_fusion.3.dproj_ref, bf16[800,1024]{1,0:T(8,128)(2,1)} %get-tuple-element.113.enc_ref, ...), custom_call_target="tpu_custom_call" | custom-call | flops 30198988800 | bytes 67108864 | tf_op jit(solution)/shard_map/rows_backward/pallas_call | solution.py:890
  339.1 4.7 all-to-all-start.1
  345.5 1.3 slice_bitcast_fusion.1
  346.7 7.2 %collective-permute-done = bf16[16,32,9344]{2,1,0:T(8,128)(2,1)} collective-permute-done((bf16[16,32,9344]{2,1,0:T(8,128)(2,1)}, bf16[16,32,9344]{2,1,0:T(8,128)(2,1)}, u32[]{:S(2)}, u32[]{:S(2)}) %collective-permute-start) | collective-permute-done | bytes 9568288 | tf_op jit(solution)/shard_map/ppermute | solution.py:1446
  354.0 4.4 convert_add_fusion
  358.4 8.0 %convert_add_fusion.1 = f32[4,2,2,32,4608]{4,3,0,2,1:T(8,128)S(1)} fusion(bf16[4,2,2,32,9344]{4,3,2,1,0:T(8,128)(2,1)} %bitcast.147, bf16[4,2,2,32,9344]{4,3,2,1,0:T(8,128)(2,1)} %bitcast.26), kind=kLoop, calls=%fused_computation.1 | loop fusion | flops 7077888 | bytes 18874368 | tf_op jit(solution)/shard_map/add | solution.py:1444
  366.6 3.3 copy-done.2
  370.0 1.6 fusion.1
  372.2 1.4 collective-permute-start.1
  373.5 52.0 %attend_back.3 = (bf16[4,800,128]{2,1,0:T(8,128)(2,1)}, bf16[4,800,128]{2,1,0:T(8,128)(2,1)}, bf16[4,800,128]{2,1,0:T(8,128)(2,1)}, f32[8,128]{1,0:T(8,128)}) custom-call(bf16[4,3200,128]{2,1,0:T(8,128)(2,1)} %get-tuple-element.157.q_ref, bf16[4,3200,128]{2,1,0:T(8,128)(2,1)} %get-tuple-element.158.k_ref.ko_ref, ...), custom_call_target="tpu_custom_call" | custom-call | flops 52428800000 | bytes 16777216 | tf_op jit(solution)/shard_map/attend_back/pallas_call | solution.py:562
  425.5 0.8 slice_bitcast_fusion.7
  426.3 3.7 bitcast_add_fusion.1
  430.1 2.4 copy-done.6
  432.6 1.2 copy-done.1
  433.8 2.2 bitcast_add_fusion
  436.1 2.2 copy-done.3
  438.9 1.0 collective-permute-start.3
  439.9 29.0 %attend_back.4 = (bf16[4,800,128]{2,1,0:T(8,128)(2,1)}, bf16[4,800,128]{2,1,0:T(8,128)(2,1)}, bf16[4,800,128]{2,1,0:T(8,128)(2,1)}, f32[8,128]{1,0:T(8,128)}) custom-call(bf16[4,3200,128]{2,1,0:T(8,128)(2,1)} %get-tuple-element.157.q_ref, bf16[4,3200,128]{2,1,0:T(8,128)(2,1)} %get-tuple-element.158.k_ref.ko_ref, ...), custom_call_target="tpu_custom_call" | custom-call | flops 26214400000 | bytes 16777216 | tf_op jit(solution)/shard_map/attend_back/pallas_call | solution.py:562
  469.0 2.4 bitcast_add_fusion.4
  471.4 1.0 copy-done.4
  473.0 2.2 copy-done.5
  476.0 31.3 %attend_back.5 = (bf16[4,800,128]{2,1,0:T(8,128)(2,1)}, bf16[4,800,128]{2,1,0:T(8,128)(2,1)}, bf16[4,800,128]{2,1,0:T(8,128)(2,1)}, f32[8,128]{1,0:T(8,128)}) custom-call(bf16[4,3200,128]{2,1,0:T(8,128)(2,1)} %get-tuple-element.157.q_ref, bf16[4,3200,128]{2,1,0:T(8,128)(2,1)} %get-tuple-element.158.k_ref.ko_ref, ...), custom_call_target="tpu_custom_call" | custom-call | flops 26214400000 | bytes 16777216 | tf_op jit(solution)/shard_map/attend_back/pallas_call | solution.py:562
  507.2 0.8 add_bitcast_fusion.3
  509.3 1.0 copy-done.11
  510.3 2.2 bitcast_add_fusion.3
  512.5 0.9 dynamic-slice_convert_fusion.5
  513.4 2.1 collective-permute-start.6
  515.5 59.3 %heads_backward.1 = (bf16[800,1024]{1,0:T(8,128)(2,1)}, f32[4,32,768]{2,1,0:T(8,128)}, f32[8,128]{1,0:T(8,128)}) custom-call(bf16[4,800,1024]{2,1,0:T(8,128)(2,1)} %gather_rest.1.x_ref.refs_0_, bf16[1024,768]{1,0:T(8,128)(2,1)} %bitcast.149, f32[800,1024]{1,0:T(8,128)} %get-tuple-element.123.refs_2_, f32[4,8,8,128]{3,2,1,0:T(8,128)} %bitcast.155, ...), custom_call_target="tpu_custom_call" | custom-call | tf_op jit(solution)/shard_map/heads_backward/pallas_call | solution.py:1100
  574.8 1.2 reshape.179
  576.3 1.6 fusion.13
  577.9 1.3 slice.262
  581.5 1.5 slice_bitcast_fusion.2
  583.0 1.3 slice_bitcast_fusion
  584.4 0.7 fusion.7
  585.1 0.8 slice.289
  586.5 0.8 pad_maximum_fusion.2
  (109 shorter events, 15.7 us)
Async XLA Ops:
  7.2 202.4 %all-gather.2.cloned.1.call-start = ((), (), s32[]{:S(2)}) async-start(), calls=%async_computation.2 | async-start | bytes 19734528 | tf_op jit(solution)/shard_map/all_gather | solution.py:1392
  18.8 41.5 %copy-start.12 = (bf16[32,9344]{1,0:T(8,128)(2,1)}, bf16[32,9344]{1,0:T(8,128)(2,1)S(1)}, u32[]{:S(2)}) copy-start(bf16[32,9344]{1,0:T(8,128)(2,1)S(1)} %constant_dynamic-update-slice_fusion) | copy-start | bytes 1794052
  144.8 4.8 copy-start.16
  144.8 5.6 copy-start.7
  144.8 5.6 copy-start.13
  144.8 42.1 %all-to-all-start = ((bf16[4,800,256]{2,1,0:T(8,128)(2,1)}), bf16[4,800,256]{2,1,0:T(8,128)(2,1)S(1)}, u32[]{:S(2)}, u32[]{:S(2)}) async-start(bf16[4,800,256]{2,1,0:T(8,128)(2,1)} %get-tuple-element.109), calls=%async_computation | async-start | bytes 3276800 | tf_op jit(solution)/shard_map/all_to_all | solution.py:1415
  186.9 22.7 %copy-start.8 = (bf16[4,800,256]{2,1,0:T(8,128)(2,1)}, bf16[4,800,256]{2,1,0:T(8,128)(2,1)S(1)}, u32[]{:S(2)}) copy-start(bf16[4,800,256]{2,1,0:T(8,128)(2,1)S(1)} %all-to-all-done.att_ref) | copy-start | bytes 4915204
  338.7 5.1 copy-start.14
  338.7 5.3 copy-start.17
  338.7 6.1 %copy-start.9 = (bf16[800,1024]{1,0:T(8,128)(2,1)S(1)}, bf16[800,1024]{1,0:T(8,128)(2,1)}, u32[]{:S(2)}) copy-start(bf16[800,1024]{1,0:T(8,128)(2,1)} %get-tuple-element.113.enc_ref) | copy-start | bytes 4915204
  338.7 15.3 %collective-permute-start = (bf16[16,32,9344]{2,1,0:T(8,128)(2,1)}, bf16[16,32,9344]{2,1,0:T(8,128)(2,1)}, u32[]{:S(2)}, u32[]{:S(2)}) collective-permute-start(bf16[16,32,9344]{2,1,0:T(8,128)(2,1)} %get-tuple-element.125), channel_id=1, source_target_pairs={{0,1},{1,0},{2,3},{3,2},{4,5},{5,4},{6,7},{7,6},{8,9},{9,8},{10,11... | collective-permute-start | bytes 28704776 | tf_op jit(solution)/shard_map/ppermute | solution.py:1446
  339.1 32.5 %all-to-all-start.1 = ((bf16[4,800,256]{2,1,0:T(8,128)(2,1)}), bf16[4,800,256]{2,1,0:T(8,128)(2,1)}, u32[]{:S(2)}, u32[]{:S(2)}) async-start(bf16[4,800,256]{2,1,0:T(8,128)(2,1)} %get-tuple-element.127), calls=%async_computation.1 | async-start | bytes 3276800 | tf_op jit(solution)/shard_map/all_to_all | solution.py:1429
  358.3 8.0 %copy-start = (f32[4,2,2,32,4736]{4,3,0,1,2:T(8,128)}, f32[4,2,2,32,4736]{4,3,0,1,2:T(8,128)S(1)}, u32[]{:S(2)}) copy-start(f32[4,2,2,32,4736]{4,3,0,1,2:T(8,128)S(1)} %convert_add_fusion) | copy-start | bytes 29097988
  366.3 3.6 copy-start.2
  371.6 54.7 %collective-permute-start.2 = (bf16[4,2,32,4736]{3,2,0,1:T(8,128)(2,1)S(1)}, bf16[4,2,32,4736]{3,2,0,1:T(8,128)(2,1)}, u32[]{:S(2)}, u32[]{:S(2)}) collective-permute-start(bf16[4,2,32,4736]{3,2,0,1:T(8,128)(2,1)S(1)} %fusion), channel_id=1, source_target_pairs={{0,2},{1,3},{2,0},{3,1},{4,6},{5,7},{6,4},{7,5},{8,10},{9,11},{10,... | collective-permute-start | bytes 7274504 | tf_op jit(solution)/shard_map/ppermute | solution.py:1454
  372.2 54.2 %collective-permute-start.1 = (bf16[4,2,32,4608]{3,2,0,1:T(8,128)(2,1)}, bf16[4,2,32,4608]{3,2,0,1:T(8,128)(2,1)}, u32[]{:S(2)}, u32[]{:S(2)}) collective-permute-start(bf16[4,2,32,4608]{3,2,0,1:T(8,128)(2,1)} %fusion.1), channel_id=1, source_target_pairs={{0,4},{4,0},{8,12},{12,8},{16,20},{20,16},{24,28},{28,24},{1,5},{5... | collective-permute-start | bytes 7077896 | tf_op jit(solution)/shard_map/ppermute | solution.py:1453
  426.3 7.5 %copy-start.1 = (f32[4,2,2,32,4736]{4,3,0,1,2:T(8,128)S(1)}, f32[4,2,2,32,4736]{4,3,0,1,2:T(8,128)}, u32[]{:S(2)}) copy-start(f32[4,2,2,32,4736]{4,3,0,1,2:T(8,128)} %copy-done) | copy-start | bytes 29097988
  430.1 2.4 copy-start.6
  436.1 2.2 copy-start.3
  438.4 30.6 %collective-permute-start.4 = (bf16[4,32,4736]{2,1,0:T(8,128)(2,1)S(1)}, bf16[4,32,4736]{2,1,0:T(8,128)(2,1)S(1)}, u32[]{:S(2)}, u32[]{:S(2)}) collective-permute-start(bf16[4,32,4736]{2,1,0:T(8,128)(2,1)S(1)} %fusion.2), channel_id=1, source_target_pairs={{0,4},{4,0},{8,12},{12,8},{16,20},{20,16},{24,28},{28,24},{1,5},{5... | collective-permute-start | bytes 3637256 | tf_op jit(solution)/shard_map/ppermute | solution.py:1465
  438.9 30.1 %collective-permute-start.3 = (bf16[4,32,4608]{2,1,0:T(8,128)(2,1)S(1)}, bf16[4,32,4608]{2,1,0:T(8,128)(2,1)}, u32[]{:S(2)}, u32[]{:S(2)}) collective-permute-start(bf16[4,32,4608]{2,1,0:T(8,128)(2,1)S(1)} %fusion.4), channel_id=1, source_target_pairs={{0,2},{1,3},{2,0},{3,1},{4,6},{5,7},{6,4},{7,5},{8,10},{9,11},{10,... | collective-permute-start | bytes 3538952 | tf_op jit(solution)/shard_map/ppermute | solution.py:1464
  469.0 3.4 copy-start.4
  473.0 2.2 copy-start.5
  475.3 33.1 %copy-start.15 = (f32[1,4096]{1,0:T(1,128)S(1)}, f32[1,4096]{1,0:T(1,128)}, u32[]{:S(2)}) copy-start(f32[1,4096]{1,0:T(1,128)} %get-tuple-element.166) | copy-start | bytes 49156
  475.4 33.9 %collective-permute-start.5 = (bf16[2,32,9344]{2,1,0:T(8,128)(2,1)S(1)}, bf16[2,32,9344]{2,1,0:T(8,128)(2,1)S(1)}, u32[]{:S(2)}, u32[]{:S(2)}) collective-permute-start(bf16[2,32,9344]{2,1,0:T(8,128)(2,1)S(1)} %fusion.3), channel_id=1, source_target_pairs={{0,8},{4,12},{8,0},{12,4},{16,24},{20,28},{24,16},{28,20},{1,9},{5... | collective-permute-start | bytes 3588104 | tf_op jit(solution)/shard_map/ppermute | solution.py:1481
  509.3 1.0 copy-start.11
  513.4 70.8 %collective-permute-start.6 = (bf16[1,32,9344]{2,1,0:T(8,128)(2,1)}, bf16[1,32,9344]{2,1,0:T(8,128)(2,1)S(1)}, u32[]{:S(2)}, u32[]{:S(2)}) collective-permute-start(bf16[1,32,9344]{2,1,0:T(8,128)(2,1)} %dynamic-slice_convert_fusion.5), channel_id=1, source_target_pairs={{0,16},{4,20},{8,24},{12,28},{16,0},{20,4},{24,8},{28,12},{1,17},{... | collective-permute-start | bytes 1794056 | tf_op jit(solution)/shard_map/ppermute | solution.py:1481
  576.0 7.0 %copy-start.10 = (bf16[800,1024]{1,0:T(8,128)(2,1)S(1)}, bf16[800,1024]{1,0:T(8,128)(2,1)}, u32[]{:S(2)}) copy-start(bf16[800,1024]{1,0:T(8,128)(2,1)} %get-tuple-element.178) | copy-start | bytes 4915204
Sparse Core Ops, SparseCore 0:
  60.5 149.0 all-gather.1
